TPU v7x, 32 devices: a whole 2x2x4 slice. The times are simulated.
32 devices in a mesh: col: 4 (over x, core), row: 8 (over z, y).
Axes of the slice: x: 2, y: 2, z: 4, core: 2. Of those that a mesh axis runs over, the one named last changes fastest.
Arguments:
- slip: bfloat16 [64, 32768], P(None, ('col', 'row')), may hold values from -6 to 6
- lowrank_u: bfloat16 [4, 8192, 2048], P(None, 'row', 'col'), may hold values from -0.5 to 0.5
- lowrank_v: bfloat16 [4, 64, 2048, 128], P(None, 'col', 'row'), may hold values from -0.09375 to 0.09375
- ranks: int32 [4, 64, 64], P(None, 'row', 'col'), may hold values from 8 to 32
- near_slot: int32 [4, 64, 8], P(None, 'row', 'col'), may hold values from 0 to 15, as said below
- near_blocks: bfloat16 [4, 8192, 1024], P(None, 'row', 'col'), may hold values from -0.09375 to 0.09375
- velocity: float32 [64, 8192], P(None, ('col', 'row')), may hold values from 0.3 to 3
- theta: float32 [64, 8192], P(None, ('col', 'row')), may hold values from 0.3 to 3
- a_sigma: float32 [8192], P(('col', 'row')), may hold values from 0.5 to 2
- b_sigma: float32 [8192], P(('col', 'row')), may hold values from 0.5 to 2
Outputs:
- stress_rate: float32 [64, 8192], P(None, ('col', 'row'))
- accel: float32 [64, 8192], P(None, ('col', 'row'))
Inputs may be any that keep to these rules, and one draw needn't show every extreme that they name: `near_slot`: for each section, source block and receiver group, the 2 entries are distinct receiver blocks of that group. `ranks`: ranks of near-field blocks are not used.
All inputs are finite; a program needn't handle non-finite values.
Results may differ from a plain program's by a relative error of at most 0.002.
Values may be sent and summed in bfloat16 or wider, within the bound.
No kernel may reach another device: no remote copies, remote signals or barrier semaphores. Data moves between devices by JAX's collectives and lax.ppermute only.
A program may use at most 64 MiB of HBM per device.

v0:
```python
import jax
import jax.numpy as jnp
from jax import lax
from jax.sharding import PartitionSpec as P


def from_root(block, axis, holder):
    block = jnp.where(lax.axis_index(axis) == holder, block, jnp.zeros_like(block))
    return lax.psum(block, axis)


def section_stress(source_rows, left_factor, right_factor, block_ranks, slot_rows, dense_blocks):
    members, count, width = source_rows.shape
    receivers = block_ranks.shape[1]
    kmax_here = left_factor.shape[1] // receivers
    slots = slot_rows.shape[1]
    projected = jnp.einsum(
        "mbs,bsq->mbq",
        source_rows,
        left_factor.reshape(count, width, receivers * kmax_here),
        preferred_element_type=jnp.float32,
    )
    projected = projected.reshape(members, count, receivers, kmax_here)
    near_hits = slot_rows[:, :, None] == jnp.arange(receivers, dtype=jnp.int32)[None, None, :]
    nearby = jnp.any(near_hits, axis=1)
    keep_mask = (
        jnp.arange(kmax_here, dtype=jnp.int32)[None, None, :] < block_ranks[:, :, None]
    ) & ~nearby[:, :, None]
    coeffs = jnp.where(keep_mask[None], projected, 0.0).astype(jnp.bfloat16)
    far_part = jnp.einsum(
        "mbjk,jbkr->mjr",
        coeffs,
        right_factor.reshape(receivers, count, kmax_here, width),
        preferred_element_type=jnp.float32,
    )
    dense_out = jnp.einsum(
        "mbs,bsqr->mbqr",
        source_rows,
        dense_blocks.reshape(count, width, slots, width),
        preferred_element_type=jnp.float32,
    )
    near_part = jnp.einsum(
        "mbqr,bqj->mjr", dense_out, near_hits.astype(jnp.float32), precision=lax.Precision.HIGHEST
    )
    return (far_part + near_part).reshape(members, receivers * width)


def body(
    slip, lowrank_u, lowrank_v, ranks, near_slot, near_blocks, velocity, theta, a_sigma, b_sigma
):
    groups = lax.axis_size("col")
    members = slip.shape[0]
    piece_width = slip.shape[1]
    count = ranks.shape[1]
    width = piece_width // count
    owned_rows = jnp.zeros(velocity.shape, jnp.float32)
    for section_index in range(groups):
        sources = from_root(slip, "col", section_index)
        partials = section_stress(
            sources.reshape(members, count, width),
            lowrank_u[section_index],
            lowrank_v[section_index],
            ranks[section_index],
            near_slot[section_index],
            near_blocks[section_index],
        )
        owned_rows = owned_rows + lax.psum_scatter(partials, "row", scatter_dimension=1, tiled=True)
    theta_rate = 1.0 - velocity * theta
    accel = (owned_rows - b_sigma[None, :] * theta_rate / theta) / (
        a_sigma[None, :] / velocity + 0.5
    )
    return (owned_rows, accel)


def solution(mesh):
    placed = (
        P(None, ("col", "row")),
        P(None, "row", "col"),
        P(None, "col", "row", None),
        P(None, "row", "col"),
        P(None, "row", "col"),
        P(None, "row", "col"),
        P(None, ("col", "row")),
        P(None, ("col", "row")),
        P(("col", "row")),
        P(("col", "row")),
    )
    return jax.shard_map(
        body,
        mesh=mesh,
        in_specs=placed,
        out_specs=(P(None, ("col", "row")), P(None, ("col", "row"))),
        check_vma=False,
    )
```

profile of v0, /device:TPU:0, one launch (start us, length us, event | category | flops | bytes accessed | tf_op | source)
XLA Modules:
  0.0 144.5 jit_solution(12559332400496910434)
XLA Ops:
  7.2 0.0 copy-start.23
  7.2 0.0 copy-start.22
  7.2 0.0 copy-start.7
  7.2 0.0 all-reduce.3.cloned.1.call-start
  7.3 1.1 select_bitcast_fusion.3
  8.3 0.8 copy_bitcast_fusion.3
  9.1 0.8 copy_bitcast_fusion.1
  9.9 0.0 all-reduce.3.cloned.1.call-update
  9.9 0.0 reduce-scatter.2.cloned.1.call-start
  10.0 0.0 copy-done.23
  10.0 0.1 fusion.49
  10.1 0.1 fusion.45
  10.2 0.0 copy-done.22
  10.2 0.0 copy-done.7
  10.2 0.0 copy-start
  10.2 1.4 fusion.66
  11.6 1.6 %copy-done = bf16[4,1024,512]{2,1,0:T(8,128)(2,1)S(1)} copy-done((bf16[4,1024,512]{2,1,0:T(8,128)(2,1)S(1)}, bf16[4,1024,512]{2,1,0:T(8,128)(2,1)}, u32[]{:S(2)}) %copy-start) | copy-done | bytes 4194328
  13.2 1.4 fusion.65
  14.6 1.1 copy-done.1
  15.7 2.1 %fusion.64 = (bf16[1,16,256,128]{3,2,1,0:T(8,128)(2,1)}, bf16[1,16,256,128]{3,2,1,0:T(8,128)(2,1)}, bf16[1,16,256,128]{3,2,1,0:T(8,128)(2,1)}, bf16[1,16,256,128]{3,2,1,0:T(8,128)(2,1)}) fusion(bf16[4,16,256,128]{3,2,1,0:T(8,128)(2,1)S(1)} %copy-done.1), kind=kLoop, calls=%fused_computation.102 | loop fusion | bytes 8388608 | tf_op jit(solution)/shard_map/slice | solution.py:62
  17.8 0.1 fusion.40
  17.9 0.1 fusion.43
  18.0 0.1 fusion.47
  18.1 2.0 %reshape_squeeze.38 = bf16[8,128,2,128]{3,2,1,0:T(2,128)(2,1)} reshape(bf16[1,1024,256]{2,1,0:T(8,128)(2,1)} %get-tuple-element.14) | data formatting | bytes 1048576 | tf_op jit(solution)/shard_map/reshape;squeeze | solution.py:39
  20.1 2.0 %reshape_squeeze.41 = bf16[8,128,2,128]{3,2,1,0:T(2,128)(2,1)} reshape(bf16[1,1024,256]{2,1,0:T(8,128)(2,1)} %get-tuple-element.15) | data formatting | bytes 1048576 | tf_op jit(solution)/shard_map/reshape;squeeze | solution.py:39
  22.0 2.0 %reshape_squeeze.47 = bf16[8,128,2,128]{3,2,1,0:T(2,128)(2,1)} reshape(bf16[1,1024,256]{2,1,0:T(8,128)(2,1)} %get-tuple-element.16) | data formatting | bytes 1048576 | tf_op jit(solution)/shard_map/reshape;squeeze | solution.py:39
  24.0 2.0 %reshape_squeeze.44 = bf16[8,128,2,128]{3,2,1,0:T(2,128)(2,1)} reshape(bf16[1,1024,256]{2,1,0:T(8,128)(2,1)} %get-tuple-element.17) | data formatting | bytes 1048576 | tf_op jit(solution)/shard_map/reshape;squeeze | solution.py:39
  26.0 0.1 fusion.41
  26.1 20.6 %all-reduce.3.cloned.1.call-done = (bf16[64,8,128]{2,0,1:T(8,128)(2,1)}, bf16[64,8,128]{2,0,1:T(8,128)(2,1)}, bf16[64,8,128]{2,0,1:T(8,128)(2,1)}, bf16[64,8,128]{2,0,1:T(8,128)(2,1)}) async-done(((bf16[64,8,128]{2,0,1:T(8,128)(2,1)}, bf16[64,8,128]{2,0,1:T(8,128)(2,1)}, bf16[64,8,128]{2,0,1:T(8,128)(2,1)}, bf16[64,8,128]{2,0,1:T(8,128)(2,1)}), (bf16[64,8,128]{2,0,1:T(8,128)(2,1)}, ...) | async-done | bytes 524304 | tf_op jit(solution)/shard_map/psum | solution.py:9
  46.7 1.4 fusion.34
  48.1 1.5 %convolution_bitcast_fusion.11 = f32[16,64,128]{2,0,1:T(8,128)} fusion(f32[8,64,2,128]{3,1,2,0:T(8,128)S(1)} %fusion.34, s32[8,2]{0,1:T(2,128)S(1)} %get-tuple-element.26), kind=kOutput, calls=%fused_computation.15 | convolution fusion | flops 25166080 | bytes 1048640 | tf_op jit(solution)/shard_map/mbqr,bqj->mjr/dot_general | solution.py:42
  49.7 0.0 copy-done.10
  49.7 0.2 fusion.31
  49.9 1.5 %convolution_bitcast_fusion.10 = f32[16,64,128]{2,0,1:T(8,128)} fusion(f32[8,64,2,128]{3,1,2,0:T(8,128)S(1)} %fusion.31, s32[8,2]{0,1:T(2,128)S(1)} %get-tuple-element.27), kind=kOutput, calls=%fused_computation.14 | convolution fusion | flops 25166080 | bytes 1048640 | tf_op jit(solution)/shard_map/mbqr,bqj->mjr/dot_general | solution.py:42
  51.4 0.0 copy-done.17
  51.5 0.2 fusion.25
  51.7 1.5 %convolution_bitcast_fusion.8 = f32[16,64,128]{2,0,1:T(8,128)} fusion(f32[8,64,2,128]{3,1,2,0:T(8,128)S(1)} %fusion.25, s32[8,2]{0,1:T(2,128)S(1)} %get-tuple-element.28), kind=kOutput, calls=%fused_computation.12 | convolution fusion | flops 25166080 | bytes 1048640 | tf_op jit(solution)/shard_map/mbqr,bqj->mjr/dot_general | solution.py:42
  53.2 0.2 fusion.28
  53.4 1.6 %convolution_bitcast_fusion.9 = f32[16,64,128]{2,0,1:T(8,128)} fusion(f32[8,64,2,128]{3,1,2,0:T(8,128)S(1)} %fusion.28, s32[8,2]{0,1:T(2,128)S(1)} %get-tuple-element.29), kind=kOutput, calls=%fused_computation.13 | convolution fusion | flops 25166080 | bytes 1048640 | tf_op jit(solution)/shard_map/mbqr,bqj->mjr/dot_general | solution.py:42
  55.1 1.2 convolution_bitcast_fusion.3
  56.2 1.1 convolution_bitcast_fusion.2
  57.3 0.3 convolution_bitcast_fusion
  57.6 0.3 convolution_bitcast_fusion.1
  57.9 1.3 copy.33
  59.2 1.3 copy.37
  60.6 0.5 copy.29
  61.1 0.0 copy-done.5
  61.1 0.5 copy.25
  61.6 0.0 copy-start.11
  61.6 0.0 copy-start.13
  61.6 0.0 copy-start.15
  61.6 3.1 %fusion.6 = f32[16,64,128]{2,1,0:T(8,128)S(1)} fusion(bf16[64,8,16,32]{0,3,2,1:T(8,128)(2,1)} %bitcast.155, bf16[16,8,32,128]{3,2,1,0:T(8,128)(2,1)} %bitcast.158, pred[8,16,32]{2,1,0:T(8,128)(4,1)S(1)} %get-tuple-element.35, f32[16,64,128]{2,0,1:T(8,128)} %convolution_bitcast_fusion.9), kind=kOutput, calls=%fused_computation.22 | convolution fusion | flops 67502080 | bytes 2625536 | tf_op jit(solution)/shard_map/mbjk,jbkr->mjr/dot_general | solution.py:30
  64.8 2.6 %fusion.7 = f32[16,64,128]{2,1,0:T(8,128)S(1)} fusion(bf16[64,8,16,32]{0,3,2,1:T(8,128)(2,1)S(1)} %bitcast.154, bf16[16,8,32,128]{3,2,1,0:T(8,128)(2,1)S(1)} %bitcast.157, pred[8,16,32]{2,1,0:T(8,128)(4,1)S(1)} %fusion.43, f32[16,64,128]{2,0,1:T(8,128)S(1)} %copy-done.15), kind=kOutput, calls=%fused_computation.23 | convolution fusion | flops 67502080 | bytes 2625536 | tf_op jit(solution)/shard_map/mbjk,jbkr->mjr/dot_general | solution.py:30
  67.4 2.6 %fusion.5 = f32[16,64,128]{2,1,0:T(8,128)S(1)} fusion(bf16[64,8,16,32]{0,3,2,1:T(8,128)(2,1)S(1)} %bitcast.153, bf16[16,8,32,128]{3,2,1,0:T(8,128)(2,1)S(1)} %bitcast.156, pred[8,16,32]{2,1,0:T(8,128)(4,1)S(1)} %get-tuple-element.34, f32[16,64,128]{2,0,1:T(8,128)S(1)} %copy-done.14), kind=kOutput, calls=%fused_computation.21 | convolution fusion | flops 67502080 | bytes 2625536 | tf_op jit(solution)/shard_map/mbjk,jbkr->mjr/dot_general | solution.py:30
  70.0 0.0 copy-start.20
  70.0 0.0 copy-start.21
  70.1 0.0 copy-start.24
  70.1 0.0 copy-start.25
  70.1 2.6 %fusion.4 = f32[16,8,8,128]{3,2,1,0:T(8,128)S(1)} fusion(f32[16,64,128]{2,1,0:T(8,128)S(1)} %fusion.7, f32[16,64,128]{2,1,0:T(8,128)S(1)} %fusion.6, f32[16,64,128]{2,1,0:T(8,128)S(1)} %fusion.5, bf16[64,8,16,32]{0,3,2,1:T(8,128)(2,1)S(1)} %bitcast.146, bf16[16,8,32,128]{3,2,1,0:T(8,128)(2,1)S(1)} %bitcast.151, pred[8,16,32]{2,1,0:T(8,128)(4,1)S(1)} %fusion.40, ...), kind=kOutput, calls=%fused_computation.20 | convolution fusion | flops 67895296 | bytes 4198400 | tf_op jit(solution)/shard_map/mbjk,jbkr->mjr/dot_general | solution.py:30
  72.7 0.8 copy.111
  73.6 0.0 reduce-scatter.2.cloned.1.call-update
  73.6 62.6 %reduce-scatter.2.cloned.1.call-done = f32[64,256]{1,0:T(8,128)} async-done(((f32[64,2048]{1,0:T(8,128)}), f32[64,256]{1,0:T(8,128)}) %reduce-scatter.2.cloned.1.call-update) | async-done | bytes 65552 | tf_op jit(solution)/shard_map/reduce_scatter | solution.py:67
  136.2 0.0 copy-done.21
  136.2 1.5 %add_divide_fusion = f32[64,256]{1,0:T(8,128)} fusion(f32[64,256]{1,0:T(8,128)S(1)} %copy-done.20, f32[64,256]{1,0:T(8,128)} %reduce-scatter.2.cloned.1.call-done, f32[64,256]{1,0:T(8,128)S(1)} %copy-done.21, f32[256]{0:T(256)S(1)} %copy-done.24, f32[256]{0:T(256)S(1)} %copy-done.25), kind=kLoop, calls=%fused_computation.65 | loop fusion | flops 131072 | bytes 264192 | tf_op jit(solution)/shard_map/div | solution.py:69
  (38 shorter events, 0.1 us)
Async XLA Ops:
  7.2 2.8 %copy-start.23 = (s32[4,8,2]{1,2,0:T(2,128)S(1)}, s32[4,8,2]{1,2,0:T(2,128)}, u32[]{:S(2)}) copy-start(s32[4,8,2]{1,2,0:T(2,128)} %param.14) | copy-start | bytes 772
  7.2 3.0 %copy-start.22 = (s32[4,8,16]{2,1,0:T(8,128)S(1)}, s32[4,8,16]{2,1,0:T(8,128)}, u32[]{:S(2)}) copy-start(s32[4,8,16]{2,1,0:T(8,128)} %param.13) | copy-start | bytes 6148
  7.2 3.0 %copy-start.7 = (bf16[4,1024,256]{2,1,0:T(8,128)(2,1)S(1)}, bf16[4,1024,256]{2,1,0:T(8,128)(2,1)}, u32[]{:S(2)}) copy-start(bf16[4,1024,256]{2,1,0:T(8,128)(2,1)} %param.15) | copy-start | bytes 6291460
  7.2 39.5 %all-reduce.3.cloned.1.call-start = ((), (), s32[]{:S(2)}) async-start(), calls=%async_computation.2 | async-start | bytes 1048576 | tf_op jit(solution)/shard_map/psum | solution.py:9
  9.9 126.2 %reduce-scatter.2.cloned.1.call-start = ((), (), s32[]{:S(2)}) async-start(), calls=%async_computation.1 | async-start | bytes 589824 | tf_op jit(solution)/shard_map/reduce_scatter | solution.py:67
  10.2 2.9 %copy-start = (bf16[4,1024,512]{2,1,0:T(8,128)(2,1)S(1)}, bf16[4,1024,512]{2,1,0:T(8,128)(2,1)}, u32[]{:S(2)}) copy-start(bf16[4,1024,512]{2,1,0:T(8,128)(2,1)} %param.11) | copy-start | bytes 12582916
  13.1 2.6 %copy-start.1 = (bf16[4,16,256,128]{3,2,1,0:T(8,128)(2,1)S(1)}, bf16[4,16,256,128]{3,2,1,0:T(8,128)(2,1)}, u32[]{:S(2)}) copy-start(bf16[4,16,256,128]{3,2,1,0:T(8,128)(2,1)} %param.12) | copy-start | bytes 12582916
  46.7 3.0 %copy-start.10 = (bf16[8,128,2,128]{3,2,1,0:T(2,128)(2,1)S(1)}, bf16[8,128,2,128]{3,2,1,0:T(2,128)(2,1)}, u32[]{:S(2)}) copy-start(bf16[8,128,2,128]{3,2,1,0:T(2,128)(2,1)} %reshape_squeeze.41) | copy-start | bytes 1572868
  46.7 3.0 %copy-start.18 = (bf16[64,8,128]{2,0,1:T(8,128)(2,1)S(1)}, bf16[64,8,128]{2,0,1:T(8,128)(2,1)}, u32[]{:S(2)}) copy-start(bf16[64,8,128]{2,0,1:T(8,128)(2,1)} %get-tuple-element.4) | copy-start | bytes 393220
  46.7 4.7 %copy-start.9 = (bf16[8,128,2,128]{3,2,1,0:T(2,128)(2,1)S(1)}, bf16[8,128,2,128]{3,2,1,0:T(2,128)(2,1)}, u32[]{:S(2)}) copy-start(bf16[8,128,2,128]{3,2,1,0:T(2,128)(2,1)} %reshape_squeeze.47) | copy-start | bytes 1572868
  46.7 4.7 %copy-start.17 = (bf16[64,8,128]{2,0,1:T(8,128)(2,1)S(1)}, bf16[64,8,128]{2,0,1:T(8,128)(2,1)}, u32[]{:S(2)}) copy-start(bf16[64,8,128]{2,0,1:T(8,128)(2,1)} %get-tuple-element.2) | copy-start | bytes 393220
  49.7 3.5 %copy-start.8 = (bf16[8,128,2,128]{3,2,1,0:T(2,128)(2,1)S(1)}, bf16[8,128,2,128]{3,2,1,0:T(2,128)(2,1)}, u32[]{:S(2)}) copy-start(bf16[8,128,2,128]{3,2,1,0:T(2,128)(2,1)} %reshape_squeeze.44) | copy-start | bytes 1572868
  49.7 3.5 %copy-start.16 = (bf16[64,8,128]{2,0,1:T(8,128)(2,1)S(1)}, bf16[64,8,128]{2,0,1:T(8,128)(2,1)}, u32[]{:S(2)}) copy-start(bf16[64,8,128]{2,0,1:T(8,128)(2,1)} %get-tuple-element.3) | copy-start | bytes 393220
  51.4 3.6 %copy-start.2 = (bf16[1,1024,512]{2,1,0:T(8,128)(2,1)S(1)}, bf16[1,1024,512]{2,1,0:T(8,128)(2,1)}, u32[]{:S(2)}) copy-start(bf16[1,1024,512]{2,1,0:T(8,128)(2,1)} %get-tuple-element.10) | copy-start | bytes 3145732
  51.5 3.6 %copy-start.19 = (bf16[64,8,128]{2,0,1:T(8,128)(2,1)S(1)}, bf16[64,8,128]{2,0,1:T(8,128)(2,1)}, u32[]{:S(2)}) copy-start(bf16[64,8,128]{2,0,1:T(8,128)(2,1)} %get-tuple-element.5) | copy-start | bytes 393220
  57.6 3.0 %copy-start.6 = (bf16[64,8,512]{2,0,1:T(8,128)(2,1)S(1)}, bf16[64,8,512]{2,0,1:T(8,128)(2,1)}, u32[]{:S(2)}) copy-start(bf16[64,8,512]{2,0,1:T(8,128)(2,1)} %convolution_bitcast_fusion.2) | copy-start | bytes 1572868
  57.9 3.2 %copy-start.5 = (bf16[64,8,512]{2,0,1:T(8,128)(2,1)S(1)}, bf16[64,8,512]{2,0,1:T(8,128)(2,1)}, u32[]{:S(2)}) copy-start(bf16[64,8,512]{2,0,1:T(8,128)(2,1)} %convolution_bitcast_fusion.3) | copy-start | bytes 1572868
  61.6 3.2 %copy-start.11 = (bf16[64,8,512]{0,2,1:T(8,128)(2,1)S(1)}, bf16[64,8,512]{0,2,1:T(8,128)(2,1)}, u32[]{:S(2)}) copy-start(bf16[64,8,512]{0,2,1:T(8,128)(2,1)} %copy.37) | copy-start | bytes 1572868
  61.6 3.2 %copy-start.13 = (bf16[1,16,256,128]{3,2,1,0:T(8,128)(2,1)S(1)}, bf16[1,16,256,128]{3,2,1,0:T(8,128)(2,1)}, u32[]{:S(2)}) copy-start(bf16[1,16,256,128]{3,2,1,0:T(8,128)(2,1)} %get-tuple-element.8) | copy-start | bytes 3145732
  61.6 3.2 %copy-start.15 = (f32[16,64,128]{2,0,1:T(8,128)S(1)}, f32[16,64,128]{2,0,1:T(8,128)}, u32[]{:S(2)}) copy-start(f32[16,64,128]{2,0,1:T(8,128)} %convolution_bitcast_fusion.8) | copy-start | bytes 1572868
  64.8 2.6 %copy-start.12 = (bf16[1,16,256,128]{3,2,1,0:T(8,128)(2,1)S(1)}, bf16[1,16,256,128]{3,2,1,0:T(8,128)(2,1)}, u32[]{:S(2)}) copy-start(bf16[1,16,256,128]{3,2,1,0:T(8,128)(2,1)} %get-tuple-element.7) | copy-start | bytes 3145732
  64.8 2.6 %copy-start.14 = (f32[16,64,128]{2,0,1:T(8,128)S(1)}, f32[16,64,128]{2,0,1:T(8,128)}, u32[]{:S(2)}) copy-start(f32[16,64,128]{2,0,1:T(8,128)} %convolution_bitcast_fusion.10) | copy-start | bytes 1572868
  67.4 2.6 %copy-start.3 = (bf16[1,16,256,128]{3,2,1,0:T(8,128)(2,1)S(1)}, bf16[1,16,256,128]{3,2,1,0:T(8,128)(2,1)}, u32[]{:S(2)}) copy-start(bf16[1,16,256,128]{3,2,1,0:T(8,128)(2,1)} %get-tuple-element.6) | copy-start | bytes 3145732
  67.4 2.6 %copy-start.4 = (f32[16,64,128]{2,0,1:T(8,128)S(1)}, f32[16,64,128]{2,0,1:T(8,128)}, u32[]{:S(2)}) copy-start(f32[16,64,128]{2,0,1:T(8,128)} %convolution_bitcast_fusion.11) | copy-start | bytes 1572868
  70.0 66.1 %copy-start.20 = (f32[64,256]{1,0:T(8,128)S(1)}, f32[64,256]{1,0:T(8,128)}, u32[]{:S(2)}) copy-start(f32[64,256]{1,0:T(8,128)} %param.16) | copy-start | bytes 196612
  70.0 66.1 %copy-start.21 = (f32[64,256]{1,0:T(8,128)S(1)}, f32[64,256]{1,0:T(8,128)}, u32[]{:S(2)}) copy-start(f32[64,256]{1,0:T(8,128)} %param.17) | copy-start | bytes 196612
  70.1 66.1 %copy-start.24 = (f32[256]{0:T(256)S(1)}, f32[256]{0:T(256)}, u32[]{:S(2)}) copy-start(f32[256]{0:T(256)} %param.18) | copy-start | bytes 3076
  70.1 66.1 %copy-start.25 = (f32[256]{0:T(256)S(1)}, f32[256]{0:T(256)}, u32[]{:S(2)}) copy-start(f32[256]{0:T(256)} %param.19) | copy-start | bytes 3076
Sparse Core Ops, SparseCore 0:
  10.6 36.0 all-reduce.2
  73.7 62.4 reduce-scatter.1
where the time goes:
time: 145 us
  waiting for transfers between devices  83.2 us (57%)
  matrix products  22.1 us (15%)
  local copies, waits for them, and re-layouts  21.6 us (15%)
  between operations  14.4 us (10%)
  other arithmetic  3.18 us (2%)
    reduce_scatter x1, waiting for transfers between devices, body(): lax.psum_scatter(partials, 'row', scatter_dimension=1, tiled=True)  62.6 us
    psum x1, waiting for transfers between devices, from_root(): return lax.psum(block, axis)  20.6 us
    dot_general x4, matrix products, section_stress(): jnp.einsum('mbjk,jbkr->mjr', coeffs, right_factor.reshape(receivers, coun...  11 us
    another operation x4, local copies, waits for them, and re-layouts, section_stress(): dense_blocks.reshape(count, width, slots, width)  7.88 us
    dot_general x4, matrix products, section_stress(): jnp.einsum('mbqr,bqj->mjr', dense_out, near_hits.astype(jnp.float32), pre...  6.21 us
    transpose x4, local copies, waits for them, and re-layouts, section_stress(): jnp.einsum('mbs,bsq->mbq', source_rows, left_factor.reshape(count, width,...  3.62 us
  transfers between devices with their start and end apart: 2, of which 2 were waited for; matrix products, arithmetic and copies ran while one was open for 9% of the time, Pallas kernels for 0%

commit v1 on v0

v1 whole, which is shorter than its diff:
```python
import functools

import jax
import jax.numpy as jnp
from jax import lax
from jax.experimental import pallas as pl
from jax.experimental.pallas import tpu as pltpu
from jax.sharding import PartitionSpec as P

BF16, F32, I32 = jnp.bfloat16, jnp.float32, jnp.int32
LANES = 128
VMEM_LIMIT = 16 * 2**20


def dot(left, right):
    return jnp.dot(left, right, preferred_element_type=F32)


def keep_masks(ranks, slots):
    count, receivers = ranks.shape
    kmax = 32
    width = receivers * kmax
    block = lax.broadcasted_iota(I32, (count, receivers), 1)
    for slot in range(slots.shape[1]):
        ranks = jnp.where(slots[:, slot : slot + 1] == block, 0, ranks)
    lane = lax.broadcasted_iota(I32, (receivers, width), 1)
    spread = lane // kmax == lax.broadcasted_iota(I32, (receivers, width), 0)
    wide = dot(ranks.astype(F32).astype(BF16), spread.astype(BF16))
    rank_index = lax.broadcasted_iota(I32, (count, width), 1) % kmax
    return (rank_index.astype(F32) < wide).astype(F32)


def regrouped(parts, lane):
    half = lane >= 64
    odd = (lane // 32) % 2 == 1
    swapped = [None] * 4
    for i in range(2):
        low, high = parts[i], parts[i + 2]
        swapped[i] = jnp.where(half, pltpu.roll(high, 64, 1), low)
        swapped[i + 2] = jnp.where(half, high, pltpu.roll(low, 64, 1))
    out = [None] * 4
    for i in (0, 2):
        low, high = swapped[i], swapped[i + 1]
        out[i] = jnp.where(odd, pltpu.roll(high, 32, 1), low)
        out[i + 1] = jnp.where(odd, high, pltpu.roll(low, 96, 1))
    return out


def add_section(slip, u_ref, v_ref, near_ref, ranks, slots, slot_at, total, coeffs):
    receivers = total.shape[0]
    count = ranks.shape[0]
    kept = keep_masks(ranks, slots)
    lane = lax.broadcasted_iota(I32, (1, LANES), 1)
    for first in range(0, count, 4):
        projected = []
        for b in range(first, first + 4):
            rows = slice(b * LANES, (b + 1) * LANES)
            value = dot(slip[:, rows], u_ref[rows, :])
            projected.append(jnp.where(kept[b : b + 1, :] > 0, value, 0.0))
        for group in range(receivers // 4):
            lanes = slice(group * LANES, (group + 1) * LANES)
            pieces = regrouped([p[:, lanes] for p in projected], lane)
            for i, piece in enumerate(pieces):
                coeffs[group * 4 + i, :, first * 32 : (first + 4) * 32] = piece.astype(BF16)
    for b in range(count):
        rows = slice(b * LANES, (b + 1) * LANES)
        dense = dot(slip[:, rows], near_ref[rows, :])
        for slot in range(slots.shape[1]):
            total[slot_at(b, slot)] += dense[:, slot * LANES : (slot + 1) * LANES]
    for j in range(receivers):
        total[j] += dot(coeffs[j], v_ref[j])


def stress_kernel(axis, offsets, final, *refs):
    slips = refs[: len(offsets)]
    u_ref, v_ref, near_ref, ranks_ref, slots_ref, slots_smem = refs[len(offsets) : len(offsets) + 6]
    rest = refs[len(offsets) + 6 :]
    if len(rest) == 4:
        start_ref, out_ref, total, coeffs = rest
        total[...] = start_ref[...]
    else:
        out_ref, total, coeffs = rest
        total[...] = jnp.zeros_like(total)
    me = lax.axis_index(axis)
    for slip_ref, offset in zip(slips, offsets):
        s = me ^ offset
        add_section(
            slip_ref[...],
            u_ref.at[s],
            v_ref.at[s],
            near_ref.at[s],
            ranks_ref[s],
            slots_ref[s],
            lambda b, slot: slots_smem[s, b, slot],
            total,
            coeffs,
        )
    if not final:
        out_ref[...] = total[...]
    else:
        owners, _, owned = out_ref.shape
        for r in range(owners):
            for at in range(0, owned, LANES):
                take = min(owned, LANES)
                j, lane = divmod(r * owned + at, LANES)
                out_ref[r, :, at : at + take] = total[j, :, lane : lane + take].astype(BF16)


def stress(slips, offsets, weights, start, out_shape, final):
    u, v, near, ranks, slots = weights
    members = slips[0].shape[0]
    receivers, kdim = v.shape[1], v.shape[2]
    used = len(slips) * (u.size + v.size + near.size) // u.shape[0]
    vmem = pl.BlockSpec(memory_space=pltpu.VMEM)
    args = [*slips, u, v, near, ranks, slots, slots]
    specs = [vmem] * (len(args) - 1) + [pl.BlockSpec(memory_space=pltpu.SMEM)]
    if start is not None:
        args.append(start)
        specs.append(vmem)
    return pl.pallas_call(
        functools.partial(stress_kernel, "col", offsets, final),
        out_shape=out_shape,
        in_specs=specs,
        out_specs=vmem,
        scratch_shapes=[
            pltpu.VMEM((receivers, members, LANES), F32),
            pltpu.VMEM((receivers, members, kdim), BF16),
        ],
        compiler_params=pltpu.CompilerParams(vmem_limit_bytes=VMEM_LIMIT),
        cost_estimate=pl.CostEstimate(
            flops=2 * members * used,
            bytes_accessed=2 * used,
            transcendentals=0,
        ),
    )(*args)


def swapped_with(value, offset, groups):
    return lax.ppermute(value, "col", [(i, i ^ offset) for i in range(groups)])


def body(
    slip, lowrank_u, lowrank_v, ranks, near_slot, near_blocks, velocity, theta, a_sigma, b_sigma
):
    groups = lax.axis_size("col")
    owners = lax.axis_size("row")
    members = slip.shape[0]
    receivers = lowrank_v.shape[1]
    owned = velocity.shape[1]
    weights = [
        pltpu.with_memory_space_constraint(w, pltpu.VMEM) for w in (lowrank_u, lowrank_v, near_blocks)
    ] + [ranks, near_slot]
    across = swapped_with(slip, 2, groups)
    sibling = swapped_with(slip, 1, groups)
    total_shape = jax.ShapeDtypeStruct((receivers, members, LANES), F32)
    total = stress([slip, sibling], (0, 1), weights, None, total_shape, False)
    beyond = swapped_with(across, 1, groups)
    total = stress([across], (2,), weights, total, total_shape, False)
    sent_shape = jax.ShapeDtypeStruct((owners, members, owned), BF16)
    sent = stress([beyond], (3,), weights, total, sent_shape, True)
    received = lax.all_to_all(sent, "row", 0, 0, tiled=True)
    owned_rows = jnp.sum(received.astype(F32), axis=0)
    theta_rate = 1.0 - velocity * theta
    accel = (owned_rows - b_sigma[None, :] * theta_rate / theta) / (
        a_sigma[None, :] / velocity + 0.5
    )
    return (owned_rows, accel)


def solution(mesh):
    placed = (
        P(None, ("col", "row")),
        P(None, "row", "col"),
        P(None, "col", "row", None),
        P(None, "row", "col"),
        P(None, "row", "col"),
        P(None, "row", "col"),
        P(None, ("col", "row")),
        P(None, ("col", "row")),
        P(("col", "row")),
        P(("col", "row")),
    )
    return jax.shard_map(
        body,
        mesh=mesh,
        in_specs=placed,
        out_specs=(P(None, ("col", "row")), P(None, ("col", "row"))),
        check_vma=False,
    )
```

time: 145 us -> 40 us (0.28)
  waiting for transfers between devices: 83.2 us -> 3.71 us
  matrix products: 22.1 us -> 0 us
  blocking collectives: 0 us -> 15.5 us
  between operations: 14.4 us -> 0.75 us
  local copies, waits for them, and re-layouts: 21.6 us -> 9.95 us
  Pallas kernels: 0 us -> 6.02 us
  starting transfers between devices: 0.08 us -> 3.01 us
  other arithmetic: 3.18 us -> 0.71 us
    reduce_scatter x1 -> x0, waiting for transfers between devices: 62.6 us -> none  [body(): lax.psum_scatter(partials, 'row', scatter_dimension=1, tiled=True)]
    dot_general x16 -> x0, matrix products: 22.1 us -> none  [the longest x4 11 us: section_stress(): jnp.einsum('mbjk,jbkr->mjr', coeffs, right_factor.reshape(receivers, coun...]
    psum x1 -> x0, waiting for transfers between devices: 20.6 us -> none  [from_root(): return lax.psum(block, axis)]
    all_to_all x0 -> x1, blocking collectives: none -> 15.5 us  [body(): received = lax.all_to_all(sent, 'row', 0, 0, tiled=True)]
    another operation x4 -> x0, local copies, waits for them, and re-layouts: 7.88 us -> none  [section_stress(): dense_blocks.reshape(count, width, slots, width)]
    unnamed x52 -> x29, local copies, waits for them, and re-layouts: 2.8 us -> 9.95 us
    pallas_call x0 -> x3, Pallas kernels: none -> 6.02 us  [stress(): pl.pallas_call(functools.partial(stress_kernel, 'col', offsets, final), o...]
    slice x3 -> x0, local copies, waits for them, and re-layouts: 4.89 us -> none  [the longest x1 2.08 us: body(): lowrank_v[section_index]]
  transfers between devices with their start and end apart: 2 -> 3, of which waited for: 2 -> 1; matrix products, arithmetic and copies ran while one was open for 9% -> 2% of each run, Pallas kernels for 0% -> 11%
where the time goes in v1:
time: 40 us; the launch traced here: 39.6 us
  blocking collectives  15.5 us (39%)
  local copies, waits for them, and re-layouts  9.95 us (25%)
  Pallas kernels  6.02 us (15%)
  waiting for transfers between devices  3.71 us (9%)
  starting transfers between devices  3.01 us (8%)
  between operations  0.75 us (2%)
  other arithmetic  0.71 us (2%)
    all_to_all x1, blocking collectives, body(): received = lax.all_to_all(sent, 'row', 0, 0, tiled=True)  15.5 us
    unnamed x29, local copies, waits for them, and re-layouts  9.95 us
    pallas_call x3, Pallas kernels, stress(): pl.pallas_call(functools.partial(stress_kernel, 'col', offsets, final), o...  6.02 us
    ppermute x3, waiting for transfers between devices, swapped_with(): return lax.ppermute(value, 'col', [(i, i ^ offset) for i in range(groups)])  3.71 us
    ppermute x3, starting transfers between devices, swapped_with(): return lax.ppermute(value, 'col', [(i, i ^ offset) for i in range(groups)])  3.01 us
  transfers between devices with their start and end apart: 3, of which 1 were waited for; matrix products, arithmetic and copies ran while one was open for 2% of the time, Pallas kernels for 11%

profile of v1, /device:TPU:0, one launch (start us, length us, event | category | flops | bytes accessed | tf_op | source)
XLA Modules:
  0.0 39.6 jit_solution(5322771476636588234)
XLA Ops:
  0.6 3.0 %collective-permute-start = (bf16[64,1024]{1,0:T(8,128)(2,1)}, bf16[64,1024]{1,0:T(8,128)(2,1)S(1)}, u32[]{:S(2)}, u32[]{:S(2)}) collective-permute-start(bf16[64,1024]{1,0:T(8,128)(2,1)} %refs_0_.1), channel_id=1, source_target_pairs={{0,16},{8,24},{16,0},{24,8},{1,17},{9,25},{17,1},{25,9},{2,18},{10... | collective-permute-start | bytes 393224 | tf_op jit(solution)/shard_map/ppermute | solution.py:139
  3.6 0.0 collective-permute-start.2
  3.6 3.7 %collective-permute-done.refs_0_ = bf16[64,1024]{1,0:T(8,128)(2,1)S(1)} collective-permute-done((bf16[64,1024]{1,0:T(8,128)(2,1)}, bf16[64,1024]{1,0:T(8,128)(2,1)S(1)}, u32[]{:S(2)}, u32[]{:S(2)}) %collective-permute-start) | collective-permute-done | bytes 131104 | tf_op jit(solution)/shard_map/ppermute | solution.py:139
  7.3 0.0 collective-permute-start.1
  7.3 0.8 %copy.16.refs_6_.refs_7_.refs_5_ = s32[4,8,2]{2,1,0:T(8,128)S(1)} copy(s32[4,8,2]{1,2,0:T(2,128)} %param.14) | data formatting | bytes 512 | tf_op args[4]
  8.1 0.0 collective-permute-done.2.refs_1_
  8.1 0.0 copy-start
  8.1 2.2 %copy-done = bf16[4,1024,512]{2,1,0:T(8,128)(2,1)S(1)} copy-done((bf16[4,1024,512]{2,1,0:T(8,128)(2,1)S(1)}, bf16[4,1024,512]{2,1,0:T(8,128)(2,1)}, u32[]{:S(2)}) %copy-start) | copy-done | bytes 4194328
  10.3 0.0 copy-start.2
  10.3 2.2 %copy-done.2 = bf16[4,16,256,128]{3,2,1,0:T(8,128)(2,1)S(1)} copy-done((bf16[4,16,256,128]{3,2,1,0:T(8,128)(2,1)S(1)}, bf16[4,16,256,128]{3,2,1,0:T(8,128)(2,1)}, u32[]{:S(2)}) %copy-start.2) | copy-done | bytes 4194328
  12.5 0.0 copy-start.4
  12.5 1.6 %copy-done.4 = bf16[4,1024,256]{2,1,0:T(8,128)(2,1)S(1)} copy-done((bf16[4,1024,256]{2,1,0:T(8,128)(2,1)S(1)}, bf16[4,1024,256]{2,1,0:T(8,128)(2,1)}, u32[]{:S(2)}) %copy-start.4) | copy-done | bytes 2097176
  14.1 0.0 copy-start.6
  14.1 0.7 %copy-done.6 = s32[4,8,16]{2,1,0:T(8,128)S(1)} copy-done((s32[4,8,16]{2,1,0:T(8,128)S(1)}, s32[4,8,16]{2,1,0:T(8,128)}, u32[]{:S(2)}) %copy-start.6) | copy-done | bytes 2072
  14.8 0.0 copy-start.8
  14.8 0.9 %copy-done.8 = bf16[64,1024]{1,0:T(8,128)(2,1)S(1)} copy-done((bf16[64,1024]{1,0:T(8,128)(2,1)S(1)}, bf16[64,1024]{1,0:T(8,128)(2,1)}, u32[]{:S(2)}) %copy-start.8) | copy-done | bytes 131096
  15.7 0.0 copy-start.1
  15.7 0.0 copy-start.3
  15.7 0.0 copy-start.5
  15.7 2.5 %shard_map.113.refs_7_ = f32[16,64,128]{2,1,0:T(8,128)S(1)} custom-call(bf16[64,1024]{1,0:T(8,128)(2,1)S(1)} %copy-done.8, bf16[64,1024]{1,0:T(8,128)(2,1)S(1)} %collective-permute-done.2.refs_1_, bf16[4,1024,512]{2,1,0:T(8,128)(2,1)S(1)} %copy-done, bf16[4,16,256,128]{3,2,1,0:T(8,128)(2,1)S(1)} %copy-done.2, bf16[4,1024,256]{2,1,0:T(8,128)(2,1)S(1)} %copy-done.4, ...), custom_call_target="tpu_custom_call" | custom-call | flops 335544320 | bytes 5242880 | tf_op jit(solution)/shard_map/pallas_call | solution.py:120
  18.2 0.0 copy-done.1
  18.2 0.9 %copy-done.3 = bf16[4,16,256,128]{3,2,1,0:T(8,128)(2,1)S(1)} copy-done((bf16[4,16,256,128]{3,2,1,0:T(8,128)(2,1)S(1)}, bf16[4,16,256,128]{3,2,1,0:T(8,128)(2,1)}, u32[]{:S(2)}) %copy-start.3) | copy-done | bytes 4194328
  19.2 0.6 %copy-done.5 = bf16[4,1024,256]{2,1,0:T(8,128)(2,1)S(1)} copy-done((bf16[4,1024,256]{2,1,0:T(8,128)(2,1)S(1)}, bf16[4,1024,256]{2,1,0:T(8,128)(2,1)}, u32[]{:S(2)}) %copy-start.5) | copy-done | bytes 2097176
  19.8 0.0 copy-start.7
  19.8 1.8 %shard_map.114.refs_7_ = f32[16,64,128]{2,1,0:T(8,128)S(1)} custom-call(bf16[64,1024]{1,0:T(8,128)(2,1)S(1)} %collective-permute-done.refs_0_, bf16[4,1024,512]{2,1,0:T(8,128)(2,1)S(1)} %copy-done.1, bf16[4,16,256,128]{3,2,1,0:T(8,128)(2,1)S(1)} %copy-done.3, bf16[4,1024,256]{2,1,0:T(8,128)(2,1)S(1)} %copy-done.5, s32[4,8,16]{2,1,0:T(8,128)S(1)} %copy-done.6, ...), custom_call_target="tpu_custom_call" | custom-call | flops 167772160 | bytes 2621440 | tf_op jit(solution)/shard_map/pallas_call | solution.py:120
  21.5 0.0 copy-start.10
  21.6 0.0 copy-start.11
  21.6 0.0 copy-start.12
  21.6 0.0 copy-start.13
  21.6 0.0 collective-permute-done.1.refs_0_
  21.6 0.0 copy-done.7
  21.6 1.8 %shard_map.115 = bf16[8,64,256]{2,1,0:T(8,128)(2,1)S(1)} custom-call(bf16[64,1024]{1,0:T(8,128)(2,1)S(1)} %collective-permute-done.1.refs_0_, bf16[4,1024,512]{2,1,0:T(8,128)(2,1)S(1)} %copy-done.1, bf16[4,16,256,128]{3,2,1,0:T(8,128)(2,1)S(1)} %copy-done.3, bf16[4,1024,256]{2,1,0:T(8,128)(2,1)S(1)} %copy-done.5, s32[4,8,16]{2,1,0:T(8,128)S(1)} %copy-done.7, ...), custom_call_target="tpu_custom_call" | custom-call | flops 167772160 | bytes 2621440 | tf_op jit(solution)/shard_map/pallas_call | solution.py:120
  23.4 15.5 %all_to_all.5 = bf16[8,64,256]{2,1,0:T(8,128)(2,1)S(1)} all-to-all(bf16[8,64,256]{2,1,0:T(8,128)(2,1)S(1)} %shard_map.115), channel_id=1, replica_groups=mesh['col'=4,'row'=8] {'row'}, dimensions={0} | all-to-all | bytes 524288 | tf_op jit(solution)/shard_map/all_to_all | solution.py:161
  38.9 0.0 copy-done.10
  38.9 0.0 copy-done.11
  38.9 0.0 copy-done.12
  38.9 0.0 copy-done.13
  38.9 0.0 copy-start.9
  38.9 0.7 %add_divide_fusion = f32[64,256]{1,0:T(8,128)} fusion(f32[64,256]{1,0:T(8,128)S(1)} %copy-done.10, f32[64,256]{1,0:T(8,128)S(1)} %convert_reduce_fusion, f32[64,256]{1,0:T(8,128)S(1)} %copy-done.11, f32[256]{0:T(256)S(1)} %copy-done.12, f32[256]{0:T(256)S(1)} %copy-done.13), kind=kLoop, calls=%fused_computation.1 | loop fusion | flops 131072 | bytes 264192 | tf_op jit(solution)/shard_map/div | solution.py:164
  39.6 0.0 copy-done.9
  (1 shorter events, 0.0 us)
Async XLA Ops:
  0.6 6.7 %collective-permute-start = (bf16[64,1024]{1,0:T(8,128)(2,1)}, bf16[64,1024]{1,0:T(8,128)(2,1)S(1)}, u32[]{:S(2)}, u32[]{:S(2)}) collective-permute-start(bf16[64,1024]{1,0:T(8,128)(2,1)} %refs_0_.1), channel_id=1, source_target_pairs={{0,16},{8,24},{16,0},{24,8},{1,17},{9,25},{17,1},{25,9},{2,18},{10... | collective-permute-start | bytes 393224 | tf_op jit(solution)/shard_map/ppermute | solution.py:139
  3.6 4.5 %collective-permute-start.2 = (bf16[64,1024]{1,0:T(8,128)(2,1)}, bf16[64,1024]{1,0:T(8,128)(2,1)S(1)}, u32[]{:S(2)}, u32[]{:S(2)}) collective-permute-start(bf16[64,1024]{1,0:T(8,128)(2,1)} %refs_0_.1), channel_id=1, source_target_pairs={{0,8},{8,0},{16,24},{24,16},{1,9},{9,1},{17,25},{25,17},{2,10},{10... | collective-permute-start | bytes 393224 | tf_op jit(solution)/shard_map/ppermute | solution.py:139
  7.3 14.3 %collective-permute-start.1 = (bf16[64,1024]{1,0:T(8,128)(2,1)S(1)}, bf16[64,1024]{1,0:T(8,128)(2,1)S(1)}, u32[]{:S(2)}, u32[]{:S(2)}) collective-permute-start(bf16[64,1024]{1,0:T(8,128)(2,1)S(1)} %collective-permute-done.refs_0_), channel_id=1, source_target_pairs={{0,8},{8,0},{16,24},{24,16},{1,9},{9,1},{17,25},{25,17},{2,10},{10... | collective-permute-start | bytes 393224 | tf_op jit(solution)/shard_map/ppermute | solution.py:139
  8.1 2.2 %copy-start = (bf16[4,1024,512]{2,1,0:T(8,128)(2,1)S(1)}, bf16[4,1024,512]{2,1,0:T(8,128)(2,1)}, u32[]{:S(2)}) copy-start(bf16[4,1024,512]{2,1,0:T(8,128)(2,1)} %refs_1_.3) | copy-start | bytes 12582916
  10.3 2.2 %copy-start.2 = (bf16[4,16,256,128]{3,2,1,0:T(8,128)(2,1)S(1)}, bf16[4,16,256,128]{3,2,1,0:T(8,128)(2,1)}, u32[]{:S(2)}) copy-start(bf16[4,16,256,128]{3,2,1,0:T(8,128)(2,1)} %refs_2_.5) | copy-start | bytes 12582916
  12.5 1.6 %copy-start.4 = (bf16[4,1024,256]{2,1,0:T(8,128)(2,1)S(1)}, bf16[4,1024,256]{2,1,0:T(8,128)(2,1)}, u32[]{:S(2)}) copy-start(bf16[4,1024,256]{2,1,0:T(8,128)(2,1)} %refs_3_.5) | copy-start | bytes 6291460
  14.1 0.7 %copy-start.6 = (s32[4,8,16]{2,1,0:T(8,128)S(1)}, s32[4,8,16]{2,1,0:T(8,128)}, u32[]{:S(2)}) copy-start(s32[4,8,16]{2,1,0:T(8,128)} %refs_4_.5) | copy-start | bytes 6148
  14.8 0.9 %copy-start.8 = (bf16[64,1024]{1,0:T(8,128)(2,1)S(1)}, bf16[64,1024]{1,0:T(8,128)(2,1)}, u32[]{:S(2)}) copy-start(bf16[64,1024]{1,0:T(8,128)(2,1)} %refs_0_.1) | copy-start | bytes 393220
  15.7 2.5 %copy-start.1 = (bf16[4,1024,512]{2,1,0:T(8,128)(2,1)S(1)}, bf16[4,1024,512]{2,1,0:T(8,128)(2,1)}, u32[]{:S(2)}) copy-start(bf16[4,1024,512]{2,1,0:T(8,128)(2,1)} %refs_1_.3) | copy-start | bytes 12582916
  15.7 3.5 %copy-start.3 = (bf16[4,16,256,128]{3,2,1,0:T(8,128)(2,1)S(1)}, bf16[4,16,256,128]{3,2,1,0:T(8,128)(2,1)}, u32[]{:S(2)}) copy-start(bf16[4,16,256,128]{3,2,1,0:T(8,128)(2,1)} %refs_2_.5) | copy-start | bytes 12582916
  15.7 4.1 %copy-start.5 = (bf16[4,1024,256]{2,1,0:T(8,128)(2,1)S(1)}, bf16[4,1024,256]{2,1,0:T(8,128)(2,1)}, u32[]{:S(2)}) copy-start(bf16[4,1024,256]{2,1,0:T(8,128)(2,1)} %refs_3_.5) | copy-start | bytes 6291460
  19.8 1.8 %copy-start.7 = (s32[4,8,16]{2,1,0:T(8,128)S(1)}, s32[4,8,16]{2,1,0:T(8,128)}, u32[]{:S(2)}) copy-start(s32[4,8,16]{2,1,0:T(8,128)} %refs_4_.5) | copy-start | bytes 6148
  21.5 17.3 %copy-start.10 = (f32[64,256]{1,0:T(8,128)S(1)}, f32[64,256]{1,0:T(8,128)}, u32[]{:S(2)}) copy-start(f32[64,256]{1,0:T(8,128)} %param.16) | copy-start | bytes 196612
  21.6 17.3 %copy-start.11 = (f32[64,256]{1,0:T(8,128)S(1)}, f32[64,256]{1,0:T(8,128)}, u32[]{:S(2)}) copy-start(f32[64,256]{1,0:T(8,128)} %param.17) | copy-start | bytes 196612
  21.6 17.3 %copy-start.12 = (f32[256]{0:T(256)S(1)}, f32[256]{0:T(256)}, u32[]{:S(2)}) copy-start(f32[256]{0:T(256)} %param.18) | copy-start | bytes 3076
  21.6 17.3 %copy-start.13 = (f32[256]{0:T(256)S(1)}, f32[256]{0:T(256)}, u32[]{:S(2)}) copy-start(f32[256]{0:T(256)} %param.19) | copy-start | bytes 3076
  38.9 0.7 %copy-start.9 = (f32[64,256]{1,0:T(8,128)}, f32[64,256]{1,0:T(8,128)S(1)}, u32[]{:S(2)}) copy-start(f32[64,256]{1,0:T(8,128)S(1)} %convert_reduce_fusion) | copy-start | bytes 196612

commit v2 on v0

v2 whole, which is shorter than its diff:
```python
import functools

import jax
import jax.numpy as jnp
from jax import lax
from jax.experimental import pallas as pl
from jax.experimental.pallas import tpu as pltpu
from jax.sharding import PartitionSpec as P

BF16, F32, I32 = jnp.bfloat16, jnp.float32, jnp.int32
LANES = 128
KMAX = 32
VMEM_LIMIT = 32 * 2**20
HBM_SPEC = pl.BlockSpec(memory_space=pltpu.HBM)
VMEM_SPEC = pl.BlockSpec(memory_space=pltpu.VMEM)


def dot(left, right):
    return jnp.dot(left, right, preferred_element_type=F32)


def regrouped(parts, lane):
    half = lane >= 64
    odd = (lane // KMAX) % 2 == 1
    swapped = [None] * 4
    for i in range(2):
        low, high = parts[i], parts[i + 2]
        swapped[i] = jnp.where(half, pltpu.roll(high, 64, 1), low)
        swapped[i + 2] = jnp.where(half, high, pltpu.roll(low, 64, 1))
    out = [None] * 4
    for i in (0, 2):
        low, high = swapped[i], swapped[i + 1]
        out[i] = jnp.where(odd, pltpu.roll(high, 32, 1), low)
        out[i + 1] = jnp.where(odd, high, pltpu.roll(low, 96, 1))
    return out


def add_section(slip, u_ref, v_ref, near_ref, kept_ref, slot_at, start, total, coeffs):
    receivers = total.shape[0]
    count = kept_ref.shape[0]
    slots = near_ref.shape[1] // LANES
    lane = lax.broadcasted_iota(I32, (1, LANES), 1)
    for first in range(0, count, 4):
        projected = []
        for b in range(first, first + 4):
            rows = slice(b * LANES, (b + 1) * LANES)
            value = dot(slip[:, rows], u_ref[rows, :])
            projected.append(jnp.where(kept_ref[b : b + 1, :] > 0, value, 0.0))
        for group in range(receivers // 4):
            lanes = slice(group * LANES, (group + 1) * LANES)
            pieces = regrouped([p[:, lanes] for p in projected], lane)
            for i, piece in enumerate(pieces):
                coeffs[group * 4 + i, :, first * KMAX : (first + 4) * KMAX] = piece.astype(BF16)
    for j in range(receivers):
        value = dot(coeffs[j], v_ref[j])
        total[j] = value if start is None else start[j] + value
    for b in range(count):
        rows = slice(b * LANES, (b + 1) * LANES)
        dense = dot(slip[:, rows], near_ref[rows, :])
        for slot in range(slots):
            total[slot_at(slot, b)] += dense[:, slot * LANES : (slot + 1) * LANES]


def first_kernel(
    slip_hbm, sibling, u_hbm, v_hbm, near_hbm, ranks_hbm, slots_hbm, velocity_hbm, theta_hbm,
    a_hbm, b_hbm,
    total, u_out, v_out, near_out, kept_out, gain, shift,
    slip, u_in, v_in, near_in, ranks, slots, velocity, theta, a_sigma, b_sigma, kept, coeffs, sems,
):
    me = lax.axis_index("col")
    used = iter(range(sems.shape[0]))

    def fetch(source, target):
        copy = pltpu.make_async_copy(source, target, sems.at[next(used)])
        copy.start()
        return copy

    small = [fetch(ranks_hbm, ranks), fetch(slots_hbm, slots)]
    loads = []
    for i in range(2):
        s = me ^ i
        loads.append([fetch(u_hbm.at[s], u_in.at[i])])
        if i == 0:
            loads[0].append(fetch(slip_hbm, slip))
        loads[i].append(fetch(v_hbm.at[s], v_in.at[i]))
        loads[i].append(fetch(near_hbm.at[s], near_in.at[i]))
    params = [
        fetch(velocity_hbm, velocity),
        fetch(theta_hbm, theta),
        fetch(a_hbm, a_sigma),
        fetch(b_hbm, b_sigma),
    ]
    later = []
    for i in range(2):
        s = me ^ (2 + i)
        later.append(fetch(u_hbm.at[s], u_out.at[i]))
        later.append(fetch(v_hbm.at[s], v_out.at[i]))
        later.append(fetch(near_hbm.at[s], near_out.at[i]))

    for copy in small:
        copy.wait()
    _, count, receivers = ranks.shape
    width = receivers * KMAX
    column = lax.broadcasted_iota(I32, (receivers, width), 1)
    spread = column // KMAX == lax.broadcasted_iota(I32, (receivers, width), 0)
    lane = lax.broadcasted_iota(I32, (1, width), 1)
    block, index = lane // KMAX, (lane % KMAX).astype(F32)
    for i in range(4):
        s = me ^ i
        wide = dot(ranks[s].astype(F32).astype(BF16), spread.astype(BF16))
        target = kept.at[i] if i < 2 else kept_out.at[i - 2]
        for b in range(count):
            keep = index < wide[b : b + 1, :]
            for slot in range(slots.shape[1]):
                keep = keep & (block != slots[s, slot, b])
            target[b : b + 1, :] = keep.astype(F32)

    for i in range(2):
        s = me ^ i
        for copy in loads[i]:
            copy.wait()
        add_section(
            slip[...] if i == 0 else sibling[...],
            u_in.at[i], v_in.at[i], near_in.at[i], kept.at[i],
            lambda slot, b: slots[s, slot, b],
            None if i == 0 else total, total, coeffs,
        )
    for copy in params:
        copy.wait()
    rate, state = velocity[...], theta[...]
    divisor = 1.0 / (a_sigma[...] / rate + 0.5)
    gain[...] = divisor
    shift[...] = -(b_sigma[...] * (1.0 - rate * state) / state) * divisor
    for copy in later:
        copy.wait()


def later_kernel(which, final, slip, u_ref, v_ref, near_ref, kept, slots_hbm, start, *refs):
    me = lax.axis_index("col")
    s = me ^ (2 + which)
    if final:
        sent, own, total, slots, coeffs, sem = refs
    else:
        total, slots, coeffs, sem = refs
    copy = pltpu.make_async_copy(slots_hbm, slots, sem)
    copy.start()
    waited = []

    def slot_at(slot, b):
        if not waited:
            copy.wait()
            waited.append(True)
        return slots[s, slot, b]

    add_section(
        slip[...], u_ref.at[which], v_ref.at[which], near_ref.at[which], kept.at[which],
        slot_at, start, total, coeffs,
    )
    if not final:
        return
    owners, _, owned = sent.shape
    row = lax.axis_index("row")
    for r in range(owners):
        for at in range(0, owned, LANES):
            take = min(owned, LANES)
            j, lane = divmod(r * owned + at, LANES)
            sent[r, :, at : at + take] = total[j, :, lane : lane + take].astype(BF16)
    sent[row] = jnp.zeros(own.shape, BF16)
    if owned % LANES == 0:
        blocks = owned // LANES
        for i in range(blocks):
            own[:, i * LANES : (i + 1) * LANES] = total[row * blocks + i]
    else:
        value = jnp.zeros(own.shape, F32)
        for r in range(owners):
            j, lane = divmod(r * owned, LANES)
            value = jnp.where(row == r, total[j, :, lane : lane + owned], value)
        own[...] = value


def in_hbm(value):
    return pltpu.with_memory_space_constraint(value, pltpu.HBM)


def params(flops, size):
    return dict(
        compiler_params=pltpu.CompilerParams(vmem_limit_bytes=VMEM_LIMIT),
        cost_estimate=pl.CostEstimate(flops=flops, bytes_accessed=size, transcendentals=0),
    )


def body(
    slip, lowrank_u, lowrank_v, ranks, near_slot, near_blocks, velocity, theta, a_sigma, b_sigma
):
    groups, owners = lax.axis_size("col"), lax.axis_size("row")
    members = slip.shape[0]
    _, receivers, depth, _ = lowrank_v.shape
    owned = velocity.shape[1]
    _, count, slots = near_slot.shape
    weights = (lowrank_u, lowrank_v, near_blocks)
    size = sum(w.size for w in weights) // groups
    slots_by = jnp.swapaxes(near_slot, 1, 2)

    def swapped_with(value, offset):
        return lax.ppermute(value, "col", [(i, i ^ offset) for i in range(groups)])

    across = swapped_with(slip, 2)
    sibling = swapped_with(slip, 1)

    def two(w):
        return (2,) + w.shape[1:]

    kept_shape = (2, count, receivers * KMAX)
    coeffs = pltpu.VMEM((receivers, members, depth), BF16)
    total_shape = pltpu.VMEM((receivers, members, LANES), F32)
    row_shape = velocity.shape
    total, u_two, v_two, near_two, kept, gain, shift = pl.pallas_call(
        first_kernel,
        out_shape=(
            [total_shape]
            + [pltpu.VMEM(two(w), BF16) for w in weights]
            + [pltpu.VMEM(kept_shape, F32), pltpu.VMEM(row_shape, F32), pltpu.VMEM(row_shape, F32)]
        ),
        in_specs=[HBM_SPEC, VMEM_SPEC] + [HBM_SPEC] * 9,
        out_specs=[VMEM_SPEC] * 7,
        scratch_shapes=[
            pltpu.VMEM(slip.shape, BF16),
            *[pltpu.VMEM(two(w), BF16) for w in weights],
            pltpu.VMEM(ranks.shape, I32),
            pltpu.SMEM(slots_by.shape, I32),
            pltpu.VMEM(row_shape, F32),
            pltpu.VMEM(row_shape, F32),
            pltpu.VMEM((1, owned), F32),
            pltpu.VMEM((1, owned), F32),
            pltpu.VMEM(kept_shape, F32),
            coeffs,
            pltpu.SemaphoreType.DMA((19,)),
        ],
        **params(4 * members * size, 8 * size),
    )(
        in_hbm(slip), sibling, *map(in_hbm, weights), in_hbm(ranks), in_hbm(slots_by),
        in_hbm(velocity), in_hbm(theta),
        in_hbm(a_sigma.reshape(1, owned)), in_hbm(b_sigma.reshape(1, owned)),
    )
    across, total = lax.optimization_barrier((across, total))

    def later(which, value, total):
        final = which == 1
        if final:
            out_shape = [
                jax.ShapeDtypeStruct((owners, members, owned), BF16),
                pltpu.VMEM((members, owned), F32),
            ]
        else:
            out_shape = [total_shape]
        return pl.pallas_call(
            functools.partial(later_kernel, which, final),
            out_shape=out_shape,
            in_specs=[VMEM_SPEC] * 5 + [HBM_SPEC, VMEM_SPEC],
            out_specs=[VMEM_SPEC] * len(out_shape),
            scratch_shapes=([total_shape] if final else [])
            + [pltpu.SMEM(slots_by.shape, I32), coeffs, pltpu.SemaphoreType.DMA],
            **params(2 * members * size, 2 * size),
        )(value, u_two, v_two, near_two, kept, in_hbm(slots_by), total)

    beyond = swapped_with(across, 1)
    (total,) = later(0, across, total)
    sent, own = later(1, beyond, total)
    received = lax.all_to_all(sent, "row", 0, 0, tiled=True)
    stress_rate = own + jnp.sum(received.astype(F32), axis=0)
    return (stress_rate, stress_rate * gain + shift)


def solution(mesh):
    placed = (
        P(None, ("col", "row")),
        P(None, "row", "col"),
        P(None, "col", "row", None),
        P(None, "row", "col"),
        P(None, "row", "col"),
        P(None, "row", "col"),
        P(None, ("col", "row")),
        P(None, ("col", "row")),
        P(("col", "row")),
        P(("col", "row")),
    )
    return jax.shard_map(
        body,
        mesh=mesh,
        in_specs=placed,
        out_specs=(P(None, ("col", "row")), P(None, ("col", "row"))),
        check_vma=False,
    )
```

time: 145 us -> 26.8 us (0.18)
  waiting for transfers between devices: 83.2 us -> 0.11 us
  matrix products: 22.1 us -> 0 us
  local copies, waits for them, and re-layouts: 21.6 us -> 0 us
  blocking collectives: 0 us -> 15.3 us
  between operations: 14.4 us -> 0.66 us
  Pallas kernels: 0 us -> 6.51 us
  starting transfers between devices: 0.08 us -> 3.26 us
  other arithmetic: 3.18 us -> 0.71 us
    reduce_scatter x1 -> x0, waiting for transfers between devices: 62.6 us -> none  [body(): lax.psum_scatter(partials, 'row', scatter_dimension=1, tiled=True)]
    dot_general x16 -> x0, matrix products: 22.1 us -> none  [the longest x4 11 us: section_stress(): jnp.einsum('mbjk,jbkr->mjr', coeffs, right_factor.reshape(receivers, coun...]
    psum x1 -> x0, waiting for transfers between devices: 20.6 us -> none  [from_root(): return lax.psum(block, axis)]
    all_to_all x0 -> x1, blocking collectives: none -> 15.3 us  [body(): received = lax.all_to_all(sent, 'row', 0, 0, tiled=True)]
    another operation x4 -> x0, local copies, waits for them, and re-layouts: 7.88 us -> none  [section_stress(): dense_blocks.reshape(count, width, slots, width)]
    pallas_call x0 -> x3, Pallas kernels: none -> 6.51 us  [the longest x1 4.23 us: body(): pl.pallas_call(first_kernel, out_shape=[total_shape] + [pltpu.VMEM(two(w)...]
    slice x3 -> x0, local copies, waits for them, and re-layouts: 4.89 us -> none  [the longest x1 2.08 us: body(): lowrank_v[section_index]]
    transpose x4 -> x0, local copies, waits for them, and re-layouts: 3.62 us -> none  [section_stress(): jnp.einsum('mbs,bsq->mbq', source_rows, left_factor.reshape(count, width,...]
  transfers between devices with their start and end apart: 2 -> 3, of which waited for: 2 -> 1; matrix products, arithmetic and copies ran while one was open for 9% -> 0% of each run, Pallas kernels for 0% -> 20%
where the time goes in v2:
time: 26.8 us; the launch traced here: 26.5 us
  blocking collectives  15.3 us (57%)
  Pallas kernels  6.51 us (24%)
  starting transfers between devices  3.26 us (12%)
  other arithmetic  0.71 us (3%)
  between operations  0.66 us (2%)
    all_to_all x1, blocking collectives, body(): received = lax.all_to_all(sent, 'row', 0, 0, tiled=True)  15.3 us
    pallas_call x1, Pallas kernels, body(): pl.pallas_call(first_kernel, out_shape=[total_shape] + [pltpu.VMEM(two(w)...  4.23 us
    ppermute x3, starting transfers between devices, swapped_with(): return lax.ppermute(value, 'col', [(i, i ^ offset) for i in range(groups)])  3.26 us
    pallas_call x2, Pallas kernels, later(): pl.pallas_call(functools.partial(later_kernel, which, final), out_shape=o...  2.28 us
    add x1, other arithmetic, body(): return (stress_rate, stress_rate * gain + shift)  0.67 us
  transfers between devices with their start and end apart: 3, of which 1 were waited for; matrix products, arithmetic and copies ran while one was open for 0% of the time, Pallas kernels for 20%

profile of v2, /device:TPU:0, one launch (start us, length us, event | category | flops | bytes accessed | tf_op | source)
XLA Modules:
  0.0 26.5 jit_solution(14274932895390329327)
XLA Ops:
  0.6 0.5 %collective-permute-start.1 = (bf16[64,1024]{1,0:T(8,128)(2,1)}, bf16[64,1024]{1,0:T(8,128)(2,1)S(1)}, u32[]{:S(2)}, u32[]{:S(2)}) collective-permute-start(bf16[64,1024]{1,0:T(8,128)(2,1)} %slip_hbm.1), channel_id=1, source_target_pairs={{0,8},{8,0},{16,24},{24,16},{1,9},{9,1},{17,25},{25,17},{2,10},{10... | collective-permute-start | bytes 393224 | tf_op jit(solution)/shard_map/ppermute | solution.py:205
  1.2 2.6 %collective-permute-start = (bf16[64,1024]{1,0:T(8,128)(2,1)}, bf16[64,1024]{1,0:T(8,128)(2,1)S(1)}, u32[]{:S(2)}, u32[]{:S(2)}) collective-permute-start(bf16[64,1024]{1,0:T(8,128)(2,1)} %slip_hbm.1), channel_id=1, source_target_pairs={{0,16},{8,24},{16,0},{24,8},{1,17},{9,25},{17,1},{25,9},{2,18},{10... | collective-permute-start | bytes 393224 | tf_op jit(solution)/shard_map/ppermute | solution.py:205
  3.7 0.0 collective-permute-done.1.sibling
  3.7 4.2 %shard_map.113 = (f32[16,64,128]{2,1,0:T(8,128)S(1)}, bf16[2,1024,512]{2,1,0:T(8,128)(2,1)S(1)}, bf16[2,16,256,128]{3,2,1,0:T(8,128)(2,1)S(1)}, bf16[2,1024,256]...) custom-call(bf16[64,1024]{1,0:T(8,128)(2,1)} %slip_hbm.1, ...), custom_call_target="tpu_custom_call" | custom-call | flops 335544320 | bytes 10485760 | tf_op jit(solution)/shard_map/pallas_call | solution.py:217
  8.0 0.1 collective-permute-done.slip
  8.0 0.2 collective-permute-start.2
  8.2 1.1 %shard_map.114.start = f32[16,64,128]{2,1,0:T(8,128)S(1)} custom-call(bf16[64,1024]{1,0:T(8,128)(2,1)S(1)} %collective-permute-done.slip, bf16[2,1024,512]{2,1,0:T(8,128)(2,1)S(1)} %get-tuple-element.15.u_ref, bf16[2,16,256,128]{3,2,1,0:T(8,128)(2,1)S(1)} %get-tuple-element.16.v_ref, bf16[2,1024,256]{2,1,0:T(8,128)(2,1)S(1)} %get-tuple-element.17.near_ref, ...), custom_call_target="tpu_custom_call" | custom-call | flops 167772160 | bytes 2621440 | tf_op jit(solution)/shard_map/pallas_call | solution.py:256
  9.3 0.0 collective-permute-done.2.slip
  9.4 1.2 %shard_map.115 = (bf16[8,64,256]{2,1,0:T(8,128)(2,1)S(1)}, f32[64,256]{1,0:T(8,128)S(1)}) custom-call(bf16[64,1024]{1,0:T(8,128)(2,1)S(1)} %collective-permute-done.2.slip, bf16[2,1024,512]{2,1,0:T(8,128)(2,1)S(1)} %get-tuple-element.15.u_ref, bf16[2,16,256,128]{3,2,1,0:T(8,128)(2,1)S(1)} %get-tuple-element.16.v_ref, ...), custom_call_target="tpu_custom_call" | custom-call | flops 167772160 | bytes 2621440 | tf_op jit(solution)/shard_map/pallas_call | solution.py:256
  10.5 15.3 %all_to_all.5 = bf16[8,64,256]{2,1,0:T(8,128)(2,1)S(1)} all-to-all(bf16[8,64,256]{2,1,0:T(8,128)(2,1)S(1)} %get-tuple-element.21), channel_id=1, replica_groups=mesh['col'=4,'row'=8] {'row'}, dimensions={0} | all-to-all | bytes 524288 | tf_op jit(solution)/shard_map/all_to_all | solution.py:269
  25.9 0.7 %multiply_add_fusion = (f32[64,256]{1,0:T(8,128)}, f32[64,256]{1,0:T(8,128)}) fusion(f32[64,256]{1,0:T(8,128)S(1)} %get-tuple-element.23, f32[64,256]{1,0:T(8,128)S(1)} %get-tuple-element.22, f32[64,256]{1,0:T(8,128)S(1)} %get-tuple-element.20, f32[64,256]{1,0:T(8,128)S(1)} %convert_reduce_fusion), kind=kLoop, calls=%fused_computation.1 | loop fusion | flops 49152 | bytes 393216 | tf_op jit(solution)/shard_map/add | solution.py:271
  (1 shorter events, 0.0 us)
Async XLA Ops:
  0.6 3.1 %collective-permute-start.1 = (bf16[64,1024]{1,0:T(8,128)(2,1)}, bf16[64,1024]{1,0:T(8,128)(2,1)S(1)}, u32[]{:S(2)}, u32[]{:S(2)}) collective-permute-start(bf16[64,1024]{1,0:T(8,128)(2,1)} %slip_hbm.1), channel_id=1, source_target_pairs={{0,8},{8,0},{16,24},{24,16},{1,9},{9,1},{17,25},{25,17},{2,10},{10... | collective-permute-start | bytes 393224 | tf_op jit(solution)/shard_map/ppermute | solution.py:205
  1.2 6.9 %collective-permute-start = (bf16[64,1024]{1,0:T(8,128)(2,1)}, bf16[64,1024]{1,0:T(8,128)(2,1)S(1)}, u32[]{:S(2)}, u32[]{:S(2)}) collective-permute-start(bf16[64,1024]{1,0:T(8,128)(2,1)} %slip_hbm.1), channel_id=1, source_target_pairs={{0,16},{8,24},{16,0},{24,8},{1,17},{9,25},{17,1},{25,9},{2,18},{10... | collective-permute-start | bytes 393224 | tf_op jit(solution)/shard_map/ppermute | solution.py:205
  8.0 1.4 %collective-permute-start.2 = (bf16[64,1024]{1,0:T(8,128)(2,1)S(1)}, bf16[64,1024]{1,0:T(8,128)(2,1)S(1)}, u32[]{:S(2)}, u32[]{:S(2)}) collective-permute-start(bf16[64,1024]{1,0:T(8,128)(2,1)S(1)} %collective-permute-done.slip), channel_id=1, source_target_pairs={{0,8},{8,0},{16,24},{24,16},{1,9},{9,1},{17,25},{25,17},{2,10},{10... | collective-permute-start | bytes 393224 | tf_op jit(solution)/shard_map/ppermute | solution.py:205

commit v3 on v0

v3 whole, which is shorter than its diff:
```python
import functools

import jax
import jax.numpy as jnp
from jax import lax
from jax.experimental import pallas as pl
from jax.experimental.pallas import tpu as pltpu
from jax.sharding import PartitionSpec as P

BF16, F32, I32 = jnp.bfloat16, jnp.float32, jnp.int32
LANES = 128
KMAX = 32
PACK = LANES // KMAX
VMEM_LIMIT = 32 * 2**20
HBM_SPEC = pl.BlockSpec(memory_space=pltpu.HBM)
VMEM_SPEC = pl.BlockSpec(memory_space=pltpu.VMEM)
SMEM_SPEC = pl.BlockSpec(memory_space=pltpu.SMEM)


def dot(left, right):
    return jnp.dot(left, right, preferred_element_type=F32)


def add_far(slip, u_ref, v_ref, kept_ref, total, coeffs, fresh=False):
    count, width = kept_ref.shape
    place = lax.broadcasted_iota(I32, (1, LANES), 1) // KMAX
    for first in range(0, count, PACK):
        projected = []
        for b in range(first, first + PACK):
            rows = slice(b * LANES, (b + 1) * LANES)
            value = dot(slip[:, rows], u_ref[rows, :])
            projected.append(jnp.where(kept_ref[b : b + 1, :] > 0, value, 0.0))
        for g in range(width // LANES):
            turned = []
            for i, value in enumerate(projected):
                value = value[:, g * LANES : (g + 1) * LANES]
                value = pltpu.roll(value, i * KMAX, 1) if i else value
                turned.append(value.astype(BF16))
            for i in range(PACK):
                row = turned[-i % PACK]
                for c in range(1, PACK):
                    row = jnp.where(place == c, turned[(c - i) % PACK], row)
                coeffs[g * PACK + i, :, first * KMAX : (first + PACK) * KMAX] = row
    for j in range(total.shape[0]):
        order = []
        for first in range(0, count, PACK):
            order += [first + (c - j) % PACK for c in range(PACK)]
        right = jnp.concatenate([v_ref[j, b * KMAX : (b + 1) * KMAX, :] for b in order], axis=0)
        value = dot(coeffs[j], right)
        total[j] = value if fresh else total[j] + value


def add_near(slip, near_ref, slots, s, total):
    count = near_ref.shape[0] // LANES
    for b in range(count):
        rows = slice(b * LANES, (b + 1) * LANES)
        dense = dot(slip[:, rows], near_ref[rows, :])
        for slot in range(near_ref.shape[1] // LANES):
            total[slots[s, slot, b]] += dense[:, slot * LANES : (slot + 1) * LANES]


class Fetches:
    def __init__(self, sems):
        self.sems, self.used = sems, 0

    def __call__(self, source, target):
        copy = pltpu.make_async_copy(source, target, self.sems.at[self.used])
        self.used += 1
        copy.start()
        return copy


def wait_all(copies):
    for copy in copies:
        copy.wait()


def own_kernel(
    slip_hbm, u_hbm, v_hbm, near_hbm, ranks_hbm, slots_hbm, velocity_hbm, theta_hbm, a_hbm, b_hbm,
    total, u_out, v_out, near_out, kept, gain, shift, slots,
    slip, u_in, v_in, near_in, ranks, velocity, theta, a_sigma, b_sigma, coeffs, sems,
):
    me = lax.axis_index("col")
    fetch = Fetches(sems)
    small = [fetch(ranks_hbm, ranks), fetch(slots_hbm, slots)]
    mine = [
        fetch(slip_hbm, slip),
        fetch(u_hbm.at[me], u_in),
        fetch(v_hbm.at[me], v_in),
        fetch(near_hbm.at[me], near_in),
    ]
    later = []
    for i in range(3):
        s = me ^ (1 + i)
        later += [
            fetch(u_hbm.at[s], u_out.at[i]),
            fetch(v_hbm.at[s], v_out.at[i]),
            fetch(near_hbm.at[s], near_out.at[i]),
        ]
    fields = [
        fetch(velocity_hbm, velocity),
        fetch(theta_hbm, theta),
        fetch(a_hbm, a_sigma),
        fetch(b_hbm, b_sigma),
    ]
    wait_all(small)
    _, count, receivers = ranks.shape
    width = receivers * KMAX
    column = lax.broadcasted_iota(I32, (receivers, width), 1)
    spread = column // KMAX == lax.broadcasted_iota(I32, (receivers, width), 0)
    lane = lax.broadcasted_iota(I32, (1, width), 1)
    block, index = lane // KMAX, (lane % KMAX).astype(F32)
    for i in range(4):
        s = me ^ i
        wide = dot(ranks[s].astype(F32).astype(BF16), spread.astype(BF16))
        for b in range(count):
            keep = index < wide[b : b + 1, :]
            for slot in range(slots.shape[1]):
                keep = keep & (block != slots[s, slot, b])
            kept[i, b : b + 1, :] = keep.astype(F32)

    wait_all(mine)
    add_far(slip[...], u_in, v_in, kept.at[0], total, coeffs, fresh=True)
    add_near(slip[...], near_in, slots, me, total)
    wait_all(later)
    wait_all(fields)
    rate, state = velocity[...], theta[...]
    divisor = 1.0 / (a_sigma[...] / rate + 0.5)
    gain[...] = divisor
    shift[...] = -(b_sigma[...] * (1.0 - rate * state) / state) * divisor


def later_kernel(offsets, final, *refs):
    slips, refs = refs[: len(offsets)], refs[len(offsets) :]
    u_ref, v_ref, near_ref, kept, slots, start, total, *refs = refs
    *sent, coeffs = refs
    me = lax.axis_index("col")
    for slip, i in zip(slips, offsets):
        add_far(slip[...], u_ref.at[i - 1], v_ref.at[i - 1], kept.at[i], total, coeffs)
        add_near(slip[...], near_ref.at[i - 1], slots, me ^ i, total)
    if not final:
        return
    owners = lax.axis_size("row")
    blocks = total.shape[0] // PACK
    mine = lax.axis_index("row") // (owners // blocks)
    for k, target in enumerate(sent):
        for i in range(PACK):
            target[i] = total[(mine ^ k) * PACK + i].astype(target.dtype)


def gather_kernel(place, *refs):
    own, *received, sent, kept, total = refs
    for i in range(PACK):
        value = own[i]
        for part in received:
            value = value + part[i].astype(F32)
        total[i] = value
    side = (lax.axis_index("row") >> place) & 1
    low, owned = 1 << place, sent.shape[2]
    for n in range(sent.shape[0]):
        high, low_n = divmod(n, low)
        for at in range(0, owned, LANES):
            take = min(owned, LANES)
            block, lane = divmod(low_n * owned + at, LANES)
            for target, half in ((sent, 1 - side), (kept, side)):
                base = (2 * high + half) * (low * owned // LANES)
                target[n, :, at : at + take] = total[base + block][:, lane : lane + take]


def halve_kernel(place, kept, received, sent, own):
    side = (lax.axis_index("row") >> place) & 1
    low = 1 << place
    for n in range(sent.shape[0]):
        base = (n // low) * 2 * low + n % low
        for target, half in ((sent, 1 - side), (own, side)):
            i = base + half * low
            target[n] = kept[i] + received[i]


def in_hbm(value):
    return pltpu.with_memory_space_constraint(value, pltpu.HBM)


def params(flops, size):
    return dict(
        compiler_params=pltpu.CompilerParams(vmem_limit_bytes=VMEM_LIMIT),
        cost_estimate=pl.CostEstimate(flops=flops, bytes_accessed=size, transcendentals=0),
    )


def body(
    slip, lowrank_u, lowrank_v, ranks, near_slot, near_blocks, velocity, theta, a_sigma, b_sigma
):
    groups, owners = lax.axis_size("col"), lax.axis_size("row")
    members = slip.shape[0]
    _, receivers, depth, _ = lowrank_v.shape
    owned = velocity.shape[1]
    _, count, _ = near_slot.shape
    n_groups = receivers // PACK
    per_group = owners // n_groups
    slots_by = jnp.swapaxes(near_slot, 1, 2)
    size = (lowrank_u.size + lowrank_v.size + near_blocks.size) // groups

    def col_swap(value, offset):
        return lax.ppermute(value, "col", [(i, i ^ offset) for i in range(groups)])

    def row_swap(value, offset):
        return lax.ppermute(value, "row", [(i, i ^ offset) for i in range(owners)])

    across = col_swap(slip, 2)
    sibling = col_swap(slip, 1)

    weights = (lowrank_u, lowrank_v, near_blocks)
    field = pltpu.VMEM(velocity.shape, F32)
    coeffs = pltpu.VMEM((receivers, members, depth), BF16)
    total_shape = pltpu.VMEM((receivers, members, LANES), F32)
    slots_smem = pltpu.SMEM(slots_by.shape, I32)
    total, u_later, v_later, near_later, kept, gain, shift, slots = pl.pallas_call(
        own_kernel,
        out_shape=[
            total_shape,
            *[pltpu.VMEM((3, *w.shape[1:]), BF16) for w in weights],
            pltpu.VMEM((groups, count, receivers * KMAX), F32), field, field, slots_smem,
        ],
        in_specs=[HBM_SPEC] * 10,
        out_specs=[VMEM_SPEC] * 7 + [SMEM_SPEC],
        scratch_shapes=[
            pltpu.VMEM(slip.shape, BF16),
            *[pltpu.VMEM(w.shape[1:], BF16) for w in weights],
            pltpu.VMEM(ranks.shape, I32), field, field,
            pltpu.VMEM((1, owned), F32), pltpu.VMEM((1, owned), F32),
            coeffs, pltpu.SemaphoreType.DMA((19,)),
        ],
        **params(2 * members * size, 8 * size),
    )(
        *map(
            in_hbm,
            (
                slip, *weights, ranks, slots_by, velocity, theta,
                a_sigma.reshape(1, owned), b_sigma.reshape(1, owned),
            ),
        )
    )
    across, total = lax.optimization_barrier((across, total))

    def later(offsets, slips, total):
        final = offsets[-1] == 3
        out_shape = [total_shape]
        if final:
            shape = (PACK, members, LANES)
            out_shape += [pltpu.VMEM(shape, BF16 if k else F32) for k in range(n_groups)]
        return pl.pallas_call(
            functools.partial(later_kernel, offsets, final),
            out_shape=out_shape,
            in_specs=[VMEM_SPEC] * (len(slips) + 4) + [SMEM_SPEC, VMEM_SPEC],
            out_specs=[VMEM_SPEC] * len(out_shape),
            scratch_shapes=[coeffs],
            input_output_aliases={len(slips) + 5: 0},
            **params(2 * members * size * len(slips), 2 * size * len(slips)),
        )(*slips, u_later, v_later, near_later, kept, slots, total)

    beyond = col_swap(across, 1)
    (total,) = later((1, 2), (sibling, across), total)
    _, own, *sent = later((3,), (beyond,), total)
    order = (1, 2, 0)
    received = [row_swap(sent[k], (k + 1) * per_group) for k in order]
    place = per_group.bit_length() - 2
    shape = (per_group // 2, members, owned)
    sent, own = pl.pallas_call(
        functools.partial(gather_kernel, place),
        out_shape=[pltpu.VMEM(shape, F32)] * 2,
        in_specs=[VMEM_SPEC] * (1 + len(received)),
        out_specs=[VMEM_SPEC] * 2,
        scratch_shapes=[pltpu.VMEM((PACK, members, LANES), F32)],
        **params(0, 40 * own.size),
    )(own, *received)
    received = row_swap(sent, 1 << place)
    for place in reversed(range(place)):
        shape = (own.shape[0] // 2, members, owned)
        sent, own = pl.pallas_call(
            functools.partial(halve_kernel, place),
            out_shape=[pltpu.VMEM(shape, F32)] * 2,
            in_specs=[VMEM_SPEC] * 2,
            out_specs=[VMEM_SPEC] * 2,
            **params(0, 12 * own.size),
        )(own, received)
        received = row_swap(sent, 1 << place)
    stress_rate = own[0] + received[0]
    return (stress_rate, stress_rate * gain + shift)


def solution(mesh):
    placed = (
        P(None, ("col", "row")),
        P(None, "row", "col"),
        P(None, "col", "row", None),
        P(None, "row", "col"),
        P(None, "row", "col"),
        P(None, "row", "col"),
        P(None, ("col", "row")),
        P(None, ("col", "row")),
        P(("col", "row")),
        P(("col", "row")),
    )
    return jax.shard_map(
        body,
        mesh=mesh,
        in_specs=placed,
        out_specs=(P(None, ("col", "row")), P(None, ("col", "row"))),
        check_vma=False,
    )
```

time: 145 us -> 25.1 us (0.17)
  waiting for transfers between devices: 83.2 us -> 7.79 us
  matrix products: 22.1 us -> 0 us
  local copies, waits for them, and re-layouts: 21.6 us -> 0 us
  between operations: 14.4 us -> 0.68 us
  starting transfers between devices: 0.08 us -> 9.41 us
  Pallas kernels: 0 us -> 6.37 us
  other arithmetic: 3.18 us -> 0.67 us
    reduce_scatter x1 -> x0, waiting for transfers between devices: 62.6 us -> none  [body(): lax.psum_scatter(partials, 'row', scatter_dimension=1, tiled=True)]
    dot_general x16 -> x0, matrix products: 22.1 us -> none  [the longest x4 11 us: section_stress(): jnp.einsum('mbjk,jbkr->mjr', coeffs, right_factor.reshape(receivers, coun...]
    psum x1 -> x0, waiting for transfers between devices: 20.6 us -> none  [from_root(): return lax.psum(block, axis)]
    ppermute x0 -> x7, starting transfers between devices: none -> 9.41 us  [the longest x4 5.83 us: row_swap(): return lax.ppermute(value, 'row', [(i, i ^ offset) for i in range(owners)])]
    another operation x4 -> x0, local copies, waits for them, and re-layouts: 7.88 us -> none  [section_stress(): dense_blocks.reshape(count, width, slots, width)]
    ppermute x0 -> x7, waiting for transfers between devices: none -> 7.79 us  [the longest x4 7.78 us: row_swap(): return lax.ppermute(value, 'row', [(i, i ^ offset) for i in range(owners)])]
    pallas_call x0 -> x4, Pallas kernels: none -> 6.37 us  [the longest x1 4.25 us: body(): pl.pallas_call(own_kernel, out_shape=[total_shape, *[pltpu.VMEM((3, *w.sh...]
    slice x3 -> x0, local copies, waits for them, and re-layouts: 4.89 us -> none  [the longest x1 2.08 us: body(): lowrank_v[section_index]]
  transfers between devices with their start and end apart: 2 -> 7, of which waited for: 2 -> 4; matrix products, arithmetic and copies ran while one was open for 9% -> 0% of each run, Pallas kernels for 0% -> 22%
where the time goes in v3:
time: 25.1 us; the launch traced here: 24.9 us
  starting transfers between devices  9.41 us (37%)
  waiting for transfers between devices  7.79 us (31%)
  Pallas kernels  6.37 us (25%)
  between operations  0.68 us (3%)
  other arithmetic  0.67 us (3%)
    ppermute x4, waiting for transfers between devices, row_swap(): return lax.ppermute(value, 'row', [(i, i ^ offset) for i in range(owners)])  7.78 us
    ppermute x4, starting transfers between devices, row_swap(): return lax.ppermute(value, 'row', [(i, i ^ offset) for i in range(owners)])  5.83 us
    pallas_call x1, Pallas kernels, body(): pl.pallas_call(own_kernel, out_shape=[total_shape, *[pltpu.VMEM((3, *w.sh...  4.25 us
    ppermute x3, starting transfers between devices, col_swap(): return lax.ppermute(value, 'col', [(i, i ^ offset) for i in range(groups)])  3.58 us
    pallas_call x2, Pallas kernels, later(): pl.pallas_call(functools.partial(later_kernel, offsets, final), out_shape...  2.08 us
    add x1, other arithmetic, body(): return (stress_rate, stress_rate * gain + shift)  0.67 us
  transfers between devices with their start and end apart: 7, of which 4 were waited for; matrix products, arithmetic and copies ran while one was open for 0% of the time, Pallas kernels for 22%

profile of v3, /device:TPU:0, one launch (start us, length us, event | category | flops | bytes accessed | tf_op | source)
XLA Modules:
  0.0 24.9 jit_solution(1442218751052848153)
XLA Ops:
  0.6 3.0 %collective-permute-start = (bf16[64,1024]{1,0:T(8,128)(2,1)}, bf16[64,1024]{1,0:T(8,128)(2,1)S(1)}, u32[]{:S(2)}, u32[]{:S(2)}) collective-permute-start(bf16[64,1024]{1,0:T(8,128)(2,1)} %slip_hbm.1), channel_id=1, source_target_pairs={{0,16},{8,24},{16,0},{24,8},{1,17},{9,25},{17,1},{25,9},{2,18},{10... | collective-permute-start | bytes 393224 | tf_op jit(solution)/shard_map/ppermute | solution.py:205
  3.6 0.0 collective-permute-start.2
  3.6 4.3 %shard_map.113 = (f32[16,64,128]{2,1,0:T(8,128)S(1)}, bf16[3,1024,512]{2,1,0:T(8,128)(2,1)S(1)}, bf16[3,16,256,128]{3,2,1,0:T(8,128)(2,1)S(1)}, bf16[3,1024,256]...) custom-call(bf16[64,1024]{1,0:T(8,128)(2,1)} %slip_hbm.1, ...), custom_call_target="tpu_custom_call" | custom-call | flops 167772160 | bytes 10485760 | tf_op jit(solution)/shard_map/pallas_call | solution.py:218
  7.9 0.0 collective-permute-done.refs_1_
  7.9 0.6 %collective-permute-start.1 = (bf16[64,1024]{1,0:T(8,128)(2,1)S(1)}, bf16[64,1024]{1,0:T(8,128)(2,1)S(1)}, u32[]{:S(2)}, u32[]{:S(2)}) collective-permute-start(bf16[64,1024]{1,0:T(8,128)(2,1)S(1)} %collective-permute-done.refs_1_), channel_id=1, source_target_pairs={{0,8},{8,0},{16,24},{24,16},{1,9},{9,1},{17,25},{25,17},{2,10},{10... | collective-permute-start | bytes 393224 | tf_op jit(solution)/shard_map/ppermute | solution.py:205
  8.5 0.0 collective-permute-done.2.refs_0_
  8.5 1.3 %shard_map.114.refs_6_ = f32[16,64,128]{2,1,0:T(8,128)S(1)} custom-call(bf16[64,1024]{1,0:T(8,128)(2,1)S(1)} %collective-permute-done.2.refs_0_, bf16[64,1024]{1,0:T(8,128)(2,1)S(1)} %collective-permute-done.refs_1_, bf16[3,1024,512]{2,1,0:T(8,128)(2,1)S(1)} %get-tuple-element.20.refs_2_.refs_1_, ...), custom_call_target="tpu_custom_call", output_to_operand_aliasing={{}: (7, {})} | custom-call | flops 335544320 | bytes 5242880 | tf_op jit(solution)/shard_map/pallas_call | solution.py:252
  9.8 0.0 collective-permute-done.1.refs_0_
  9.8 0.8 %shard_map.115 = (f32[16,64,128]{2,1,0:T(8,128)S(1)}, f32[4,64,128]{2,1,0:T(8,128)S(1)}, bf16[4,64,128]{2,1,0:T(8,128)(2,1)S(1)}, bf16[4,64,128]{2,1,0:T(8,128)(2,1)S(1)}, bf16[4,64,128]{2,1,0:T(8,128)(2,1)S(1)}) custom-call(bf16[64,1024]{1,0:T(8,128)(2,1)S(1)} %collective-permute-done.1.refs_0_, ...), custom_call_target="tpu_custom_call", output_to_operand_aliasing={{0}: (6, {})} | custom-call | flops 167772160 | bytes 2621440 | tf_op jit(solution)/shard_map/pallas_call | solution.py:252
  10.6 2.7 %collective-permute-start.3 = (bf16[4,64,128]{2,1,0:T(8,128)(2,1)S(1)}, bf16[4,64,128]{2,1,0:T(8,128)(2,1)S(1)}, u32[]{:S(2)}, u32[]{:S(2)}) collective-permute-start(bf16[4,64,128]{2,1,0:T(8,128)(2,1)S(1)} %get-tuple-element.27), channel_id=1, source_target_pairs={{0,4},{1,5},{2,6},{3,7},{4,0},{5,1},{6,2},{7,3},{8,12},{9,13},{10,... | collective-permute-start | bytes 196616 | tf_op jit(solution)/shard_map/ppermute | solution.py:208
  13.2 1.3 %collective-permute-start.4 = (bf16[4,64,128]{2,1,0:T(8,128)(2,1)S(1)}, bf16[4,64,128]{2,1,0:T(8,128)(2,1)S(1)}, u32[]{:S(2)}, u32[]{:S(2)}) collective-permute-start(bf16[4,64,128]{2,1,0:T(8,128)(2,1)S(1)} %get-tuple-element.28), channel_id=1, source_target_pairs={{0,6},{1,7},{2,4},{3,5},{4,2},{5,3},{6,0},{7,1},{8,14},{9,15},{10,... | collective-permute-start | bytes 196616 | tf_op jit(solution)/shard_map/ppermute | solution.py:208
  14.6 0.2 collective-permute-start.5
  14.8 3.5 %collective-permute-done.3.refs_1_ = bf16[4,64,128]{2,1,0:T(8,128)(2,1)S(1)} collective-permute-done((bf16[4,64,128]{2,1,0:T(8,128)(2,1)S(1)}, bf16[4,64,128]{2,1,0:T(8,128)(2,1)S(1)}, u32[]{:S(2)}, u32[]{:S(2)}) %collective-permute-start.3) | collective-permute-done | bytes 65568 | tf_op jit(solution)/shard_map/ppermute | solution.py:208
  18.3 1.3 %collective-permute-done.4.refs_2_ = bf16[4,64,128]{2,1,0:T(8,128)(2,1)S(1)} collective-permute-done((bf16[4,64,128]{2,1,0:T(8,128)(2,1)S(1)}, bf16[4,64,128]{2,1,0:T(8,128)(2,1)S(1)}, u32[]{:S(2)}, u32[]{:S(2)}) %collective-permute-start.4) | collective-permute-done | bytes 65568 | tf_op jit(solution)/shard_map/ppermute | solution.py:208
  19.7 0.2 collective-permute-done.5.refs_3_
  19.9 1.6 %collective-permute-start.6 = (f32[1,64,256]{2,1,0:T(8,128)S(1)}, f32[1,64,256]{2,1,0:T(8,128)S(1)}, u32[]{:S(2)}, u32[]{:S(2)}) collective-permute-start(f32[1,64,256]{2,1,0:T(8,128)S(1)} %get-tuple-element.31), channel_id=1, source_target_pairs={{0,1},{1,0},{2,3},{3,2},{4,5},{5,4},{6,7},{7,6},{8,9},{9,8},{10,11... | collective-permute-start | bytes 196616 | tf_op jit(solution)/shard_map/ppermute | solution.py:208
  21.5 2.7 %collective-permute-done.6 = f32[1,64,256]{2,1,0:T(8,128)S(1)} collective-permute-done((f32[1,64,256]{2,1,0:T(8,128)S(1)}, f32[1,64,256]{2,1,0:T(8,128)S(1)}, u32[]{:S(2)}, u32[]{:S(2)}) %collective-permute-start.6) | collective-permute-done | bytes 65568 | tf_op jit(solution)/shard_map/ppermute | solution.py:208
  24.3 0.7 %multiply_add_fusion = (f32[64,256]{1,0:T(8,128)}, f32[64,256]{1,0:T(8,128)}) fusion(f32[64,256]{1,0:T(8,128)S(1)} %get-tuple-element.33, f32[64,256]{1,0:T(8,128)S(1)} %get-tuple-element.32, f32[1,64,256]{2,1,0:T(8,128)S(1)} %get-tuple-element.30, f32[1,64,256]{2,1,0:T(8,128)S(1)} %collective-permute-done.6), kind=kLoop, calls=%fused_computation | loop fusion | flops 49152 | bytes 393216 | tf_op jit(solution)/shard_map/add | solution.py:289
  (1 shorter events, 0.0 us)
Async XLA Ops:
  0.6 7.3 %collective-permute-start = (bf16[64,1024]{1,0:T(8,128)(2,1)}, bf16[64,1024]{1,0:T(8,128)(2,1)S(1)}, u32[]{:S(2)}, u32[]{:S(2)}) collective-permute-start(bf16[64,1024]{1,0:T(8,128)(2,1)} %slip_hbm.1), channel_id=1, source_target_pairs={{0,16},{8,24},{16,0},{24,8},{1,17},{9,25},{17,1},{25,9},{2,18},{10... | collective-permute-start | bytes 393224 | tf_op jit(solution)/shard_map/ppermute | solution.py:205
  3.6 4.9 %collective-permute-start.2 = (bf16[64,1024]{1,0:T(8,128)(2,1)}, bf16[64,1024]{1,0:T(8,128)(2,1)S(1)}, u32[]{:S(2)}, u32[]{:S(2)}) collective-permute-start(bf16[64,1024]{1,0:T(8,128)(2,1)} %slip_hbm.1), channel_id=1, source_target_pairs={{0,8},{8,0},{16,24},{24,16},{1,9},{9,1},{17,25},{25,17},{2,10},{10... | collective-permute-start | bytes 393224 | tf_op jit(solution)/shard_map/ppermute | solution.py:205
  7.9 1.9 %collective-permute-start.1 = (bf16[64,1024]{1,0:T(8,128)(2,1)S(1)}, bf16[64,1024]{1,0:T(8,128)(2,1)S(1)}, u32[]{:S(2)}, u32[]{:S(2)}) collective-permute-start(bf16[64,1024]{1,0:T(8,128)(2,1)S(1)} %collective-permute-done.refs_1_), channel_id=1, source_target_pairs={{0,8},{8,0},{16,24},{24,16},{1,9},{9,1},{17,25},{25,17},{2,10},{10... | collective-permute-start | bytes 393224 | tf_op jit(solution)/shard_map/ppermute | solution.py:205
  10.6 7.7 %collective-permute-start.3 = (bf16[4,64,128]{2,1,0:T(8,128)(2,1)S(1)}, bf16[4,64,128]{2,1,0:T(8,128)(2,1)S(1)}, u32[]{:S(2)}, u32[]{:S(2)}) collective-permute-start(bf16[4,64,128]{2,1,0:T(8,128)(2,1)S(1)} %get-tuple-element.27), channel_id=1, source_target_pairs={{0,4},{1,5},{2,6},{3,7},{4,0},{5,1},{6,2},{7,3},{8,12},{9,13},{10,... | collective-permute-start | bytes 196616 | tf_op jit(solution)/shard_map/ppermute | solution.py:208
  13.2 6.4 %collective-permute-start.4 = (bf16[4,64,128]{2,1,0:T(8,128)(2,1)S(1)}, bf16[4,64,128]{2,1,0:T(8,128)(2,1)S(1)}, u32[]{:S(2)}, u32[]{:S(2)}) collective-permute-start(bf16[4,64,128]{2,1,0:T(8,128)(2,1)S(1)} %get-tuple-element.28), channel_id=1, source_target_pairs={{0,6},{1,7},{2,4},{3,5},{4,2},{5,3},{6,0},{7,1},{8,14},{9,15},{10,... | collective-permute-start | bytes 196616 | tf_op jit(solution)/shard_map/ppermute | solution.py:208
  14.6 5.3 %collective-permute-start.5 = (bf16[4,64,128]{2,1,0:T(8,128)(2,1)S(1)}, bf16[4,64,128]{2,1,0:T(8,128)(2,1)S(1)}, u32[]{:S(2)}, u32[]{:S(2)}) collective-permute-start(bf16[4,64,128]{2,1,0:T(8,128)(2,1)S(1)} %get-tuple-element.29), channel_id=1, source_target_pairs={{0,2},{1,3},{2,0},{3,1},{4,6},{5,7},{6,4},{7,5},{8,10},{9,11},{10,... | collective-permute-start | bytes 196616 | tf_op jit(solution)/shard_map/ppermute | solution.py:208
  19.9 4.3 %collective-permute-start.6 = (f32[1,64,256]{2,1,0:T(8,128)S(1)}, f32[1,64,256]{2,1,0:T(8,128)S(1)}, u32[]{:S(2)}, u32[]{:S(2)}) collective-permute-start(f32[1,64,256]{2,1,0:T(8,128)S(1)} %get-tuple-element.31), channel_id=1, source_target_pairs={{0,1},{1,0},{2,3},{3,2},{4,5},{5,4},{6,7},{7,6},{8,9},{9,8},{10,11... | collective-permute-start | bytes 196616 | tf_op jit(solution)/shard_map/ppermute | solution.py:208

commit v4 on v3

--- a/solution.py
+++ b/solution.py
@@ -12,6 +12,7 @@
 KMAX = 32
 PACK = LANES // KMAX
 VMEM_LIMIT = 32 * 2**20
+PAD = 16
 HBM_SPEC = pl.BlockSpec(memory_space=pltpu.HBM)
 VMEM_SPEC = pl.BlockSpec(memory_space=pltpu.VMEM)
 SMEM_SPEC = pl.BlockSpec(memory_space=pltpu.SMEM)
@@ -89,6 +90,12 @@
         fetch(v_hbm.at[me], v_in),
         fetch(near_hbm.at[me], near_in),
     ]
+    fields = [
+        fetch(velocity_hbm, velocity),
+        fetch(theta_hbm, theta),
+        fetch(a_hbm, a_sigma),
+        fetch(b_hbm, b_sigma),
+    ]
     later = []
     for i in range(3):
         s = me ^ (1 + i)
@@ -97,12 +104,6 @@
             fetch(v_hbm.at[s], v_out.at[i]),
             fetch(near_hbm.at[s], near_out.at[i]),
         ]
-    fields = [
-        fetch(velocity_hbm, velocity),
-        fetch(theta_hbm, theta),
-        fetch(a_hbm, a_sigma),
-        fetch(b_hbm, b_sigma),
-    ]
     wait_all(small)
     _, count, receivers = ranks.shape
     width = receivers * KMAX
@@ -122,12 +123,12 @@
     wait_all(mine)
     add_far(slip[...], u_in, v_in, kept.at[0], total, coeffs, fresh=True)
     add_near(slip[...], near_in, slots, me, total)
-    wait_all(later)
     wait_all(fields)
     rate, state = velocity[...], theta[...]
     divisor = 1.0 / (a_sigma[...] / rate + 0.5)
     gain[...] = divisor
     shift[...] = -(b_sigma[...] * (1.0 - rate * state) / state) * divisor
+    wait_all(later)
 
 
 def later_kernel(offsets, final, *refs):
@@ -140,41 +141,53 @@
         add_near(slip[...], near_ref.at[i - 1], slots, me ^ i, total)
     if not final:
         return
-    owners = lax.axis_size("row")
-    blocks = total.shape[0] // PACK
-    mine = lax.axis_index("row") // (owners // blocks)
-    for k, target in enumerate(sent):
-        for i in range(PACK):
-            target[i] = total[(mine ^ k) * PACK + i].astype(target.dtype)
-
-
-def gather_kernel(place, *refs):
-    own, *received, sent, kept, total = refs
-    for i in range(PACK):
-        value = own[i]
-        for part in received:
-            value = value + part[i].astype(F32)
-        total[i] = value
-    side = (lax.axis_index("row") >> place) & 1
-    low, owned = 1 << place, sent.shape[2]
-    for n in range(sent.shape[0]):
-        high, low_n = divmod(n, low)
-        for at in range(0, owned, LANES):
-            take = min(owned, LANES)
-            block, lane = divmod(low_n * owned + at, LANES)
-            for target, half in ((sent, 1 - side), (kept, side)):
-                base = (2 * high + half) * (low * owned // LANES)
-                target[n, :, at : at + take] = total[base + block][:, lane : lane + take]
-
-
-def halve_kernel(place, kept, received, sent, own):
+    swapped, same, other = sent
+    mine, side, half = row_place(total)
+    for k in range(3):
+        for i in range(half):
+            block = total[(mine ^ k) * PACK + (1 - side) * half + i]
+            swapped[k * half + i] = block.astype(swapped.dtype)
+    for target, to_side in ((same, side), (other, 1 - side)):
+        target[:, total.shape[1] :, :] = jnp.zeros_like(target[:, total.shape[1] :, :])
+        for i in range(half):
+            write_block(target, i, total[(mine ^ 3) * PACK + to_side * half + i])
+
+
+def row_place(total):
+    row, groups = lax.axis_index("row"), total.shape[0] // PACK
+    per_group = lax.axis_size("row") // groups
+    return row // per_group, row % per_group // (per_group // 2), PACK // 2
+
+
+def write_block(target, i, block):
+    owned, block = target.shape[2], block.astype(target.dtype)
+    if owned >= LANES:
+        n, at = divmod(i * LANES, owned)
+        target[n, : block.shape[0], at : at + LANES] = block
+    else:
+        for at in range(0, LANES, owned):
+            target[(i * LANES + at) // owned, : block.shape[0], :] = block[:, at : at + owned]
+
+
+def join_kernel(total, received, *outs):
+    mine, side, half = row_place(total)
+    for k, target in enumerate(outs):
+        for i in range(half):
+            block = total[(mine ^ k) * PACK + side * half + i] + received[k * half + i].astype(F32)
+            write_block(target, i, block)
+
+
+def halve_kernel(place, kept, *refs):
+    *received, sent, own = refs
     side = (lax.axis_index("row") >> place) & 1
     low = 1 << place
     for n in range(sent.shape[0]):
         base = (n // low) * 2 * low + n % low
         for target, half in ((sent, 1 - side), (own, side)):
-            i = base + half * low
-            target[n] = kept[i] + received[i]
+            value = kept[base + half * low]
+            for part in received:
+                value = value + part[base + half * low, : value.shape[0]].astype(F32)
+            target[n] = value
 
 
 def in_hbm(value):
@@ -243,12 +256,14 @@
     )
     across, total = lax.optimization_barrier((across, total))
 
+    shards = (per_group // 2, members, owned)
+
     def later(offsets, slips, total):
         final = offsets[-1] == 3
         out_shape = [total_shape]
         if final:
-            shape = (PACK, members, LANES)
-            out_shape += [pltpu.VMEM(shape, BF16 if k else F32) for k in range(n_groups)]
+            out_shape.append(pltpu.VMEM((3 * PACK // 2, members, LANES), BF16))
+            out_shape += [pltpu.VMEM((shards[0], members + PAD, owned), BF16)] * 2
         return pl.pallas_call(
             functools.partial(later_kernel, offsets, final),
             out_shape=out_shape,
@@ -261,31 +276,31 @@
 
     beyond = col_swap(across, 1)
     (total,) = later((1, 2), (sibling, across), total)
-    _, own, *sent = later((3,), (beyond,), total)
-    order = (1, 2, 0)
-    received = [row_swap(sent[k], (k + 1) * per_group) for k in order]
-    place = per_group.bit_length() - 2
-    shape = (per_group // 2, members, owned)
-    sent, own = pl.pallas_call(
-        functools.partial(gather_kernel, place),
-        out_shape=[pltpu.VMEM(shape, F32)] * 2,
-        in_specs=[VMEM_SPEC] * (1 + len(received)),
-        out_specs=[VMEM_SPEC] * 2,
-        scratch_shapes=[pltpu.VMEM((PACK, members, LANES), F32)],
-        **params(0, 40 * own.size),
-    )(own, *received)
-    received = row_swap(sent, 1 << place)
-    for place in reversed(range(place)):
+    total, swapped, same, other = later((3,), (beyond,), total)
+    swapped = row_swap(swapped, per_group // 2)
+    other = row_swap(other, 3 * per_group + per_group // 2)
+    same = row_swap(same, 3 * per_group)
+    own, first, second = pl.pallas_call(
+        join_kernel,
+        out_shape=[pltpu.VMEM(shards, dtype) for dtype in (F32, BF16, BF16)],
+        in_specs=[VMEM_SPEC] * 2,
+        out_specs=[VMEM_SPEC] * 3,
+        **params(0, 8 * swapped.size),
+    )(total, swapped)
+    received = [other, same, row_swap(second, 2 * per_group), row_swap(first, per_group)]
+    for place in reversed(range(per_group.bit_length() - 2)):
         shape = (own.shape[0] // 2, members, owned)
         sent, own = pl.pallas_call(
             functools.partial(halve_kernel, place),
             out_shape=[pltpu.VMEM(shape, F32)] * 2,
-            in_specs=[VMEM_SPEC] * 2,
+            in_specs=[VMEM_SPEC] * (1 + len(received)),
             out_specs=[VMEM_SPEC] * 2,
             **params(0, 12 * own.size),
-        )(own, received)
-        received = row_swap(sent, 1 << place)
-    stress_rate = own[0] + received[0]
+        )(own, *received)
+        received = [row_swap(sent, 1 << place)]
+    stress_rate = own[0]
+    for part in received:
+        stress_rate = stress_rate + part[0, :members].astype(F32)
     return (stress_rate, stress_rate * gain + shift)
 
 

time: 25.1 us -> 23 us (0.916)
  waiting for transfers between devices: 7.79 us -> 1.9 us
  starting transfers between devices: 9.41 us -> 13.2 us
    ppermute x4 -> x5, waiting for transfers between devices: 7.78 us -> 1.89 us  [row_swap(): return lax.ppermute(value, 'row', [(i, i ^ offset) for i in range(owners)])]
    ppermute x4 -> x5, starting transfers between devices: 5.83 us -> 9.58 us  [row_swap(): return lax.ppermute(value, 'row', [(i, i ^ offset) for i in range(owners)])]
  transfers between devices with their start and end apart: 7 -> 8, of which waited for: 4 -> 2; matrix products, arithmetic and copies ran while one was open for 0% -> 0% of each run, Pallas kernels for 22% -> 25%
where the time goes in v4:
time: 23 us; the launch traced here: 22.8 us
  starting transfers between devices  13.2 us (57%)
  Pallas kernels  6.37 us (28%)
  waiting for transfers between devices  1.9 us (8%)
  between operations  0.69 us (3%)
  other arithmetic  0.68 us (3%)
    ppermute x5, starting transfers between devices, row_swap(): return lax.ppermute(value, 'row', [(i, i ^ offset) for i in range(owners)])  9.58 us
    pallas_call x1, Pallas kernels, body(): pl.pallas_call(own_kernel, out_shape=[total_shape, *[pltpu.VMEM((3, *w.sh...  4.27 us
    ppermute x3, starting transfers between devices, col_swap(): return lax.ppermute(value, 'col', [(i, i ^ offset) for i in range(groups)])  3.58 us
    pallas_call x2, Pallas kernels, later(): pl.pallas_call(functools.partial(later_kernel, offsets, final), out_shape...  2.07 us
    ppermute x5, waiting for transfers between devices, row_swap(): return lax.ppermute(value, 'row', [(i, i ^ offset) for i in range(owners)])  1.89 us
    add x1, other arithmetic, body(): return (stress_rate, stress_rate * gain + shift)  0.68 us
  transfers between devices with their start and end apart: 8, of which 2 were waited for; matrix products, arithmetic and copies ran while one was open for 0% of the time, Pallas kernels for 25%

profile of v4, /device:TPU:0, one launch (start us, length us, event | category | flops | bytes accessed | tf_op | source)
XLA Modules:
  0.0 22.8 jit_solution(2958637185032279840)
XLA Ops:
  0.6 3.0 %collective-permute-start = (bf16[64,1024]{1,0:T(8,128)(2,1)}, bf16[64,1024]{1,0:T(8,128)(2,1)S(1)}, u32[]{:S(2)}, u32[]{:S(2)}) collective-permute-start(bf16[64,1024]{1,0:T(8,128)(2,1)} %slip_hbm.1), channel_id=1, source_target_pairs={{0,16},{8,24},{16,0},{24,8},{1,17},{9,25},{17,1},{25,9},{2,18},{10... | collective-permute-start | bytes 393224 | tf_op jit(solution)/shard_map/ppermute | solution.py:218
  3.6 0.0 collective-permute-start.2
  3.6 4.3 %shard_map.113 = (f32[16,64,128]{2,1,0:T(8,128)S(1)}, bf16[3,1024,512]{2,1,0:T(8,128)(2,1)S(1)}, bf16[3,16,256,128]{3,2,1,0:T(8,128)(2,1)S(1)}, bf16[3,1024,256]...) custom-call(bf16[64,1024]{1,0:T(8,128)(2,1)} %slip_hbm.1, ...), custom_call_target="tpu_custom_call" | custom-call | flops 167772160 | bytes 10485760 | tf_op jit(solution)/shard_map/pallas_call | solution.py:231
  7.9 0.0 collective-permute-done.refs_1_
  7.9 0.6 %collective-permute-start.1 = (bf16[64,1024]{1,0:T(8,128)(2,1)S(1)}, bf16[64,1024]{1,0:T(8,128)(2,1)S(1)}, u32[]{:S(2)}, u32[]{:S(2)}) collective-permute-start(bf16[64,1024]{1,0:T(8,128)(2,1)S(1)} %collective-permute-done.refs_1_), channel_id=1, source_target_pairs={{0,8},{8,0},{16,24},{24,16},{1,9},{9,1},{17,25},{25,17},{2,10},{10... | collective-permute-start | bytes 393224 | tf_op jit(solution)/shard_map/ppermute | solution.py:218
  8.5 0.0 collective-permute-done.2.refs_0_
  8.5 1.3 %shard_map.114.refs_6_ = f32[16,64,128]{2,1,0:T(8,128)S(1)} custom-call(bf16[64,1024]{1,0:T(8,128)(2,1)S(1)} %collective-permute-done.2.refs_0_, bf16[64,1024]{1,0:T(8,128)(2,1)S(1)} %collective-permute-done.refs_1_, bf16[3,1024,512]{2,1,0:T(8,128)(2,1)S(1)} %get-tuple-element.21.refs_2_.refs_1_, ...), custom_call_target="tpu_custom_call", output_to_operand_aliasing={{}: (7, {})} | custom-call | flops 335544320 | bytes 5242880 | tf_op jit(solution)/shard_map/pallas_call | solution.py:267
  9.8 0.0 collective-permute-done.1.refs_0_
  9.8 0.8 %shard_map.115 = (f32[16,64,128]{2,1,0:T(8,128)S(1)}, bf16[6,64,128]{2,1,0:T(8,128)(2,1)S(1)}, bf16[1,80,256]{2,1,0:T(8,128)(2,1)S(1)}, bf16[1,80,256]{2,1,0:T(8,128)(2,1)S(1)}) custom-call(bf16[64,1024]{1,0:T(8,128)(2,1)S(1)} %collective-permute-done.1.refs_0_, ...), custom_call_target="tpu_custom_call", output_to_operand_aliasing={{0}: (6, {})} | custom-call | flops 167772160 | bytes 2621440 | tf_op jit(solution)/shard_map/pallas_call | solution.py:267
  10.6 1.6 %collective-permute-start.3 = (bf16[6,64,128]{2,1,0:T(8,128)(2,1)S(1)}, bf16[6,64,128]{2,1,0:T(8,128)(2,1)S(1)}, u32[]{:S(2)}, u32[]{:S(2)}) collective-permute-start(bf16[6,64,128]{2,1,0:T(8,128)(2,1)S(1)} %get-tuple-element.28), channel_id=1, source_target_pairs={{0,1},{1,0},{2,3},{3,2},{4,5},{5,4},{6,7},{7,6},{8,9},{9,8},{10,11... | collective-permute-start | bytes 294920 | tf_op jit(solution)/shard_map/ppermute | solution.py:221
  12.2 3.5 %collective-permute-start.4 = (bf16[1,80,256]{2,1,0:T(8,128)(2,1)S(1)}, bf16[1,80,256]{2,1,0:T(8,128)(2,1)S(1)}, u32[]{:S(2)}, u32[]{:S(2)}) collective-permute-start(bf16[1,80,256]{2,1,0:T(8,128)(2,1)S(1)} %get-tuple-element.30), channel_id=1, source_target_pairs={{0,7},{1,6},{2,5},{3,4},{4,3},{5,2},{6,1},{7,0},{8,15},{9,14},{10,... | collective-permute-start | bytes 122888 | tf_op jit(solution)/shard_map/ppermute | solution.py:221
  15.7 0.2 %collective-permute-start.5 = (bf16[1,80,256]{2,1,0:T(8,128)(2,1)S(1)}, bf16[1,80,256]{2,1,0:T(8,128)(2,1)S(1)}, u32[]{:S(2)}, u32[]{:S(2)}) collective-permute-start(bf16[1,80,256]{2,1,0:T(8,128)(2,1)S(1)} %get-tuple-element.31), channel_id=1, source_target_pairs={{0,6},{1,7},{2,4},{3,5},{4,2},{5,3},{6,0},{7,1},{8,14},{9,15},{10,... | collective-permute-start | bytes 122888 | tf_op jit(solution)/shard_map/ppermute | solution.py:221
  16.0 0.0 collective-permute-done.3.received
  16.0 2.1 %collective-permute-start.6 = (bf16[1,64,256]{2,1,0:T(8,128)(2,1)S(1)}, bf16[1,64,256]{2,1,0:T(8,128)(2,1)S(1)}, u32[]{:S(2)}, u32[]{:S(2)}) collective-permute-start(bf16[1,64,256]{2,1,0:T(8,128)(2,1)S(1)} %get-tuple-element.32), channel_id=1, source_target_pairs={{0,4},{1,5},{2,6},{3,7},{4,0},{5,1},{6,2},{7,3},{8,12},{9,13},{10,... | collective-permute-start | bytes 98312 | tf_op jit(solution)/shard_map/ppermute | solution.py:221
  18.1 2.2 %collective-permute-start.7 = (bf16[1,64,256]{2,1,0:T(8,128)(2,1)S(1)}, bf16[1,64,256]{2,1,0:T(8,128)(2,1)S(1)}, u32[]{:S(2)}, u32[]{:S(2)}) collective-permute-start(bf16[1,64,256]{2,1,0:T(8,128)(2,1)S(1)} %get-tuple-element.33), channel_id=1, source_target_pairs={{0,2},{1,3},{2,0},{3,1},{4,6},{5,7},{6,4},{7,5},{8,10},{9,11},{10,... | collective-permute-start | bytes 98312 | tf_op jit(solution)/shard_map/ppermute | solution.py:221
  20.2 0.0 collective-permute-done.4
  20.2 1.3 %collective-permute-done.5 = bf16[1,80,256]{2,1,0:T(8,128)(2,1)S(1)} collective-permute-done((bf16[1,80,256]{2,1,0:T(8,128)(2,1)S(1)}, bf16[1,80,256]{2,1,0:T(8,128)(2,1)S(1)}, u32[]{:S(2)}, u32[]{:S(2)}) %collective-permute-start.5) | collective-permute-done | bytes 40992 | tf_op jit(solution)/shard_map/ppermute | solution.py:221
  21.5 0.0 collective-permute-done.6
  21.5 0.6 %collective-permute-done.7 = bf16[1,64,256]{2,1,0:T(8,128)(2,1)S(1)} collective-permute-done((bf16[1,64,256]{2,1,0:T(8,128)(2,1)S(1)}, bf16[1,64,256]{2,1,0:T(8,128)(2,1)S(1)}, u32[]{:S(2)}, u32[]{:S(2)}) %collective-permute-start.7) | collective-permute-done | bytes 32800 | tf_op jit(solution)/shard_map/ppermute | solution.py:221
  22.1 0.7 %multiply_add_fusion = (f32[64,256]{1,0:T(8,128)}, f32[64,256]{1,0:T(8,128)}) fusion(f32[64,256]{1,0:T(8,128)S(1)} %get-tuple-element.35, f32[64,256]{1,0:T(8,128)S(1)} %get-tuple-element.34, bf16[1,64,256]{2,1,0:T(8,128)(2,1)S(1)} %collective-permute-done.7, bf16[1,64,256]{2,1,0:T(8,128)(2,1)S(1)} %collective-permute-done.6, ...), kind=kLoop, calls=%fused_computation.1 | loop fusion | flops 163840 | bytes 458752 | tf_op jit(solution)/shard_map/add | solution.py:304
  (1 shorter events, 0.0 us)
Async XLA Ops:
  0.6 7.3 %collective-permute-start = (bf16[64,1024]{1,0:T(8,128)(2,1)}, bf16[64,1024]{1,0:T(8,128)(2,1)S(1)}, u32[]{:S(2)}, u32[]{:S(2)}) collective-permute-start(bf16[64,1024]{1,0:T(8,128)(2,1)} %slip_hbm.1), channel_id=1, source_target_pairs={{0,16},{8,24},{16,0},{24,8},{1,17},{9,25},{17,1},{25,9},{2,18},{10... | collective-permute-start | bytes 393224 | tf_op jit(solution)/shard_map/ppermute | solution.py:218
  3.6 4.9 %collective-permute-start.2 = (bf16[64,1024]{1,0:T(8,128)(2,1)}, bf16[64,1024]{1,0:T(8,128)(2,1)S(1)}, u32[]{:S(2)}, u32[]{:S(2)}) collective-permute-start(bf16[64,1024]{1,0:T(8,128)(2,1)} %slip_hbm.1), channel_id=1, source_target_pairs={{0,8},{8,0},{16,24},{24,16},{1,9},{9,1},{17,25},{25,17},{2,10},{10... | collective-permute-start | bytes 393224 | tf_op jit(solution)/shard_map/ppermute | solution.py:218
  7.9 1.9 %collective-permute-start.1 = (bf16[64,1024]{1,0:T(8,128)(2,1)S(1)}, bf16[64,1024]{1,0:T(8,128)(2,1)S(1)}, u32[]{:S(2)}, u32[]{:S(2)}) collective-permute-start(bf16[64,1024]{1,0:T(8,128)(2,1)S(1)} %collective-permute-done.refs_1_), channel_id=1, source_target_pairs={{0,8},{8,0},{16,24},{24,16},{1,9},{9,1},{17,25},{25,17},{2,10},{10... | collective-permute-start | bytes 393224 | tf_op jit(solution)/shard_map/ppermute | solution.py:218
  10.6 5.4 %collective-permute-start.3 = (bf16[6,64,128]{2,1,0:T(8,128)(2,1)S(1)}, bf16[6,64,128]{2,1,0:T(8,128)(2,1)S(1)}, u32[]{:S(2)}, u32[]{:S(2)}) collective-permute-start(bf16[6,64,128]{2,1,0:T(8,128)(2,1)S(1)} %get-tuple-element.28), channel_id=1, source_target_pairs={{0,1},{1,0},{2,3},{3,2},{4,5},{5,4},{6,7},{7,6},{8,9},{9,8},{10,11... | collective-permute-start | bytes 294920 | tf_op jit(solution)/shard_map/ppermute | solution.py:221
  12.2 8.0 %collective-permute-start.4 = (bf16[1,80,256]{2,1,0:T(8,128)(2,1)S(1)}, bf16[1,80,256]{2,1,0:T(8,128)(2,1)S(1)}, u32[]{:S(2)}, u32[]{:S(2)}) collective-permute-start(bf16[1,80,256]{2,1,0:T(8,128)(2,1)S(1)} %get-tuple-element.30), channel_id=1, source_target_pairs={{0,7},{1,6},{2,5},{3,4},{4,3},{5,2},{6,1},{7,0},{8,15},{9,14},{10,... | collective-permute-start | bytes 122888 | tf_op jit(solution)/shard_map/ppermute | solution.py:221
  15.7 5.8 %collective-permute-start.5 = (bf16[1,80,256]{2,1,0:T(8,128)(2,1)S(1)}, bf16[1,80,256]{2,1,0:T(8,128)(2,1)S(1)}, u32[]{:S(2)}, u32[]{:S(2)}) collective-permute-start(bf16[1,80,256]{2,1,0:T(8,128)(2,1)S(1)} %get-tuple-element.31), channel_id=1, source_target_pairs={{0,6},{1,7},{2,4},{3,5},{4,2},{5,3},{6,0},{7,1},{8,14},{9,15},{10,... | collective-permute-start | bytes 122888 | tf_op jit(solution)/shard_map/ppermute | solution.py:221
  16.0 5.5 %collective-permute-start.6 = (bf16[1,64,256]{2,1,0:T(8,128)(2,1)S(1)}, bf16[1,64,256]{2,1,0:T(8,128)(2,1)S(1)}, u32[]{:S(2)}, u32[]{:S(2)}) collective-permute-start(bf16[1,64,256]{2,1,0:T(8,128)(2,1)S(1)} %get-tuple-element.32), channel_id=1, source_target_pairs={{0,4},{1,5},{2,6},{3,7},{4,0},{5,1},{6,2},{7,3},{8,12},{9,13},{10,... | collective-permute-start | bytes 98312 | tf_op jit(solution)/shard_map/ppermute | solution.py:221
  18.1 4.0 %collective-permute-start.7 = (bf16[1,64,256]{2,1,0:T(8,128)(2,1)S(1)}, bf16[1,64,256]{2,1,0:T(8,128)(2,1)S(1)}, u32[]{:S(2)}, u32[]{:S(2)}) collective-permute-start(bf16[1,64,256]{2,1,0:T(8,128)(2,1)S(1)} %get-tuple-element.33), channel_id=1, source_target_pairs={{0,2},{1,3},{2,0},{3,1},{4,6},{5,7},{6,4},{7,5},{8,10},{9,11},{10,... | collective-permute-start | bytes 98312 | tf_op jit(solution)/shard_map/ppermute | solution.py:221

commit v5 on v4

--- a/solution.py
+++ b/solution.py
@@ -22,7 +22,7 @@
     return jnp.dot(left, right, preferred_element_type=F32)
 
 
-def add_far(slip, u_ref, v_ref, kept_ref, total, coeffs, fresh=False):
+def project(slip, u_ref, kept_ref, coeffs):
     count, width = kept_ref.shape
     place = lax.broadcasted_iota(I32, (1, LANES), 1) // KMAX
     for first in range(0, count, PACK):
@@ -42,13 +42,14 @@
                 for c in range(1, PACK):
                     row = jnp.where(place == c, turned[(c - i) % PACK], row)
                 coeffs[g * PACK + i, :, first * KMAX : (first + PACK) * KMAX] = row
-    for j in range(total.shape[0]):
-        order = []
-        for first in range(0, count, PACK):
-            order += [first + (c - j) % PACK for c in range(PACK)]
-        right = jnp.concatenate([v_ref[j, b * KMAX : (b + 1) * KMAX, :] for b in order], axis=0)
-        value = dot(coeffs[j], right)
-        total[j] = value if fresh else total[j] + value
+
+
+def far_block(coeffs, v_ref, j):
+    order = []
+    for first in range(0, v_ref.shape[1] // KMAX, PACK):
+        order += [first + (c - j) % PACK for c in range(PACK)]
+    rows = [v_ref[j, b * KMAX : (b + 1) * KMAX, :] for b in order]
+    return dot(coeffs[j], jnp.concatenate(rows, axis=0))
 
 
 def add_near(slip, near_ref, slots, s, total):
@@ -99,11 +100,9 @@
     later = []
     for i in range(3):
         s = me ^ (1 + i)
-        later += [
-            fetch(u_hbm.at[s], u_out.at[i]),
-            fetch(v_hbm.at[s], v_out.at[i]),
-            fetch(near_hbm.at[s], near_out.at[i]),
-        ]
+        later += [fetch(u_hbm.at[s], u_out.at[i]), fetch(near_hbm.at[s], near_out.at[i])]
+        if i < 2:
+            later.append(fetch(v_hbm.at[s], v_out.at[i]))
     wait_all(small)
     _, count, receivers = ranks.shape
     width = receivers * KMAX
@@ -121,7 +120,9 @@
             kept[i, b : b + 1, :] = keep.astype(F32)
 
     wait_all(mine)
-    add_far(slip[...], u_in, v_in, kept.at[0], total, coeffs, fresh=True)
+    project(slip[...], u_in, kept.at[0], coeffs)
+    for j in range(receivers):
+        total[j] = far_block(coeffs, v_in, j)
     add_near(slip[...], near_in, slots, me, total)
     wait_all(fields)
     rate, state = velocity[...], theta[...]
@@ -131,17 +132,37 @@
     wait_all(later)
 
 
-def later_kernel(offsets, final, *refs):
-    slips, refs = refs[: len(offsets)], refs[len(offsets) :]
-    u_ref, v_ref, near_ref, kept, slots, start, total, *refs = refs
-    *sent, coeffs = refs
+def middle_kernel(
+    sibling, across, u_ref, v_ref, near_ref, kept, slots, start, v_hbm, total, v_last,
+    coeffs, sem,
+):
     me = lax.axis_index("col")
-    for slip, i in zip(slips, offsets):
-        add_far(slip[...], u_ref.at[i - 1], v_ref.at[i - 1], kept.at[i], total, coeffs)
-        add_near(slip[...], near_ref.at[i - 1], slots, me ^ i, total)
-    if not final:
-        return
-    swapped, same, other = sent
+    copy = pltpu.make_async_copy(v_hbm.at[me ^ 3], v_last, sem)
+    copy.start()
+
+    @pl.when(me >= 0)
+    def _():
+        sections = ((1, sibling), (2, across))
+        for i, slip in sections:
+            project(slip[...], u_ref.at[i - 1], kept.at[i], coeffs.at[i - 1])
+        for i, slip in sections:
+            add_near(slip[...], near_ref.at[i - 1], slots, me ^ i, total)
+        for j in range(total.shape[0]):
+            total[j] += far_block(coeffs.at[0], v_ref.at[0], j) + far_block(
+                coeffs.at[1], v_ref.at[1], j
+            )
+
+    copy.wait()
+
+
+def last_kernel(
+    beyond, u_ref, v_ref, near_ref, kept, slots, start, total, swapped, same, other, coeffs
+):
+    me = lax.axis_index("col")
+    project(beyond[...], u_ref.at[2], kept.at[3], coeffs)
+    add_near(beyond[...], near_ref.at[2], slots, me ^ 3, total)
+    for j in range(total.shape[0]):
+        total[j] += far_block(coeffs, v_ref, j)
     mine, side, half = row_place(total)
     for k in range(3):
         for i in range(half):
@@ -232,7 +253,7 @@
         own_kernel,
         out_shape=[
             total_shape,
-            *[pltpu.VMEM((3, *w.shape[1:]), BF16) for w in weights],
+            *[pltpu.VMEM((n, *w.shape[1:]), BF16) for n, w in zip((3, 2, 3), weights)],
             pltpu.VMEM((groups, count, receivers * KMAX), F32), field, field, slots_smem,
         ],
         in_specs=[HBM_SPEC] * 10,
@@ -242,7 +263,7 @@
             *[pltpu.VMEM(w.shape[1:], BF16) for w in weights],
             pltpu.VMEM(ranks.shape, I32), field, field,
             pltpu.VMEM((1, owned), F32), pltpu.VMEM((1, owned), F32),
-            coeffs, pltpu.SemaphoreType.DMA((19,)),
+            coeffs, pltpu.SemaphoreType.DMA((18,)),
         ],
         **params(2 * members * size, 8 * size),
     )(
@@ -258,25 +279,31 @@
 
     shards = (per_group // 2, members, owned)
 
-    def later(offsets, slips, total):
-        final = offsets[-1] == 3
-        out_shape = [total_shape]
-        if final:
-            out_shape.append(pltpu.VMEM((3 * PACK // 2, members, LANES), BF16))
-            out_shape += [pltpu.VMEM((shards[0], members + PAD, owned), BF16)] * 2
-        return pl.pallas_call(
-            functools.partial(later_kernel, offsets, final),
-            out_shape=out_shape,
-            in_specs=[VMEM_SPEC] * (len(slips) + 4) + [SMEM_SPEC, VMEM_SPEC],
-            out_specs=[VMEM_SPEC] * len(out_shape),
-            scratch_shapes=[coeffs],
-            input_output_aliases={len(slips) + 5: 0},
-            **params(2 * members * size * len(slips), 2 * size * len(slips)),
-        )(*slips, u_later, v_later, near_later, kept, slots, total)
-
     beyond = col_swap(across, 1)
-    (total,) = later((1, 2), (sibling, across), total)
-    total, swapped, same, other = later((3,), (beyond,), total)
+    total, v_last = pl.pallas_call(
+        middle_kernel,
+        out_shape=[total_shape, pltpu.VMEM(lowrank_v.shape[1:], BF16)],
+        in_specs=[VMEM_SPEC] * 6 + [SMEM_SPEC, VMEM_SPEC, HBM_SPEC],
+        out_specs=[VMEM_SPEC] * 2,
+        scratch_shapes=[
+            pltpu.VMEM((2, receivers, members, depth), BF16), pltpu.SemaphoreType.DMA
+        ],
+        input_output_aliases={7: 0},
+        **params(4 * members * size, 4 * size),
+    )(sibling, across, u_later, v_later, near_later, kept, slots, total, in_hbm(lowrank_v))
+    total, swapped, same, other = pl.pallas_call(
+        last_kernel,
+        out_shape=[
+            total_shape,
+            pltpu.VMEM((3 * PACK // 2, members, LANES), BF16),
+            *[pltpu.VMEM((shards[0], members + PAD, owned), BF16)] * 2,
+        ],
+        in_specs=[VMEM_SPEC] * 5 + [SMEM_SPEC, VMEM_SPEC],
+        out_specs=[VMEM_SPEC] * 4,
+        scratch_shapes=[coeffs],
+        input_output_aliases={6: 0},
+        **params(2 * members * size, 2 * size),
+    )(beyond, u_later, v_last, near_later, kept, slots, total)
     swapped = row_swap(swapped, per_group // 2)
     other = row_swap(other, 3 * per_group + per_group // 2)
     same = row_swap(same, 3 * per_group)

time: 23 us -> 22.6 us (0.983)
  Pallas kernels: 6.37 us -> 5.91 us
    pallas_call x3, Pallas kernels: 6.34 us -> 5.88 us  [the longest x1 3.96 us: body(): pl.pallas_call(own_kernel, out_shape=[total_shape, *[pltpu.VMEM((n, *w.sh...]
  transfers between devices with their start and end apart: 8 -> 8, of which waited for: 2 -> 2; matrix products, arithmetic and copies ran while one was open for 0% -> 0% of each run, Pallas kernels for 25% -> 23%
where the time goes in v5:
time: 22.6 us; the launch traced here: 22.3 us
  starting transfers between devices  13.2 us (58%)
  Pallas kernels  5.91 us (26%)
  waiting for transfers between devices  1.9 us (8%)
  between operations  0.69 us (3%)
  other arithmetic  0.67 us (3%)
    ppermute x5, starting transfers between devices, row_swap(): return lax.ppermute(value, 'row', [(i, i ^ offset) for i in range(owners)])  9.59 us
    pallas_call x1, Pallas kernels, body(): pl.pallas_call(own_kernel, out_shape=[total_shape, *[pltpu.VMEM((n, *w.sh...  3.96 us
    ppermute x3, starting transfers between devices, col_swap(): return lax.ppermute(value, 'col', [(i, i ^ offset) for i in range(groups)])  3.58 us
    ppermute x5, waiting for transfers between devices, row_swap(): return lax.ppermute(value, 'row', [(i, i ^ offset) for i in range(owners)])  1.89 us
    pallas_call x1, Pallas kernels, body(): pl.pallas_call(middle_kernel, out_shape=[total_shape, pltpu.VMEM(lowrank_...  1.23 us
    pallas_call x1, Pallas kernels, body(): pl.pallas_call(last_kernel, out_shape=[total_shape, pltpu.VMEM((3 * PACK...  0.69 us
    add x1, other arithmetic, body(): return (stress_rate, stress_rate * gain + shift)  0.67 us
  transfers between devices with their start and end apart: 8, of which 2 were waited for; matrix products, arithmetic and copies ran while one was open for 0% of the time, Pallas kernels for 23%

profile of v5, /device:TPU:0, one launch (start us, length us, event | category | flops | bytes accessed | tf_op | source)
XLA Modules:
  0.0 22.3 jit_solution(4838428032688244758)
XLA Ops:
  0.6 3.0 %collective-permute-start = (bf16[64,1024]{1,0:T(8,128)(2,1)}, bf16[64,1024]{1,0:T(8,128)(2,1)S(1)}, u32[]{:S(2)}, u32[]{:S(2)}) collective-permute-start(bf16[64,1024]{1,0:T(8,128)(2,1)} %slip_hbm.1), channel_id=1, source_target_pairs={{0,16},{8,24},{16,0},{24,8},{1,17},{9,25},{17,1},{25,9},{2,18},{10... | collective-permute-start | bytes 393224 | tf_op jit(solution)/shard_map/ppermute | solution.py:239
  3.6 0.0 collective-permute-start.2
  3.6 4.0 %shard_map.113 = (f32[16,64,128]{2,1,0:T(8,128)S(1)}, bf16[3,1024,512]{2,1,0:T(8,128)(2,1)S(1)}, bf16[2,16,256,128]{3,2,1,0:T(8,128)(2,1)S(1)}, bf16[3,1024,256]...) custom-call(bf16[64,1024]{1,0:T(8,128)(2,1)} %slip_hbm.1, ...), custom_call_target="tpu_custom_call" | custom-call | flops 167772160 | bytes 10485760 | tf_op jit(solution)/shard_map/pallas_call | solution.py:252
  7.6 0.0 collective-permute-done.across
  7.6 0.6 %collective-permute-start.1 = (bf16[64,1024]{1,0:T(8,128)(2,1)S(1)}, bf16[64,1024]{1,0:T(8,128)(2,1)S(1)}, u32[]{:S(2)}, u32[]{:S(2)}) collective-permute-start(bf16[64,1024]{1,0:T(8,128)(2,1)S(1)} %collective-permute-done.across), channel_id=1, source_target_pairs={{0,8},{8,0},{16,24},{24,16},{1,9},{9,1},{17,25},{25,17},{2,10},{10... | collective-permute-start | bytes 393224 | tf_op jit(solution)/shard_map/ppermute | solution.py:239
  8.2 0.0 collective-permute-done.2.sibling
  8.2 1.2 %shard_map.114 = (f32[16,64,128]{2,1,0:T(8,128)S(1)}, bf16[16,256,128]{2,1,0:T(8,128)(2,1)S(1)}) custom-call(bf16[64,1024]{1,0:T(8,128)(2,1)S(1)} %collective-permute-done.2.sibling, bf16[64,1024]{1,0:T(8,128)(2,1)S(1)} %collective-permute-done.across, bf16[3,1024,512]{2,1,0:T(8,128)(2,1)S(1)} %get-tuple-element.23.u_ref, ...), custom_call_target="tpu_custom_call", output_to_operand_aliasing={{0}: (7, {})} | custom-call | flops 335544320 | bytes 5242880 | tf_op jit(solution)/shard_map/pallas_call | solution.py:283
  9.4 0.0 collective-permute-done.1.beyond
  9.4 0.7 %shard_map.115 = (f32[16,64,128]{2,1,0:T(8,128)S(1)}, bf16[6,64,128]{2,1,0:T(8,128)(2,1)S(1)}, bf16[1,80,256]{2,1,0:T(8,128)(2,1)S(1)}, bf16[1,80,256]{2,1,0:T(8,128)(2,1)S(1)}) custom-call(bf16[64,1024]{1,0:T(8,128)(2,1)S(1)} %collective-permute-done.1.beyond, bf16[3,1024,512]{2,1,0:T(8,128)(2,1)S(1)} %get-tuple-element.23.u_ref, ...), custom_call_target="tpu_custom_call", output_to_operand_aliasing={{0}: (6, {})} | custom-call | flops 167772160 | bytes 2621440 | tf_op jit(solution)/shard_map/pallas_call | solution.py:294
  10.1 1.6 %collective-permute-start.3 = (bf16[6,64,128]{2,1,0:T(8,128)(2,1)S(1)}, bf16[6,64,128]{2,1,0:T(8,128)(2,1)S(1)}, u32[]{:S(2)}, u32[]{:S(2)}) collective-permute-start(bf16[6,64,128]{2,1,0:T(8,128)(2,1)S(1)} %get-tuple-element.32), channel_id=1, source_target_pairs={{0,1},{1,0},{2,3},{3,2},{4,5},{5,4},{6,7},{7,6},{8,9},{9,8},{10,11... | collective-permute-start | bytes 294920 | tf_op jit(solution)/shard_map/ppermute | solution.py:242
  11.7 3.6 %collective-permute-start.4 = (bf16[1,80,256]{2,1,0:T(8,128)(2,1)S(1)}, bf16[1,80,256]{2,1,0:T(8,128)(2,1)S(1)}, u32[]{:S(2)}, u32[]{:S(2)}) collective-permute-start(bf16[1,80,256]{2,1,0:T(8,128)(2,1)S(1)} %get-tuple-element.34), channel_id=1, source_target_pairs={{0,7},{1,6},{2,5},{3,4},{4,3},{5,2},{6,1},{7,0},{8,15},{9,14},{10,... | collective-permute-start | bytes 122888 | tf_op jit(solution)/shard_map/ppermute | solution.py:242
  15.3 0.2 collective-permute-start.5
  15.5 0.0 collective-permute-done.3.received
  15.5 2.1 %collective-permute-start.6 = (bf16[1,64,256]{2,1,0:T(8,128)(2,1)S(1)}, bf16[1,64,256]{2,1,0:T(8,128)(2,1)S(1)}, u32[]{:S(2)}, u32[]{:S(2)}) collective-permute-start(bf16[1,64,256]{2,1,0:T(8,128)(2,1)S(1)} %get-tuple-element.36), channel_id=1, source_target_pairs={{0,4},{1,5},{2,6},{3,7},{4,0},{5,1},{6,2},{7,3},{8,12},{9,13},{10,... | collective-permute-start | bytes 98312 | tf_op jit(solution)/shard_map/ppermute | solution.py:242
  17.7 2.1 %collective-permute-start.7 = (bf16[1,64,256]{2,1,0:T(8,128)(2,1)S(1)}, bf16[1,64,256]{2,1,0:T(8,128)(2,1)S(1)}, u32[]{:S(2)}, u32[]{:S(2)}) collective-permute-start(bf16[1,64,256]{2,1,0:T(8,128)(2,1)S(1)} %get-tuple-element.37), channel_id=1, source_target_pairs={{0,2},{1,3},{2,0},{3,1},{4,6},{5,7},{6,4},{7,5},{8,10},{9,11},{10,... | collective-permute-start | bytes 98312 | tf_op jit(solution)/shard_map/ppermute | solution.py:242
  19.8 0.0 collective-permute-done.4
  19.8 1.3 %collective-permute-done.5 = bf16[1,80,256]{2,1,0:T(8,128)(2,1)S(1)} collective-permute-done((bf16[1,80,256]{2,1,0:T(8,128)(2,1)S(1)}, bf16[1,80,256]{2,1,0:T(8,128)(2,1)S(1)}, u32[]{:S(2)}, u32[]{:S(2)}) %collective-permute-start.5) | collective-permute-done | bytes 40992 | tf_op jit(solution)/shard_map/ppermute | solution.py:242
  21.1 0.0 collective-permute-done.6
  21.1 0.6 %collective-permute-done.7 = bf16[1,64,256]{2,1,0:T(8,128)(2,1)S(1)} collective-permute-done((bf16[1,64,256]{2,1,0:T(8,128)(2,1)S(1)}, bf16[1,64,256]{2,1,0:T(8,128)(2,1)S(1)}, u32[]{:S(2)}, u32[]{:S(2)}) %collective-permute-start.7) | collective-permute-done | bytes 32800 | tf_op jit(solution)/shard_map/ppermute | solution.py:242
  21.7 0.7 %multiply_add_fusion = (f32[64,256]{1,0:T(8,128)}, f32[64,256]{1,0:T(8,128)}) fusion(f32[64,256]{1,0:T(8,128)S(1)} %get-tuple-element.39, f32[64,256]{1,0:T(8,128)S(1)} %get-tuple-element.38, bf16[1,64,256]{2,1,0:T(8,128)(2,1)S(1)} %collective-permute-done.7, bf16[1,64,256]{2,1,0:T(8,128)(2,1)S(1)} %collective-permute-done.6, ...), kind=kLoop, calls=%fused_computation.1 | loop fusion | flops 163840 | bytes 458752 | tf_op jit(solution)/shard_map/add | solution.py:331
  (1 shorter events, 0.0 us)
Async XLA Ops:
  0.6 7.0 %collective-permute-start = (bf16[64,1024]{1,0:T(8,128)(2,1)}, bf16[64,1024]{1,0:T(8,128)(2,1)S(1)}, u32[]{:S(2)}, u32[]{:S(2)}) collective-permute-start(bf16[64,1024]{1,0:T(8,128)(2,1)} %slip_hbm.1), channel_id=1, source_target_pairs={{0,16},{8,24},{16,0},{24,8},{1,17},{9,25},{17,1},{25,9},{2,18},{10... | collective-permute-start | bytes 393224 | tf_op jit(solution)/shard_map/ppermute | solution.py:239
  3.6 4.6 %collective-permute-start.2 = (bf16[64,1024]{1,0:T(8,128)(2,1)}, bf16[64,1024]{1,0:T(8,128)(2,1)S(1)}, u32[]{:S(2)}, u32[]{:S(2)}) collective-permute-start(bf16[64,1024]{1,0:T(8,128)(2,1)} %slip_hbm.1), channel_id=1, source_target_pairs={{0,8},{8,0},{16,24},{24,16},{1,9},{9,1},{17,25},{25,17},{2,10},{10... | collective-permute-start | bytes 393224 | tf_op jit(solution)/shard_map/ppermute | solution.py:239
  7.6 1.8 %collective-permute-start.1 = (bf16[64,1024]{1,0:T(8,128)(2,1)S(1)}, bf16[64,1024]{1,0:T(8,128)(2,1)S(1)}, u32[]{:S(2)}, u32[]{:S(2)}) collective-permute-start(bf16[64,1024]{1,0:T(8,128)(2,1)S(1)} %collective-permute-done.across), channel_id=1, source_target_pairs={{0,8},{8,0},{16,24},{24,16},{1,9},{9,1},{17,25},{25,17},{2,10},{10... | collective-permute-start | bytes 393224 | tf_op jit(solution)/shard_map/ppermute | solution.py:239
  10.1 5.4 %collective-permute-start.3 = (bf16[6,64,128]{2,1,0:T(8,128)(2,1)S(1)}, bf16[6,64,128]{2,1,0:T(8,128)(2,1)S(1)}, u32[]{:S(2)}, u32[]{:S(2)}) collective-permute-start(bf16[6,64,128]{2,1,0:T(8,128)(2,1)S(1)} %get-tuple-element.32), channel_id=1, source_target_pairs={{0,1},{1,0},{2,3},{3,2},{4,5},{5,4},{6,7},{7,6},{8,9},{9,8},{10,11... | collective-permute-start | bytes 294920 | tf_op jit(solution)/shard_map/ppermute | solution.py:242
  11.7 8.0 %collective-permute-start.4 = (bf16[1,80,256]{2,1,0:T(8,128)(2,1)S(1)}, bf16[1,80,256]{2,1,0:T(8,128)(2,1)S(1)}, u32[]{:S(2)}, u32[]{:S(2)}) collective-permute-start(bf16[1,80,256]{2,1,0:T(8,128)(2,1)S(1)} %get-tuple-element.34), channel_id=1, source_target_pairs={{0,7},{1,6},{2,5},{3,4},{4,3},{5,2},{6,1},{7,0},{8,15},{9,14},{10,... | collective-permute-start | bytes 122888 | tf_op jit(solution)/shard_map/ppermute | solution.py:242
  15.3 5.8 %collective-permute-start.5 = (bf16[1,80,256]{2,1,0:T(8,128)(2,1)S(1)}, bf16[1,80,256]{2,1,0:T(8,128)(2,1)S(1)}, u32[]{:S(2)}, u32[]{:S(2)}) collective-permute-start(bf16[1,80,256]{2,1,0:T(8,128)(2,1)S(1)} %get-tuple-element.35), channel_id=1, source_target_pairs={{0,6},{1,7},{2,4},{3,5},{4,2},{5,3},{6,0},{7,1},{8,14},{9,15},{10,... | collective-permute-start | bytes 122888 | tf_op jit(solution)/shard_map/ppermute | solution.py:242
  15.5 5.6 %collective-permute-start.6 = (bf16[1,64,256]{2,1,0:T(8,128)(2,1)S(1)}, bf16[1,64,256]{2,1,0:T(8,128)(2,1)S(1)}, u32[]{:S(2)}, u32[]{:S(2)}) collective-permute-start(bf16[1,64,256]{2,1,0:T(8,128)(2,1)S(1)} %get-tuple-element.36), channel_id=1, source_target_pairs={{0,4},{1,5},{2,6},{3,7},{4,0},{5,1},{6,2},{7,3},{8,12},{9,13},{10,... | collective-permute-start | bytes 98312 | tf_op jit(solution)/shard_map/ppermute | solution.py:242
  17.7 4.0 %collective-permute-start.7 = (bf16[1,64,256]{2,1,0:T(8,128)(2,1)S(1)}, bf16[1,64,256]{2,1,0:T(8,128)(2,1)S(1)}, u32[]{:S(2)}, u32[]{:S(2)}) collective-permute-start(bf16[1,64,256]{2,1,0:T(8,128)(2,1)S(1)} %get-tuple-element.37), channel_id=1, source_target_pairs={{0,2},{1,3},{2,0},{3,1},{4,6},{5,7},{6,4},{7,5},{8,10},{9,11},{10,... | collective-permute-start | bytes 98312 | tf_op jit(solution)/shard_map/ppermute | solution.py:242

commit v6 on v5

--- a/solution.py
+++ b/solution.py
@@ -13,6 +13,7 @@
 PACK = LANES // KMAX
 VMEM_LIMIT = 32 * 2**20
 PAD = 16
+TURNS = (0, 1, 3)
 HBM_SPEC = pl.BlockSpec(memory_space=pltpu.HBM)
 VMEM_SPEC = pl.BlockSpec(memory_space=pltpu.VMEM)
 SMEM_SPEC = pl.BlockSpec(memory_space=pltpu.SMEM)
@@ -63,11 +64,12 @@
 
 class Fetches:
     def __init__(self, sems):
-        self.sems, self.used = sems, 0
-
-    def __call__(self, source, target):
-        copy = pltpu.make_async_copy(source, target, self.sems.at[self.used])
-        self.used += 1
+        self.sems, self.used = sems, 3
+
+    def __call__(self, source, target, shared=None):
+        own = self.used if shared is None else shared
+        copy = pltpu.make_async_copy(source, target, self.sems.at[own])
+        self.used += shared is None
         copy.start()
         return copy
 
@@ -97,39 +99,45 @@
         fetch(a_hbm, a_sigma),
         fetch(b_hbm, b_sigma),
     ]
-    later = []
     for i in range(3):
         s = me ^ (1 + i)
-        later += [fetch(u_hbm.at[s], u_out.at[i]), fetch(near_hbm.at[s], near_out.at[i])]
+        fetch(u_hbm.at[s], u_out.at[i], 0)
+        fetch(near_hbm.at[s], near_out.at[i], 1)
         if i < 2:
-            later.append(fetch(v_hbm.at[s], v_out.at[i]))
-    wait_all(small)
-    _, count, receivers = ranks.shape
-    width = receivers * KMAX
-    column = lax.broadcasted_iota(I32, (receivers, width), 1)
-    spread = column // KMAX == lax.broadcasted_iota(I32, (receivers, width), 0)
-    lane = lax.broadcasted_iota(I32, (1, width), 1)
-    block, index = lane // KMAX, (lane % KMAX).astype(F32)
-    for i in range(4):
-        s = me ^ i
-        wide = dot(ranks[s].astype(F32).astype(BF16), spread.astype(BF16))
-        for b in range(count):
-            keep = index < wide[b : b + 1, :]
-            for slot in range(slots.shape[1]):
-                keep = keep & (block != slots[s, slot, b])
-            kept[i, b : b + 1, :] = keep.astype(F32)
-
-    wait_all(mine)
-    project(slip[...], u_in, kept.at[0], coeffs)
-    for j in range(receivers):
-        total[j] = far_block(coeffs, v_in, j)
-    add_near(slip[...], near_in, slots, me, total)
-    wait_all(fields)
-    rate, state = velocity[...], theta[...]
-    divisor = 1.0 / (a_sigma[...] / rate + 0.5)
-    gain[...] = divisor
-    shift[...] = -(b_sigma[...] * (1.0 - rate * state) / state) * divisor
-    wait_all(later)
+            fetch(v_hbm.at[s], v_out.at[i], 2)
+    later = [
+        pltpu.make_async_copy(whole, whole, sems.at[n])
+        for n, whole in enumerate((u_out, near_out, v_out))
+    ]
+    @pl.when(me >= 0)
+    def _():
+        wait_all(small)
+        _, count, receivers = ranks.shape
+        width = receivers * KMAX
+        column = lax.broadcasted_iota(I32, (receivers, width), 1)
+        spread = column // KMAX == lax.broadcasted_iota(I32, (receivers, width), 0)
+        lane = lax.broadcasted_iota(I32, (1, width), 1)
+        block, index = lane // KMAX, (lane % KMAX).astype(F32)
+        for i in range(4):
+            s = me ^ i
+            wide = dot(ranks[s].astype(F32).astype(BF16), spread.astype(BF16))
+            for b in range(count):
+                keep = index < wide[b : b + 1, :]
+                for slot in range(slots.shape[1]):
+                    keep = keep & (block != slots[s, slot, b])
+                kept[i, b : b + 1, :] = keep.astype(F32)
+
+        wait_all(mine)
+        project(slip[...], u_in, kept.at[0], coeffs)
+        for j in range(receivers):
+            total[j] = far_block(coeffs, v_in, j)
+        add_near(slip[...], near_in, slots, me, total)
+        wait_all(fields)
+        rate, state = velocity[...], theta[...]
+        divisor = 1.0 / (a_sigma[...] / rate + 0.5)
+        gain[...] = divisor
+        shift[...] = -(b_sigma[...] * (1.0 - rate * state) / state) * divisor
+        wait_all(later)
 
 
 def middle_kernel(
@@ -166,12 +174,16 @@
     mine, side, half = row_place(total)
     for k in range(3):
         for i in range(half):
-            block = total[(mine ^ k) * PACK + (1 - side) * half + i]
+            block = total[turn(mine, TURNS[k]) * PACK + (1 - side) * half + i]
             swapped[k * half + i] = block.astype(swapped.dtype)
     for target, to_side in ((same, side), (other, 1 - side)):
         target[:, total.shape[1] :, :] = jnp.zeros_like(target[:, total.shape[1] :, :])
         for i in range(half):
-            write_block(target, i, total[(mine ^ 3) * PACK + to_side * half + i])
+            write_block(target, i, total[turn(mine, 2) * PACK + to_side * half + i])
+
+
+def turn(group, by):
+    return lax.rem(group + by, 4)
 
 
 def row_place(total):
@@ -194,7 +206,7 @@
     mine, side, half = row_place(total)
     for k, target in enumerate(outs):
         for i in range(half):
-            block = total[(mine ^ k) * PACK + side * half + i] + received[k * half + i].astype(F32)
+            block = total[turn(mine, TURNS[k]) * PACK + side * half + i] + received[k * half + i].astype(F32)
             write_block(target, i, block)
 
 
@@ -263,7 +275,7 @@
             *[pltpu.VMEM(w.shape[1:], BF16) for w in weights],
             pltpu.VMEM(ranks.shape, I32), field, field,
             pltpu.VMEM((1, owned), F32), pltpu.VMEM((1, owned), F32),
-            coeffs, pltpu.SemaphoreType.DMA((18,)),
+            coeffs, pltpu.SemaphoreType.DMA((13,)),
         ],
         **params(2 * members * size, 8 * size),
     )(
@@ -304,9 +316,12 @@
         input_output_aliases={6: 0},
         **params(2 * members * size, 2 * size),
     )(beyond, u_later, v_last, near_later, kept, slots, total)
+    def group_send(value, by):
+        return lax.ppermute(value, "row", [(i, (i + by * per_group) % owners) for i in range(owners)])
+
     swapped = row_swap(swapped, per_group // 2)
-    other = row_swap(other, 3 * per_group + per_group // 2)
-    same = row_swap(same, 3 * per_group)
+    other = row_swap(other, owners // 2 + per_group // 2)
+    same = row_swap(same, owners // 2)
     own, first, second = pl.pallas_call(
         join_kernel,
         out_shape=[pltpu.VMEM(shards, dtype) for dtype in (F32, BF16, BF16)],
@@ -314,7 +329,7 @@
         out_specs=[VMEM_SPEC] * 3,
         **params(0, 8 * swapped.size),
     )(total, swapped)
-    received = [other, same, row_swap(second, 2 * per_group), row_swap(first, per_group)]
+    received = [other, same, group_send(first, 1), group_send(second, 3)]
     for place in reversed(range(per_group.bit_length() - 2)):
         shape = (own.shape[0] // 2, members, owned)
         sent, own = pl.pallas_call(

time: 22.6 us -> 21.8 us (0.965)
  starting transfers between devices: 13.2 us -> 11.9 us
  waiting for transfers between devices: 1.9 us -> 2.47 us
    ppermute x5 -> x3, starting transfers between devices: 9.59 us -> 4.45 us  [row_swap(): return lax.ppermute(value, 'row', [(i, i ^ offset) for i in range(owners)])]
    ppermute x0 -> x2, starting transfers between devices: none -> 3.88 us  [group_send(): lax.ppermute(value, 'row', [(i, (i + by * per_group) % owners) for i in r...]
    ppermute x0 -> x2, waiting for transfers between devices: none -> 1.11 us  [group_send(): lax.ppermute(value, 'row', [(i, (i + by * per_group) % owners) for i in r...]
    ppermute x5 -> x3, waiting for transfers between devices: 1.89 us -> 1.34 us  [row_swap(): return lax.ppermute(value, 'row', [(i, i ^ offset) for i in range(owners)])]
  transfers between devices with their start and end apart: 8 -> 8, of which waited for: 2 -> 3; matrix products, arithmetic and copies ran while one was open for 0% -> 0% of each run, Pallas kernels for 23% -> 24%
where the time goes in v6:
time: 21.8 us; the launch traced here: 21.6 us
  starting transfers between devices  11.9 us (55%)
  Pallas kernels  5.87 us (27%)
  waiting for transfers between devices  2.47 us (11%)
  other arithmetic  0.68 us (3%)
  between operations  0.68 us (3%)
    ppermute x3, starting transfers between devices, row_swap(): return lax.ppermute(value, 'row', [(i, i ^ offset) for i in range(owners)])  4.45 us
    pallas_call x1, Pallas kernels, body(): pl.pallas_call(own_kernel, out_shape=[total_shape, *[pltpu.VMEM((n, *w.sh...  3.92 us
    ppermute x2, starting transfers between devices, group_send(): lax.ppermute(value, 'row', [(i, (i + by * per_group) % owners) for i in r...  3.88 us
    ppermute x3, starting transfers between devices, col_swap(): return lax.ppermute(value, 'col', [(i, i ^ offset) for i in range(groups)])  3.58 us
    ppermute x3, waiting for transfers between devices, row_swap(): return lax.ppermute(value, 'row', [(i, i ^ offset) for i in range(owners)])  1.34 us
    pallas_call x1, Pallas kernels, body(): pl.pallas_call(middle_kernel, out_shape=[total_shape, pltpu.VMEM(lowrank_...  1.23 us
    ppermute x2, waiting for transfers between devices, group_send(): lax.ppermute(value, 'row', [(i, (i + by * per_group) % owners) for i in r...  1.11 us
    pallas_call x1, Pallas kernels, body(): pl.pallas_call(last_kernel, out_shape=[total_shape, pltpu.VMEM((3 * PACK...  0.69 us
  transfers between devices with their start and end apart: 8, of which 3 were waited for; matrix products, arithmetic and copies ran while one was open for 0% of the time, Pallas kernels for 24%

profile of v6, /device:TPU:0, one launch (start us, length us, event | category | flops | bytes accessed | tf_op | source)
XLA Modules:
  0.0 21.6 jit_solution(8713430607226518367)
XLA Ops:
  0.6 3.0 %collective-permute-start = (bf16[64,1024]{1,0:T(8,128)(2,1)}, bf16[64,1024]{1,0:T(8,128)(2,1)S(1)}, u32[]{:S(2)}, u32[]{:S(2)}) collective-permute-start(bf16[64,1024]{1,0:T(8,128)(2,1)} %slip_hbm.1), channel_id=1, source_target_pairs={{0,16},{8,24},{16,0},{24,8},{1,17},{9,25},{17,1},{25,9},{2,18},{10... | collective-permute-start | bytes 393224 | tf_op jit(solution)/shard_map/ppermute | solution.py:251
  3.6 0.0 collective-permute-start.2
  3.6 3.9 %shard_map.113 = (f32[16,64,128]{2,1,0:T(8,128)S(1)}, bf16[3,1024,512]{2,1,0:T(8,128)(2,1)S(1)}, bf16[2,16,256,128]{3,2,1,0:T(8,128)(2,1)S(1)}, bf16[3,1024,256]...) custom-call(bf16[64,1024]{1,0:T(8,128)(2,1)} %slip_hbm.1, ...), custom_call_target="tpu_custom_call" | custom-call | flops 167772160 | bytes 10485760 | tf_op jit(solution)/shard_map/pallas_call | solution.py:264
  7.6 0.0 collective-permute-done.across
  7.6 0.6 %collective-permute-start.1 = (bf16[64,1024]{1,0:T(8,128)(2,1)S(1)}, bf16[64,1024]{1,0:T(8,128)(2,1)S(1)}, u32[]{:S(2)}, u32[]{:S(2)}) collective-permute-start(bf16[64,1024]{1,0:T(8,128)(2,1)S(1)} %collective-permute-done.across), channel_id=1, source_target_pairs={{0,8},{8,0},{16,24},{24,16},{1,9},{9,1},{17,25},{25,17},{2,10},{10... | collective-permute-start | bytes 393224 | tf_op jit(solution)/shard_map/ppermute | solution.py:251
  8.2 0.0 collective-permute-done.2.sibling
  8.2 1.2 %shard_map.114 = (f32[16,64,128]{2,1,0:T(8,128)S(1)}, bf16[16,256,128]{2,1,0:T(8,128)(2,1)S(1)}) custom-call(bf16[64,1024]{1,0:T(8,128)(2,1)S(1)} %collective-permute-done.2.sibling, bf16[64,1024]{1,0:T(8,128)(2,1)S(1)} %collective-permute-done.across, bf16[3,1024,512]{2,1,0:T(8,128)(2,1)S(1)} %get-tuple-element.23.u_ref, ...), custom_call_target="tpu_custom_call", output_to_operand_aliasing={{0}: (7, {})} | custom-call | flops 335544320 | bytes 5242880 | tf_op jit(solution)/shard_map/pallas_call | solution.py:295
  9.4 0.0 collective-permute-done.1.beyond
  9.4 0.7 %shard_map.115 = (f32[16,64,128]{2,1,0:T(8,128)S(1)}, bf16[6,64,128]{2,1,0:T(8,128)(2,1)S(1)}, bf16[1,80,256]{2,1,0:T(8,128)(2,1)S(1)}, bf16[1,80,256]{2,1,0:T(8,128)(2,1)S(1)}) custom-call(bf16[64,1024]{1,0:T(8,128)(2,1)S(1)} %collective-permute-done.1.beyond, bf16[3,1024,512]{2,1,0:T(8,128)(2,1)S(1)} %get-tuple-element.23.u_ref, ...), custom_call_target="tpu_custom_call", output_to_operand_aliasing={{0}: (6, {})} | custom-call | flops 167772160 | bytes 2621440 | tf_op jit(solution)/shard_map/pallas_call | solution.py:306
  10.1 1.6 %collective-permute-start.3 = (bf16[6,64,128]{2,1,0:T(8,128)(2,1)S(1)}, bf16[6,64,128]{2,1,0:T(8,128)(2,1)S(1)}, u32[]{:S(2)}, u32[]{:S(2)}) collective-permute-start(bf16[6,64,128]{2,1,0:T(8,128)(2,1)S(1)} %get-tuple-element.32), channel_id=1, source_target_pairs={{0,1},{1,0},{2,3},{3,2},{4,5},{5,4},{6,7},{7,6},{8,9},{9,8},{10,11... | collective-permute-start | bytes 294920 | tf_op jit(solution)/shard_map/ppermute | solution.py:254
  11.7 2.5 %collective-permute-start.4 = (bf16[1,80,256]{2,1,0:T(8,128)(2,1)S(1)}, bf16[1,80,256]{2,1,0:T(8,128)(2,1)S(1)}, u32[]{:S(2)}, u32[]{:S(2)}) collective-permute-start(bf16[1,80,256]{2,1,0:T(8,128)(2,1)S(1)} %get-tuple-element.34), channel_id=1, source_target_pairs={{0,5},{1,4},{2,7},{3,6},{4,1},{5,0},{6,3},{7,2},{8,13},{9,12},{10,... | collective-permute-start | bytes 122888 | tf_op jit(solution)/shard_map/ppermute | solution.py:254
  14.2 0.3 %collective-permute-start.5 = (bf16[1,80,256]{2,1,0:T(8,128)(2,1)S(1)}, bf16[1,80,256]{2,1,0:T(8,128)(2,1)S(1)}, u32[]{:S(2)}, u32[]{:S(2)}) collective-permute-start(bf16[1,80,256]{2,1,0:T(8,128)(2,1)S(1)} %get-tuple-element.35), channel_id=1, source_target_pairs={{0,4},{1,5},{2,6},{3,7},{4,0},{5,1},{6,2},{7,3},{8,12},{9,13},{10,... | collective-permute-start | bytes 122888 | tf_op jit(solution)/shard_map/ppermute | solution.py:254
  14.6 0.4 %collective-permute-done.3.received = bf16[6,64,128]{2,1,0:T(8,128)(2,1)S(1)} collective-permute-done((bf16[6,64,128]{2,1,0:T(8,128)(2,1)S(1)}, bf16[6,64,128]{2,1,0:T(8,128)(2,1)S(1)}, u32[]{:S(2)}, u32[]{:S(2)}) %collective-permute-start.3) | collective-permute-done | bytes 98336 | tf_op jit(solution)/shard_map/ppermute | solution.py:254
  15.0 1.6 %collective-permute-start.6 = (bf16[1,64,256]{2,1,0:T(8,128)(2,1)S(1)}, bf16[1,64,256]{2,1,0:T(8,128)(2,1)S(1)}, u32[]{:S(2)}, u32[]{:S(2)}) collective-permute-start(bf16[1,64,256]{2,1,0:T(8,128)(2,1)S(1)} %get-tuple-element.36), channel_id=1, source_target_pairs={{0,2},{1,3},{2,4},{3,5},{4,6},{5,7},{6,0},{7,1},{8,10},{9,11},{10,... | collective-permute-start | bytes 98312 | tf_op jit(solution)/shard_map/ppermute | solution.py:320
  16.6 2.2 %collective-permute-start.7 = (bf16[1,64,256]{2,1,0:T(8,128)(2,1)S(1)}, bf16[1,64,256]{2,1,0:T(8,128)(2,1)S(1)}, u32[]{:S(2)}, u32[]{:S(2)}) collective-permute-start(bf16[1,64,256]{2,1,0:T(8,128)(2,1)S(1)} %get-tuple-element.37), channel_id=1, source_target_pairs={{0,6},{1,7},{2,0},{3,1},{4,2},{5,3},{6,4},{7,5},{8,14},{9,15},{10,... | collective-permute-start | bytes 98312 | tf_op jit(solution)/shard_map/ppermute | solution.py:320
  18.9 0.0 collective-permute-done.4
  18.9 0.9 %collective-permute-done.5 = bf16[1,80,256]{2,1,0:T(8,128)(2,1)S(1)} collective-permute-done((bf16[1,80,256]{2,1,0:T(8,128)(2,1)S(1)}, bf16[1,80,256]{2,1,0:T(8,128)(2,1)S(1)}, u32[]{:S(2)}, u32[]{:S(2)}) %collective-permute-start.5) | collective-permute-done | bytes 40992 | tf_op jit(solution)/shard_map/ppermute | solution.py:254
  19.8 1.1 %collective-permute-done.6 = bf16[1,64,256]{2,1,0:T(8,128)(2,1)S(1)} collective-permute-done((bf16[1,64,256]{2,1,0:T(8,128)(2,1)S(1)}, bf16[1,64,256]{2,1,0:T(8,128)(2,1)S(1)}, u32[]{:S(2)}, u32[]{:S(2)}) %collective-permute-start.6) | collective-permute-done | bytes 32800 | tf_op jit(solution)/shard_map/ppermute | solution.py:320
  20.9 0.0 collective-permute-done.7
  20.9 0.7 %multiply_add_fusion = (f32[64,256]{1,0:T(8,128)}, f32[64,256]{1,0:T(8,128)}) fusion(f32[64,256]{1,0:T(8,128)S(1)} %get-tuple-element.39, f32[64,256]{1,0:T(8,128)S(1)} %get-tuple-element.38, bf16[1,64,256]{2,1,0:T(8,128)(2,1)S(1)} %collective-permute-done.7, bf16[1,64,256]{2,1,0:T(8,128)(2,1)S(1)} %collective-permute-done.6, ...), kind=kLoop, calls=%fused_computation.1 | loop fusion | flops 163840 | bytes 458752 | tf_op jit(solution)/shard_map/add | solution.py:346
  (1 shorter events, 0.0 us)
Async XLA Ops:
  0.6 6.9 %collective-permute-start = (bf16[64,1024]{1,0:T(8,128)(2,1)}, bf16[64,1024]{1,0:T(8,128)(2,1)S(1)}, u32[]{:S(2)}, u32[]{:S(2)}) collective-permute-start(bf16[64,1024]{1,0:T(8,128)(2,1)} %slip_hbm.1), channel_id=1, source_target_pairs={{0,16},{8,24},{16,0},{24,8},{1,17},{9,25},{17,1},{25,9},{2,18},{10... | collective-permute-start | bytes 393224 | tf_op jit(solution)/shard_map/ppermute | solution.py:251
  3.6 4.5 %collective-permute-start.2 = (bf16[64,1024]{1,0:T(8,128)(2,1)}, bf16[64,1024]{1,0:T(8,128)(2,1)S(1)}, u32[]{:S(2)}, u32[]{:S(2)}) collective-permute-start(bf16[64,1024]{1,0:T(8,128)(2,1)} %slip_hbm.1), channel_id=1, source_target_pairs={{0,8},{8,0},{16,24},{24,16},{1,9},{9,1},{17,25},{25,17},{2,10},{10... | collective-permute-start | bytes 393224 | tf_op jit(solution)/shard_map/ppermute | solution.py:251
  7.6 1.8 %collective-permute-start.1 = (bf16[64,1024]{1,0:T(8,128)(2,1)S(1)}, bf16[64,1024]{1,0:T(8,128)(2,1)S(1)}, u32[]{:S(2)}, u32[]{:S(2)}) collective-permute-start(bf16[64,1024]{1,0:T(8,128)(2,1)S(1)} %collective-permute-done.across), channel_id=1, source_target_pairs={{0,8},{8,0},{16,24},{24,16},{1,9},{9,1},{17,25},{25,17},{2,10},{10... | collective-permute-start | bytes 393224 | tf_op jit(solution)/shard_map/ppermute | solution.py:251
  10.1 4.9 %collective-permute-start.3 = (bf16[6,64,128]{2,1,0:T(8,128)(2,1)S(1)}, bf16[6,64,128]{2,1,0:T(8,128)(2,1)S(1)}, u32[]{:S(2)}, u32[]{:S(2)}) collective-permute-start(bf16[6,64,128]{2,1,0:T(8,128)(2,1)S(1)} %get-tuple-element.32), channel_id=1, source_target_pairs={{0,1},{1,0},{2,3},{3,2},{4,5},{5,4},{6,7},{7,6},{8,9},{9,8},{10,11... | collective-permute-start | bytes 294920 | tf_op jit(solution)/shard_map/ppermute | solution.py:254
  11.7 7.2 %collective-permute-start.4 = (bf16[1,80,256]{2,1,0:T(8,128)(2,1)S(1)}, bf16[1,80,256]{2,1,0:T(8,128)(2,1)S(1)}, u32[]{:S(2)}, u32[]{:S(2)}) collective-permute-start(bf16[1,80,256]{2,1,0:T(8,128)(2,1)S(1)} %get-tuple-element.34), channel_id=1, source_target_pairs={{0,5},{1,4},{2,7},{3,6},{4,1},{5,0},{6,3},{7,2},{8,13},{9,12},{10,... | collective-permute-start | bytes 122888 | tf_op jit(solution)/shard_map/ppermute | solution.py:254
  14.2 5.6 %collective-permute-start.5 = (bf16[1,80,256]{2,1,0:T(8,128)(2,1)S(1)}, bf16[1,80,256]{2,1,0:T(8,128)(2,1)S(1)}, u32[]{:S(2)}, u32[]{:S(2)}) collective-permute-start(bf16[1,80,256]{2,1,0:T(8,128)(2,1)S(1)} %get-tuple-element.35), channel_id=1, source_target_pairs={{0,4},{1,5},{2,6},{3,7},{4,0},{5,1},{6,2},{7,3},{8,12},{9,13},{10,... | collective-permute-start | bytes 122888 | tf_op jit(solution)/shard_map/ppermute | solution.py:254
  15.0 5.9 %collective-permute-start.6 = (bf16[1,64,256]{2,1,0:T(8,128)(2,1)S(1)}, bf16[1,64,256]{2,1,0:T(8,128)(2,1)S(1)}, u32[]{:S(2)}, u32[]{:S(2)}) collective-permute-start(bf16[1,64,256]{2,1,0:T(8,128)(2,1)S(1)} %get-tuple-element.36), channel_id=1, source_target_pairs={{0,2},{1,3},{2,4},{3,5},{4,6},{5,7},{6,0},{7,1},{8,10},{9,11},{10,... | collective-permute-start | bytes 98312 | tf_op jit(solution)/shard_map/ppermute | solution.py:320
  16.6 4.3 %collective-permute-start.7 = (bf16[1,64,256]{2,1,0:T(8,128)(2,1)S(1)}, bf16[1,64,256]{2,1,0:T(8,128)(2,1)S(1)}, u32[]{:S(2)}, u32[]{:S(2)}) collective-permute-start(bf16[1,64,256]{2,1,0:T(8,128)(2,1)S(1)} %get-tuple-element.37), channel_id=1, source_target_pairs={{0,6},{1,7},{2,0},{3,1},{4,2},{5,3},{6,4},{7,5},{8,14},{9,15},{10,... | collective-permute-start | bytes 98312 | tf_op jit(solution)/shard_map/ppermute | solution.py:320

commit v7 on v6

--- a/solution.py
+++ b/solution.py
@@ -12,7 +12,6 @@
 KMAX = 32
 PACK = LANES // KMAX
 VMEM_LIMIT = 32 * 2**20
-PAD = 16
 TURNS = (0, 1, 3)
 HBM_SPEC = pl.BlockSpec(memory_space=pltpu.HBM)
 VMEM_SPEC = pl.BlockSpec(memory_space=pltpu.VMEM)
@@ -177,7 +176,7 @@
             block = total[turn(mine, TURNS[k]) * PACK + (1 - side) * half + i]
             swapped[k * half + i] = block.astype(swapped.dtype)
     for target, to_side in ((same, side), (other, 1 - side)):
-        target[:, total.shape[1] :, :] = jnp.zeros_like(target[:, total.shape[1] :, :])
+
         for i in range(half):
             write_block(target, i, total[turn(mine, 2) * PACK + to_side * half + i])
 
@@ -308,7 +307,7 @@
         out_shape=[
             total_shape,
             pltpu.VMEM((3 * PACK // 2, members, LANES), BF16),
-            *[pltpu.VMEM((shards[0], members + PAD, owned), BF16)] * 2,
+            *[pltpu.VMEM(shards, BF16)] * 2,
         ],
         in_specs=[VMEM_SPEC] * 5 + [SMEM_SPEC, VMEM_SPEC],
         out_specs=[VMEM_SPEC] * 4,

time: 21.8 us -> 21.8 us (level)
    ppermute x3, waiting for transfers between devices: 1.34 us -> 1.11 us  [row_swap(): return lax.ppermute(value, 'row', [(i, i ^ offset) for i in range(owners)])]
    ppermute x2, waiting for transfers between devices: 1.11 us -> 1.34 us  [group_send(): lax.ppermute(value, 'row', [(i, (i + by * per_group) % owners) for i in r...]
where the time goes in v7:
time: 21.8 us; the launch traced here: 21.6 us
  starting transfers between devices  11.9 us (55%)
  Pallas kernels  5.87 us (27%)
  waiting for transfers between devices  2.46 us (11%)
  other arithmetic  0.68 us (3%)
  between operations  0.68 us (3%)
    ppermute x3, starting transfers between devices, row_swap(): return lax.ppermute(value, 'row', [(i, i ^ offset) for i in range(owners)])  4.45 us
    pallas_call x1, Pallas kernels, body(): pl.pallas_call(own_kernel, out_shape=[total_shape, *[pltpu.VMEM((n, *w.sh...  3.92 us
    ppermute x2, starting transfers between devices, group_send(): lax.ppermute(value, 'row', [(i, (i + by * per_group) % owners) for i in r...  3.88 us
    ppermute x3, starting transfers between devices, col_swap(): return lax.ppermute(value, 'col', [(i, i ^ offset) for i in range(groups)])  3.58 us
    ppermute x2, waiting for transfers between devices, group_send(): lax.ppermute(value, 'row', [(i, (i + by * per_group) % owners) for i in r...  1.34 us
    pallas_call x1, Pallas kernels, body(): pl.pallas_call(middle_kernel, out_shape=[total_shape, pltpu.VMEM(lowrank_...  1.23 us
    ppermute x3, waiting for transfers between devices, row_swap(): return lax.ppermute(value, 'row', [(i, i ^ offset) for i in range(owners)])  1.11 us
    pallas_call x1, Pallas kernels, body(): pl.pallas_call(last_kernel, out_shape=[total_shape, pltpu.VMEM((3 * PACK...  0.69 us
  transfers between devices with their start and end apart: 8, of which 3 were waited for; matrix products, arithmetic and copies ran while one was open for 0% of the time, Pallas kernels for 24%

profile of v7, /device:TPU:0, one launch (start us, length us, event | category | flops | bytes accessed | tf_op | source)
XLA Modules:
  0.0 21.6 jit_solution(5736121770993931341)
XLA Ops:
  0.6 3.0 %collective-permute-start = (bf16[64,1024]{1,0:T(8,128)(2,1)}, bf16[64,1024]{1,0:T(8,128)(2,1)S(1)}, u32[]{:S(2)}, u32[]{:S(2)}) collective-permute-start(bf16[64,1024]{1,0:T(8,128)(2,1)} %slip_hbm.1), channel_id=1, source_target_pairs={{0,16},{8,24},{16,0},{24,8},{1,17},{9,25},{17,1},{25,9},{2,18},{10... | collective-permute-start | bytes 393224 | tf_op jit(solution)/shard_map/ppermute | solution.py:250
  3.6 0.0 collective-permute-start.2
  3.6 3.9 %shard_map.113 = (f32[16,64,128]{2,1,0:T(8,128)S(1)}, bf16[3,1024,512]{2,1,0:T(8,128)(2,1)S(1)}, bf16[2,16,256,128]{3,2,1,0:T(8,128)(2,1)S(1)}, bf16[3,1024,256]...) custom-call(bf16[64,1024]{1,0:T(8,128)(2,1)} %slip_hbm.1, ...), custom_call_target="tpu_custom_call" | custom-call | flops 167772160 | bytes 10485760 | tf_op jit(solution)/shard_map/pallas_call | solution.py:263
  7.6 0.0 collective-permute-done.across
  7.6 0.6 %collective-permute-start.1 = (bf16[64,1024]{1,0:T(8,128)(2,1)S(1)}, bf16[64,1024]{1,0:T(8,128)(2,1)S(1)}, u32[]{:S(2)}, u32[]{:S(2)}) collective-permute-start(bf16[64,1024]{1,0:T(8,128)(2,1)S(1)} %collective-permute-done.across), channel_id=1, source_target_pairs={{0,8},{8,0},{16,24},{24,16},{1,9},{9,1},{17,25},{25,17},{2,10},{10... | collective-permute-start | bytes 393224 | tf_op jit(solution)/shard_map/ppermute | solution.py:250
  8.2 0.0 collective-permute-done.2.sibling
  8.2 1.2 %shard_map.114 = (f32[16,64,128]{2,1,0:T(8,128)S(1)}, bf16[16,256,128]{2,1,0:T(8,128)(2,1)S(1)}) custom-call(bf16[64,1024]{1,0:T(8,128)(2,1)S(1)} %collective-permute-done.2.sibling, bf16[64,1024]{1,0:T(8,128)(2,1)S(1)} %collective-permute-done.across, bf16[3,1024,512]{2,1,0:T(8,128)(2,1)S(1)} %get-tuple-element.23.u_ref, ...), custom_call_target="tpu_custom_call", output_to_operand_aliasing={{0}: (7, {})} | custom-call | flops 335544320 | bytes 5242880 | tf_op jit(solution)/shard_map/pallas_call | solution.py:294
  9.4 0.0 collective-permute-done.1.beyond
  9.4 0.7 %shard_map.115 = (f32[16,64,128]{2,1,0:T(8,128)S(1)}, bf16[6,64,128]{2,1,0:T(8,128)(2,1)S(1)}, bf16[1,64,256]{2,1,0:T(8,128)(2,1)S(1)}, bf16[1,64,256]{2,1,0:T(8,128)(2,1)S(1)}) custom-call(bf16[64,1024]{1,0:T(8,128)(2,1)S(1)} %collective-permute-done.1.beyond, bf16[3,1024,512]{2,1,0:T(8,128)(2,1)S(1)} %get-tuple-element.23.u_ref, ...), custom_call_target="tpu_custom_call", output_to_operand_aliasing={{0}: (6, {})} | custom-call | flops 167772160 | bytes 2621440 | tf_op jit(solution)/shard_map/pallas_call | solution.py:305
  10.1 1.6 %collective-permute-start.3 = (bf16[6,64,128]{2,1,0:T(8,128)(2,1)S(1)}, bf16[6,64,128]{2,1,0:T(8,128)(2,1)S(1)}, u32[]{:S(2)}, u32[]{:S(2)}) collective-permute-start(bf16[6,64,128]{2,1,0:T(8,128)(2,1)S(1)} %get-tuple-element.32), channel_id=1, source_target_pairs={{0,1},{1,0},{2,3},{3,2},{4,5},{5,4},{6,7},{7,6},{8,9},{9,8},{10,11... | collective-permute-start | bytes 294920 | tf_op jit(solution)/shard_map/ppermute | solution.py:253
  11.7 2.5 %collective-permute-start.4 = (bf16[1,64,256]{2,1,0:T(8,128)(2,1)S(1)}, bf16[1,64,256]{2,1,0:T(8,128)(2,1)S(1)}, u32[]{:S(2)}, u32[]{:S(2)}) collective-permute-start(bf16[1,64,256]{2,1,0:T(8,128)(2,1)S(1)} %get-tuple-element.34), channel_id=1, source_target_pairs={{0,5},{1,4},{2,7},{3,6},{4,1},{5,0},{6,3},{7,2},{8,13},{9,12},{10,... | collective-permute-start | bytes 98312 | tf_op jit(solution)/shard_map/ppermute | solution.py:253
  14.2 0.3 %collective-permute-start.5 = (bf16[1,64,256]{2,1,0:T(8,128)(2,1)S(1)}, bf16[1,64,256]{2,1,0:T(8,128)(2,1)S(1)}, u32[]{:S(2)}, u32[]{:S(2)}) collective-permute-start(bf16[1,64,256]{2,1,0:T(8,128)(2,1)S(1)} %get-tuple-element.35), channel_id=1, source_target_pairs={{0,4},{1,5},{2,6},{3,7},{4,0},{5,1},{6,2},{7,3},{8,12},{9,13},{10,... | collective-permute-start | bytes 98312 | tf_op jit(solution)/shard_map/ppermute | solution.py:253
  14.6 0.4 %collective-permute-done.3.received = bf16[6,64,128]{2,1,0:T(8,128)(2,1)S(1)} collective-permute-done((bf16[6,64,128]{2,1,0:T(8,128)(2,1)S(1)}, bf16[6,64,128]{2,1,0:T(8,128)(2,1)S(1)}, u32[]{:S(2)}, u32[]{:S(2)}) %collective-permute-start.3) | collective-permute-done | bytes 98336 | tf_op jit(solution)/shard_map/ppermute | solution.py:253
  15.0 1.6 %collective-permute-start.6 = (bf16[1,64,256]{2,1,0:T(8,128)(2,1)S(1)}, bf16[1,64,256]{2,1,0:T(8,128)(2,1)S(1)}, u32[]{:S(2)}, u32[]{:S(2)}) collective-permute-start(bf16[1,64,256]{2,1,0:T(8,128)(2,1)S(1)} %get-tuple-element.36), channel_id=1, source_target_pairs={{0,2},{1,3},{2,4},{3,5},{4,6},{5,7},{6,0},{7,1},{8,10},{9,11},{10,... | collective-permute-start | bytes 98312 | tf_op jit(solution)/shard_map/ppermute | solution.py:319
  16.6 2.2 %collective-permute-start.7 = (bf16[1,64,256]{2,1,0:T(8,128)(2,1)S(1)}, bf16[1,64,256]{2,1,0:T(8,128)(2,1)S(1)}, u32[]{:S(2)}, u32[]{:S(2)}) collective-permute-start(bf16[1,64,256]{2,1,0:T(8,128)(2,1)S(1)} %get-tuple-element.37), channel_id=1, source_target_pairs={{0,6},{1,7},{2,0},{3,1},{4,2},{5,3},{6,4},{7,5},{8,14},{9,15},{10,... | collective-permute-start | bytes 98312 | tf_op jit(solution)/shard_map/ppermute | solution.py:319
  18.9 0.0 collective-permute-done.4
  18.9 0.7 %collective-permute-done.5 = bf16[1,64,256]{2,1,0:T(8,128)(2,1)S(1)} collective-permute-done((bf16[1,64,256]{2,1,0:T(8,128)(2,1)S(1)}, bf16[1,64,256]{2,1,0:T(8,128)(2,1)S(1)}, u32[]{:S(2)}, u32[]{:S(2)}) %collective-permute-start.5) | collective-permute-done | bytes 32800 | tf_op jit(solution)/shard_map/ppermute | solution.py:253
  19.6 1.3 %collective-permute-done.6 = bf16[1,64,256]{2,1,0:T(8,128)(2,1)S(1)} collective-permute-done((bf16[1,64,256]{2,1,0:T(8,128)(2,1)S(1)}, bf16[1,64,256]{2,1,0:T(8,128)(2,1)S(1)}, u32[]{:S(2)}, u32[]{:S(2)}) %collective-permute-start.6) | collective-permute-done | bytes 32800 | tf_op jit(solution)/shard_map/ppermute | solution.py:319
  20.9 0.0 collective-permute-done.7
  20.9 0.7 %multiply_add_fusion = (f32[64,256]{1,0:T(8,128)}, f32[64,256]{1,0:T(8,128)}) fusion(f32[64,256]{1,0:T(8,128)S(1)} %get-tuple-element.39, f32[64,256]{1,0:T(8,128)S(1)} %get-tuple-element.38, bf16[1,64,256]{2,1,0:T(8,128)(2,1)S(1)} %collective-permute-done.7, bf16[1,64,256]{2,1,0:T(8,128)(2,1)S(1)} %collective-permute-done.6, ...), kind=kLoop, calls=%fused_computation.1 | loop fusion | flops 163840 | bytes 458752 | tf_op jit(solution)/shard_map/add | solution.py:345
  (1 shorter events, 0.0 us)
Async XLA Ops:
  0.6 6.9 %collective-permute-start = (bf16[64,1024]{1,0:T(8,128)(2,1)}, bf16[64,1024]{1,0:T(8,128)(2,1)S(1)}, u32[]{:S(2)}, u32[]{:S(2)}) collective-permute-start(bf16[64,1024]{1,0:T(8,128)(2,1)} %slip_hbm.1), channel_id=1, source_target_pairs={{0,16},{8,24},{16,0},{24,8},{1,17},{9,25},{17,1},{25,9},{2,18},{10... | collective-permute-start | bytes 393224 | tf_op jit(solution)/shard_map/ppermute | solution.py:250
  3.6 4.5 %collective-permute-start.2 = (bf16[64,1024]{1,0:T(8,128)(2,1)}, bf16[64,1024]{1,0:T(8,128)(2,1)S(1)}, u32[]{:S(2)}, u32[]{:S(2)}) collective-permute-start(bf16[64,1024]{1,0:T(8,128)(2,1)} %slip_hbm.1), channel_id=1, source_target_pairs={{0,8},{8,0},{16,24},{24,16},{1,9},{9,1},{17,25},{25,17},{2,10},{10... | collective-permute-start | bytes 393224 | tf_op jit(solution)/shard_map/ppermute | solution.py:250
  7.6 1.8 %collective-permute-start.1 = (bf16[64,1024]{1,0:T(8,128)(2,1)S(1)}, bf16[64,1024]{1,0:T(8,128)(2,1)S(1)}, u32[]{:S(2)}, u32[]{:S(2)}) collective-permute-start(bf16[64,1024]{1,0:T(8,128)(2,1)S(1)} %collective-permute-done.across), channel_id=1, source_target_pairs={{0,8},{8,0},{16,24},{24,16},{1,9},{9,1},{17,25},{25,17},{2,10},{10... | collective-permute-start | bytes 393224 | tf_op jit(solution)/shard_map/ppermute | solution.py:250
  10.1 4.9 %collective-permute-start.3 = (bf16[6,64,128]{2,1,0:T(8,128)(2,1)S(1)}, bf16[6,64,128]{2,1,0:T(8,128)(2,1)S(1)}, u32[]{:S(2)}, u32[]{:S(2)}) collective-permute-start(bf16[6,64,128]{2,1,0:T(8,128)(2,1)S(1)} %get-tuple-element.32), channel_id=1, source_target_pairs={{0,1},{1,0},{2,3},{3,2},{4,5},{5,4},{6,7},{7,6},{8,9},{9,8},{10,11... | collective-permute-start | bytes 294920 | tf_op jit(solution)/shard_map/ppermute | solution.py:253
  11.7 7.2 %collective-permute-start.4 = (bf16[1,64,256]{2,1,0:T(8,128)(2,1)S(1)}, bf16[1,64,256]{2,1,0:T(8,128)(2,1)S(1)}, u32[]{:S(2)}, u32[]{:S(2)}) collective-permute-start(bf16[1,64,256]{2,1,0:T(8,128)(2,1)S(1)} %get-tuple-element.34), channel_id=1, source_target_pairs={{0,5},{1,4},{2,7},{3,6},{4,1},{5,0},{6,3},{7,2},{8,13},{9,12},{10,... | collective-permute-start | bytes 98312 | tf_op jit(solution)/shard_map/ppermute | solution.py:253
  14.2 5.4 %collective-permute-start.5 = (bf16[1,64,256]{2,1,0:T(8,128)(2,1)S(1)}, bf16[1,64,256]{2,1,0:T(8,128)(2,1)S(1)}, u32[]{:S(2)}, u32[]{:S(2)}) collective-permute-start(bf16[1,64,256]{2,1,0:T(8,128)(2,1)S(1)} %get-tuple-element.35), channel_id=1, source_target_pairs={{0,4},{1,5},{2,6},{3,7},{4,0},{5,1},{6,2},{7,3},{8,12},{9,13},{10,... | collective-permute-start | bytes 98312 | tf_op jit(solution)/shard_map/ppermute | solution.py:253
  15.0 5.9 %collective-permute-start.6 = (bf16[1,64,256]{2,1,0:T(8,128)(2,1)S(1)}, bf16[1,64,256]{2,1,0:T(8,128)(2,1)S(1)}, u32[]{:S(2)}, u32[]{:S(2)}) collective-permute-start(bf16[1,64,256]{2,1,0:T(8,128)(2,1)S(1)} %get-tuple-element.36), channel_id=1, source_target_pairs={{0,2},{1,3},{2,4},{3,5},{4,6},{5,7},{6,0},{7,1},{8,10},{9,11},{10,... | collective-permute-start | bytes 98312 | tf_op jit(solution)/shard_map/ppermute | solution.py:319
  16.6 4.3 %collective-permute-start.7 = (bf16[1,64,256]{2,1,0:T(8,128)(2,1)S(1)}, bf16[1,64,256]{2,1,0:T(8,128)(2,1)S(1)}, u32[]{:S(2)}, u32[]{:S(2)}) collective-permute-start(bf16[1,64,256]{2,1,0:T(8,128)(2,1)S(1)} %get-tuple-element.37), channel_id=1, source_target_pairs={{0,6},{1,7},{2,0},{3,1},{4,2},{5,3},{6,4},{7,5},{8,14},{9,15},{10,... | collective-permute-start | bytes 98312 | tf_op jit(solution)/shard_map/ppermute | solution.py:319

commit v8 on v7

--- a/solution.py
+++ b/solution.py
@@ -12,7 +12,6 @@
 KMAX = 32
 PACK = LANES // KMAX
 VMEM_LIMIT = 32 * 2**20
-TURNS = (0, 1, 3)
 HBM_SPEC = pl.BlockSpec(memory_space=pltpu.HBM)
 VMEM_SPEC = pl.BlockSpec(memory_space=pltpu.VMEM)
 SMEM_SPEC = pl.BlockSpec(memory_space=pltpu.SMEM)
@@ -62,15 +61,30 @@
 
 
 class Fetches:
-    def __init__(self, sems):
-        self.sems, self.used = sems, 3
+    def __init__(self, sems, used):
+        self.sems, self.used = sems, used
+
+    def plan(self, source, target, shared=None):
+        own = self.used if shared is None else shared
+        self.used += shared is None
+        return pltpu.make_async_copy(source, target, self.sems.at[own])
 
     def __call__(self, source, target, shared=None):
-        own = self.used if shared is None else shared
-        copy = pltpu.make_async_copy(source, target, self.sems.at[own])
-        self.used += shared is None
+        copy = self.plan(source, target, shared)
         copy.start()
         return copy
+
+
+def last_copies(me, fetch, u_hbm, near_hbm, u_last, near_last):
+    return [
+        fetch.plan(u_hbm.at[me ^ 3], u_last),
+        fetch.plan(near_hbm.at[me ^ 3], near_last),
+    ]
+
+
+def start_all(copies):
+    for copy in copies:
+        copy.start()
 
 
 def wait_all(copies):
@@ -80,11 +94,11 @@
 
 def own_kernel(
     slip_hbm, u_hbm, v_hbm, near_hbm, ranks_hbm, slots_hbm, velocity_hbm, theta_hbm, a_hbm, b_hbm,
-    total, u_out, v_out, near_out, kept, gain, shift, slots,
+    total, u_out, v_out, near_out, u_last, near_last, kept, gain, shift, slots,
     slip, u_in, v_in, near_in, ranks, velocity, theta, a_sigma, b_sigma, coeffs, sems,
 ):
     me = lax.axis_index("col")
-    fetch = Fetches(sems)
+    fetch = Fetches(sems, 3)
     small = [fetch(ranks_hbm, ranks), fetch(slots_hbm, slots)]
     mine = [
         fetch(slip_hbm, slip),
@@ -98,16 +112,17 @@
         fetch(a_hbm, a_sigma),
         fetch(b_hbm, b_sigma),
     ]
-    for i in range(3):
+    for i in range(2):
         s = me ^ (1 + i)
         fetch(u_hbm.at[s], u_out.at[i], 0)
         fetch(near_hbm.at[s], near_out.at[i], 1)
-        if i < 2:
-            fetch(v_hbm.at[s], v_out.at[i], 2)
+        fetch(v_hbm.at[s], v_out.at[i], 2)
     later = [
         pltpu.make_async_copy(whole, whole, sems.at[n])
         for n, whole in enumerate((u_out, near_out, v_out))
     ]
+    last = last_copies(me, fetch, u_hbm, near_hbm, u_last, near_last)
+    pl.when(me % 2 == 0)(lambda: start_all(last))
     @pl.when(me >= 0)
     def _():
         wait_all(small)
@@ -138,14 +153,18 @@
         shift[...] = -(b_sigma[...] * (1.0 - rate * state) / state) * divisor
         wait_all(later)
 
+    pl.when(me % 2 == 0)(lambda: wait_all(last))
+
 
 def middle_kernel(
-    sibling, across, u_ref, v_ref, near_ref, kept, slots, start, v_hbm, total, v_last,
-    coeffs, sem,
+    sibling, across, u_ref, v_ref, near_ref, kept, slots, start, u_start, near_start,
+    u_hbm, v_hbm, near_hbm, total, u_last, near_last, v_last, coeffs, sems,
 ):
     me = lax.axis_index("col")
-    copy = pltpu.make_async_copy(v_hbm.at[me ^ 3], v_last, sem)
-    copy.start()
+    fetch = Fetches(sems, 0)
+    copy = fetch(v_hbm.at[me ^ 3], v_last)
+    last = last_copies(me, fetch, u_hbm, near_hbm, u_last, near_last)
+    pl.when(me % 2 != 0)(lambda: start_all(last))
 
     @pl.when(me >= 0)
     def _():
@@ -160,25 +179,40 @@
             )
 
     copy.wait()
+    pl.when(me % 2 != 0)(lambda: wait_all(last))
 
 
 def last_kernel(
     beyond, u_ref, v_ref, near_ref, kept, slots, start, total, swapped, same, other, coeffs
 ):
     me = lax.axis_index("col")
-    project(beyond[...], u_ref.at[2], kept.at[3], coeffs)
-    add_near(beyond[...], near_ref.at[2], slots, me ^ 3, total)
+    project(beyond[...], u_ref, kept.at[3], coeffs)
+    add_near(beyond[...], near_ref, slots, me ^ 3, total)
     for j in range(total.shape[0]):
         total[j] += far_block(coeffs, v_ref, j)
+    half = PACK // 2
+    swap, direct, _ = routes(total)
+    for k, first in enumerate(swap):
+        for i in range(half):
+            swapped[k * half + i] = total[first + i].astype(swapped.dtype)
+    for target, first in zip((other, same), direct):
+        for i in range(half):
+            write_block(target, i, total[first + i])
+
+
+def routes(total):
+    even = lax.axis_index("col") % 2 == 0
     mine, side, half = row_place(total)
-    for k in range(3):
-        for i in range(half):
-            block = total[turn(mine, TURNS[k]) * PACK + (1 - side) * half + i]
-            swapped[k * half + i] = block.astype(swapped.dtype)
-    for target, to_side in ((same, side), (other, 1 - side)):
-
-        for i in range(half):
-            write_block(target, i, total[turn(mine, 2) * PACK + to_side * half + i])
+
+    def at(by, there, bits, other):
+        group = jnp.where(even, turn(mine, by), mine ^ bits)
+        return group * PACK + jnp.where(even, there, other) * half
+
+    far = 1 - side
+    swap = [at(0, far, 1, side), at(1, far, 1, far), at(3, far, 3, side)]
+    direct = [at(2, far, 3, far), at(2, side, 2, far)]
+    join = [at(0, side, 0, side), at(1, side, 0, far), at(3, side, 2, side)]
+    return swap, direct, join
 
 
 def turn(group, by):
@@ -202,11 +236,11 @@
 
 
 def join_kernel(total, received, *outs):
-    mine, side, half = row_place(total)
-    for k, target in enumerate(outs):
+    half = PACK // 2
+    _, _, join = routes(total)
+    for k, (target, first) in enumerate(zip(outs, join)):
         for i in range(half):
-            block = total[turn(mine, TURNS[k]) * PACK + side * half + i] + received[k * half + i].astype(F32)
-            write_block(target, i, block)
+            write_block(target, i, total[first + i] + received[k * half + i].astype(F32))
 
 
 def halve_kernel(place, kept, *refs):
@@ -257,24 +291,26 @@
 
     weights = (lowrank_u, lowrank_v, near_blocks)
     field = pltpu.VMEM(velocity.shape, F32)
+    last_shapes = [pltpu.VMEM(w.shape[1:], BF16) for w in (lowrank_u, near_blocks)]
     coeffs = pltpu.VMEM((receivers, members, depth), BF16)
     total_shape = pltpu.VMEM((receivers, members, LANES), F32)
     slots_smem = pltpu.SMEM(slots_by.shape, I32)
-    total, u_later, v_later, near_later, kept, gain, shift, slots = pl.pallas_call(
+    total, u_later, v_later, near_later, u_last, near_last, kept, gain, shift, slots = pl.pallas_call(
         own_kernel,
         out_shape=[
             total_shape,
-            *[pltpu.VMEM((n, *w.shape[1:]), BF16) for n, w in zip((3, 2, 3), weights)],
+            *[pltpu.VMEM((2, *w.shape[1:]), BF16) for w in weights],
+            *last_shapes,
             pltpu.VMEM((groups, count, receivers * KMAX), F32), field, field, slots_smem,
         ],
         in_specs=[HBM_SPEC] * 10,
-        out_specs=[VMEM_SPEC] * 7 + [SMEM_SPEC],
+        out_specs=[VMEM_SPEC] * 9 + [SMEM_SPEC],
         scratch_shapes=[
             pltpu.VMEM(slip.shape, BF16),
             *[pltpu.VMEM(w.shape[1:], BF16) for w in weights],
             pltpu.VMEM(ranks.shape, I32), field, field,
             pltpu.VMEM((1, owned), F32), pltpu.VMEM((1, owned), F32),
-            coeffs, pltpu.SemaphoreType.DMA((13,)),
+            coeffs, pltpu.SemaphoreType.DMA((15,)),
         ],
         **params(2 * members * size, 8 * size),
     )(
@@ -291,17 +327,20 @@
     shards = (per_group // 2, members, owned)
 
     beyond = col_swap(across, 1)
-    total, v_last = pl.pallas_call(
+    total, u_last, near_last, v_last = pl.pallas_call(
         middle_kernel,
-        out_shape=[total_shape, pltpu.VMEM(lowrank_v.shape[1:], BF16)],
-        in_specs=[VMEM_SPEC] * 6 + [SMEM_SPEC, VMEM_SPEC, HBM_SPEC],
-        out_specs=[VMEM_SPEC] * 2,
+        out_shape=[total_shape, *last_shapes, pltpu.VMEM(lowrank_v.shape[1:], BF16)],
+        in_specs=[VMEM_SPEC] * 6 + [SMEM_SPEC] + [VMEM_SPEC] * 3 + [HBM_SPEC] * 3,
+        out_specs=[VMEM_SPEC] * 4,
         scratch_shapes=[
-            pltpu.VMEM((2, receivers, members, depth), BF16), pltpu.SemaphoreType.DMA
+            pltpu.VMEM((2, receivers, members, depth), BF16), pltpu.SemaphoreType.DMA((3,))
         ],
-        input_output_aliases={7: 0},
+        input_output_aliases={7: 0, 8: 1, 9: 2},
         **params(4 * members * size, 4 * size),
-    )(sibling, across, u_later, v_later, near_later, kept, slots, total, in_hbm(lowrank_v))
+    )(
+        sibling, across, u_later, v_later, near_later, kept, slots, total, u_last, near_last,
+        *map(in_hbm, weights),
+    )
     total, swapped, same, other = pl.pallas_call(
         last_kernel,
         out_shape=[
@@ -314,13 +353,20 @@
         scratch_shapes=[coeffs],
         input_output_aliases={6: 0},
         **params(2 * members * size, 2 * size),
-    )(beyond, u_later, v_last, near_later, kept, slots, total)
-    def group_send(value, by):
-        return lax.ppermute(value, "row", [(i, (i + by * per_group) % owners) for i in range(owners)])
-
-    swapped = row_swap(swapped, per_group // 2)
-    other = row_swap(other, owners // 2 + per_group // 2)
-    same = row_swap(same, owners // 2)
+    )(beyond, u_last, v_last, near_last, kept, slots, total)
+    def send(value, by, bits, halves):
+        pairs = []
+        for i in range(groups * owners):
+            col, row = divmod(i, owners)
+            group, place = divmod(row, per_group)
+            group = group ^ bits if col % 2 else (group + by) % n_groups
+            place ^= per_group // 2 if halves[col % 2] else 0
+            pairs.append((i, (col * n_groups + group) * per_group + place))
+        return lax.ppermute(value, ("col", "row"), pairs)
+
+    swapped = send(swapped, 0, 1, (True, False))
+    other = send(other, 2, 3, (True, True))
+    same = send(same, 2, 2, (False, True))
     own, first, second = pl.pallas_call(
         join_kernel,
         out_shape=[pltpu.VMEM(shards, dtype) for dtype in (F32, BF16, BF16)],
@@ -328,7 +374,9 @@
         out_specs=[VMEM_SPEC] * 3,
         **params(0, 8 * swapped.size),
     )(total, swapped)
-    received = [other, same, group_send(first, 1), group_send(second, 3)]
+    received = [
+        other, same, send(first, 1, 0, (False, True)), send(second, 3, 2, (False, False))
+    ]
     for place in reversed(range(per_group.bit_length() - 2)):
         shape = (own.shape[0] // 2, members, owned)
         sent, own = pl.pallas_call(

time: 21.8 us -> 21.6 us (level)
  starting transfers between devices: 11.9 us -> 11.5 us
    ppermute x3, starting transfers between devices: 3.58 us -> 3.17 us  [col_swap(): return lax.ppermute(value, 'col', [(i, i ^ offset) for i in range(groups)])]
  transfers between devices with their start and end apart: 8 -> 8, of which waited for: 3 -> 4; matrix products, arithmetic and copies ran while one was open for 0% -> 0% of each run, Pallas kernels for 24% -> 24%
where the time goes in v8:
time: 21.6 us; the launch traced here: 21.4 us
  starting transfers between devices  11.5 us (53%)
  Pallas kernels  5.9 us (27%)
  waiting for transfers between devices  2.63 us (12%)
  between operations  0.68 us (3%)
  other arithmetic  0.67 us (3%)
    ppermute x5, starting transfers between devices, send(): return lax.ppermute(value, ('col', 'row'), pairs)  8.33 us
    pallas_call x1, Pallas kernels, body(): pl.pallas_call(own_kernel, out_shape=[total_shape, *[pltpu.VMEM((2, *w.sh...  3.93 us
    ppermute x3, starting transfers between devices, col_swap(): return lax.ppermute(value, 'col', [(i, i ^ offset) for i in range(groups)])  3.17 us
    ppermute x5, waiting for transfers between devices, send(): return lax.ppermute(value, ('col', 'row'), pairs)  2.62 us
    pallas_call x1, Pallas kernels, body(): pl.pallas_call(middle_kernel, out_shape=[total_shape, *last_shapes, pltpu...  1.25 us
    pallas_call x1, Pallas kernels, body(): pl.pallas_call(last_kernel, out_shape=[total_shape, pltpu.VMEM((3 * PACK...  0.7 us
    add x1, other arithmetic, body(): return (stress_rate, stress_rate * gain + shift)  0.67 us
  transfers between devices with their start and end apart: 8, of which 4 were waited for; matrix products, arithmetic and copies ran while one was open for 0% of the time, Pallas kernels for 24%

profile of v8, /device:TPU:0, one launch (start us, length us, event | category | flops | bytes accessed | tf_op | source)
XLA Modules:
  0.0 21.4 jit_solution(11376666192200895508)
XLA Ops:
  0.6 3.0 %collective-permute-start = (bf16[64,1024]{1,0:T(8,128)(2,1)}, bf16[64,1024]{1,0:T(8,128)(2,1)S(1)}, u32[]{:S(2)}, u32[]{:S(2)}) collective-permute-start(bf16[64,1024]{1,0:T(8,128)(2,1)} %slip_hbm.1), channel_id=1, source_target_pairs={{0,16},{8,24},{16,0},{24,8},{1,17},{9,25},{17,1},{25,9},{2,18},{10... | collective-permute-start | bytes 393224 | tf_op jit(solution)/shard_map/ppermute | solution.py:284
  3.6 0.0 collective-permute-start.2
  3.6 3.9 %shard_map.113 = (f32[16,64,128]{2,1,0:T(8,128)S(1)}, bf16[2,1024,512]{2,1,0:T(8,128)(2,1)S(1)}, bf16[2,16,256,128]{3,2,1,0:T(8,128)(2,1)S(1)}, bf16[2,1024,256]...) custom-call(bf16[64,1024]{1,0:T(8,128)(2,1)} %slip_hbm.1, ...), custom_call_target="tpu_custom_call" | custom-call | flops 167772160 | bytes 10485760 | tf_op jit(solution)/shard_map/pallas_call | solution.py:298
  7.6 0.0 collective-permute-done.across
  7.6 0.2 collective-permute-start.1
  7.8 0.0 collective-permute-done.2.sibling
  7.8 1.3 %shard_map.114 = (f32[16,64,128]{2,1,0:T(8,128)S(1)}, bf16[1024,512]{1,0:T(8,128)(2,1)S(1)}, bf16[1024,256]{1,0:T(8,128)(2,1)S(1)}, bf16[16,256,128]{2,1,0:T(8,128)(2,1)S(1)}) custom-call(bf16[64,1024]{1,0:T(8,128)(2,1)S(1)} %collective-permute-done.2.sibling, ...), custom_call_target="tpu_custom_call", output_to_operand_aliasing={{0}: (7, {}), {1}: (8, {}), {2}: (9, {})} | custom-call | flops 335544320 | bytes 5242880 | tf_op jit(solution)/shard_map/pallas_call | solution.py:330
  9.0 0.0 collective-permute-done.1.beyond
  9.0 0.7 %shard_map.115 = (f32[16,64,128]{2,1,0:T(8,128)S(1)}, bf16[6,64,128]{2,1,0:T(8,128)(2,1)S(1)}, bf16[1,64,256]{2,1,0:T(8,128)(2,1)S(1)}, bf16[1,64,256]{2,1,0:T(8,128)(2,1)S(1)}) custom-call(bf16[64,1024]{1,0:T(8,128)(2,1)S(1)} %collective-permute-done.1.beyond, bf16[1024,512]{1,0:T(8,128)(2,1)S(1)} %get-tuple-element.35.u_ref, ...), custom_call_target="tpu_custom_call", output_to_operand_aliasing={{0}: (6, {})} | custom-call | flops 167772160 | bytes 2621440 | tf_op jit(solution)/shard_map/pallas_call | solution.py:344
  9.7 1.6 %collective-permute-start.3 = (bf16[6,64,128]{2,1,0:T(8,128)(2,1)S(1)}, bf16[6,64,128]{2,1,0:T(8,128)(2,1)S(1)}, u32[]{:S(2)}, u32[]{:S(2)}) collective-permute-start(bf16[6,64,128]{2,1,0:T(8,128)(2,1)S(1)} %get-tuple-element.40), channel_id=1, source_target_pairs={{0,1},{1,0},{2,3},{3,2},{4,5},{5,4},{6,7},{7,6},{8,10},{9,11},{10,... | collective-permute-start | bytes 294920 | tf_op jit(solution)/shard_map/ppermute | solution.py:365
  11.3 2.5 %collective-permute-start.4 = (bf16[1,64,256]{2,1,0:T(8,128)(2,1)S(1)}, bf16[1,64,256]{2,1,0:T(8,128)(2,1)S(1)}, u32[]{:S(2)}, u32[]{:S(2)}) collective-permute-start(bf16[1,64,256]{2,1,0:T(8,128)(2,1)S(1)} %get-tuple-element.42), channel_id=1, source_target_pairs={{0,5},{1,4},{2,7},{3,6},{4,1},{5,0},{6,3},{7,2},{8,15},{9,14},{10,... | collective-permute-start | bytes 98312 | tf_op jit(solution)/shard_map/ppermute | solution.py:365
  13.9 0.3 %collective-permute-start.5 = (bf16[1,64,256]{2,1,0:T(8,128)(2,1)S(1)}, bf16[1,64,256]{2,1,0:T(8,128)(2,1)S(1)}, u32[]{:S(2)}, u32[]{:S(2)}) collective-permute-start(bf16[1,64,256]{2,1,0:T(8,128)(2,1)S(1)} %get-tuple-element.43), channel_id=1, source_target_pairs={{0,4},{1,5},{2,6},{3,7},{4,0},{5,1},{6,2},{7,3},{8,13},{9,12},{10,... | collective-permute-start | bytes 98312 | tf_op jit(solution)/shard_map/ppermute | solution.py:365
  14.2 0.2 %collective-permute-done.3.received = bf16[6,64,128]{2,1,0:T(8,128)(2,1)S(1)} collective-permute-done((bf16[6,64,128]{2,1,0:T(8,128)(2,1)S(1)}, bf16[6,64,128]{2,1,0:T(8,128)(2,1)S(1)}, u32[]{:S(2)}, u32[]{:S(2)}) %collective-permute-start.3) | collective-permute-done | bytes 98336 | tf_op jit(solution)/shard_map/ppermute | solution.py:365
  14.4 1.6 %collective-permute-start.6 = (bf16[1,64,256]{2,1,0:T(8,128)(2,1)S(1)}, bf16[1,64,256]{2,1,0:T(8,128)(2,1)S(1)}, u32[]{:S(2)}, u32[]{:S(2)}) collective-permute-start(bf16[1,64,256]{2,1,0:T(8,128)(2,1)S(1)} %get-tuple-element.44), channel_id=1, source_target_pairs={{0,2},{1,3},{2,4},{3,5},{4,6},{5,7},{6,0},{7,1},{8,9},{9,8},{10,11... | collective-permute-start | bytes 98312 | tf_op jit(solution)/shard_map/ppermute | solution.py:365
  16.1 2.2 %collective-permute-start.7 = (bf16[1,64,256]{2,1,0:T(8,128)(2,1)S(1)}, bf16[1,64,256]{2,1,0:T(8,128)(2,1)S(1)}, u32[]{:S(2)}, u32[]{:S(2)}) collective-permute-start(bf16[1,64,256]{2,1,0:T(8,128)(2,1)S(1)} %get-tuple-element.45), channel_id=1, source_target_pairs={{0,6},{1,7},{2,0},{3,1},{4,2},{5,3},{6,4},{7,5},{8,12},{9,13},{10,... | collective-permute-start | bytes 98312 | tf_op jit(solution)/shard_map/ppermute | solution.py:365
  18.3 0.0 collective-permute-done.4
  18.3 0.8 %collective-permute-done.5 = bf16[1,64,256]{2,1,0:T(8,128)(2,1)S(1)} collective-permute-done((bf16[1,64,256]{2,1,0:T(8,128)(2,1)S(1)}, bf16[1,64,256]{2,1,0:T(8,128)(2,1)S(1)}, u32[]{:S(2)}, u32[]{:S(2)}) %collective-permute-start.5) | collective-permute-done | bytes 32800 | tf_op jit(solution)/shard_map/ppermute | solution.py:365
  19.1 1.1 %collective-permute-done.6 = bf16[1,64,256]{2,1,0:T(8,128)(2,1)S(1)} collective-permute-done((bf16[1,64,256]{2,1,0:T(8,128)(2,1)S(1)}, bf16[1,64,256]{2,1,0:T(8,128)(2,1)S(1)}, u32[]{:S(2)}, u32[]{:S(2)}) %collective-permute-start.6) | collective-permute-done | bytes 32800 | tf_op jit(solution)/shard_map/ppermute | solution.py:365
  20.3 0.5 %collective-permute-done.7 = bf16[1,64,256]{2,1,0:T(8,128)(2,1)S(1)} collective-permute-done((bf16[1,64,256]{2,1,0:T(8,128)(2,1)S(1)}, bf16[1,64,256]{2,1,0:T(8,128)(2,1)S(1)}, u32[]{:S(2)}, u32[]{:S(2)}) %collective-permute-start.7) | collective-permute-done | bytes 32800 | tf_op jit(solution)/shard_map/ppermute | solution.py:365
  20.7 0.7 %multiply_add_fusion = (f32[64,256]{1,0:T(8,128)}, f32[64,256]{1,0:T(8,128)}) fusion(f32[64,256]{1,0:T(8,128)S(1)} %get-tuple-element.47, f32[64,256]{1,0:T(8,128)S(1)} %get-tuple-element.46, bf16[1,64,256]{2,1,0:T(8,128)(2,1)S(1)} %collective-permute-done.7, bf16[1,64,256]{2,1,0:T(8,128)(2,1)S(1)} %collective-permute-done.6, ...), kind=kLoop, calls=%fused_computation.1 | loop fusion | flops 163840 | bytes 458752 | tf_op jit(solution)/shard_map/add | solution.py:393
  (1 shorter events, 0.0 us)
Async XLA Ops:
  0.6 7.0 %collective-permute-start = (bf16[64,1024]{1,0:T(8,128)(2,1)}, bf16[64,1024]{1,0:T(8,128)(2,1)S(1)}, u32[]{:S(2)}, u32[]{:S(2)}) collective-permute-start(bf16[64,1024]{1,0:T(8,128)(2,1)} %slip_hbm.1), channel_id=1, source_target_pairs={{0,16},{8,24},{16,0},{24,8},{1,17},{9,25},{17,1},{25,9},{2,18},{10... | collective-permute-start | bytes 393224 | tf_op jit(solution)/shard_map/ppermute | solution.py:284
  3.6 4.1 %collective-permute-start.2 = (bf16[64,1024]{1,0:T(8,128)(2,1)}, bf16[64,1024]{1,0:T(8,128)(2,1)S(1)}, u32[]{:S(2)}, u32[]{:S(2)}) collective-permute-start(bf16[64,1024]{1,0:T(8,128)(2,1)} %slip_hbm.1), channel_id=1, source_target_pairs={{0,8},{8,0},{16,24},{24,16},{1,9},{9,1},{17,25},{25,17},{2,10},{10... | collective-permute-start | bytes 393224 | tf_op jit(solution)/shard_map/ppermute | solution.py:284
  7.6 1.4 %collective-permute-start.1 = (bf16[64,1024]{1,0:T(8,128)(2,1)S(1)}, bf16[64,1024]{1,0:T(8,128)(2,1)S(1)}, u32[]{:S(2)}, u32[]{:S(2)}) collective-permute-start(bf16[64,1024]{1,0:T(8,128)(2,1)S(1)} %collective-permute-done.across), channel_id=1, source_target_pairs={{0,8},{8,0},{16,24},{24,16},{1,9},{9,1},{17,25},{25,17},{2,10},{10... | collective-permute-start | bytes 393224 | tf_op jit(solution)/shard_map/ppermute | solution.py:284
  9.7 4.7 %collective-permute-start.3 = (bf16[6,64,128]{2,1,0:T(8,128)(2,1)S(1)}, bf16[6,64,128]{2,1,0:T(8,128)(2,1)S(1)}, u32[]{:S(2)}, u32[]{:S(2)}) collective-permute-start(bf16[6,64,128]{2,1,0:T(8,128)(2,1)S(1)} %get-tuple-element.40), channel_id=1, source_target_pairs={{0,1},{1,0},{2,3},{3,2},{4,5},{5,4},{6,7},{7,6},{8,10},{9,11},{10,... | collective-permute-start | bytes 294920 | tf_op jit(solution)/shard_map/ppermute | solution.py:365
  11.3 7.0 %collective-permute-start.4 = (bf16[1,64,256]{2,1,0:T(8,128)(2,1)S(1)}, bf16[1,64,256]{2,1,0:T(8,128)(2,1)S(1)}, u32[]{:S(2)}, u32[]{:S(2)}) collective-permute-start(bf16[1,64,256]{2,1,0:T(8,128)(2,1)S(1)} %get-tuple-element.42), channel_id=1, source_target_pairs={{0,5},{1,4},{2,7},{3,6},{4,1},{5,0},{6,3},{7,2},{8,15},{9,14},{10,... | collective-permute-start | bytes 98312 | tf_op jit(solution)/shard_map/ppermute | solution.py:365
  13.9 5.3 %collective-permute-start.5 = (bf16[1,64,256]{2,1,0:T(8,128)(2,1)S(1)}, bf16[1,64,256]{2,1,0:T(8,128)(2,1)S(1)}, u32[]{:S(2)}, u32[]{:S(2)}) collective-permute-start(bf16[1,64,256]{2,1,0:T(8,128)(2,1)S(1)} %get-tuple-element.43), channel_id=1, source_target_pairs={{0,4},{1,5},{2,6},{3,7},{4,0},{5,1},{6,2},{7,3},{8,13},{9,12},{10,... | collective-permute-start | bytes 98312 | tf_op jit(solution)/shard_map/ppermute | solution.py:365
  14.4 5.8 %collective-permute-start.6 = (bf16[1,64,256]{2,1,0:T(8,128)(2,1)S(1)}, bf16[1,64,256]{2,1,0:T(8,128)(2,1)S(1)}, u32[]{:S(2)}, u32[]{:S(2)}) collective-permute-start(bf16[1,64,256]{2,1,0:T(8,128)(2,1)S(1)} %get-tuple-element.44), channel_id=1, source_target_pairs={{0,2},{1,3},{2,4},{3,5},{4,6},{5,7},{6,0},{7,1},{8,9},{9,8},{10,11... | collective-permute-start | bytes 98312 | tf_op jit(solution)/shard_map/ppermute | solution.py:365
  16.1 4.6 %collective-permute-start.7 = (bf16[1,64,256]{2,1,0:T(8,128)(2,1)S(1)}, bf16[1,64,256]{2,1,0:T(8,128)(2,1)S(1)}, u32[]{:S(2)}, u32[]{:S(2)}) collective-permute-start(bf16[1,64,256]{2,1,0:T(8,128)(2,1)S(1)} %get-tuple-element.45), channel_id=1, source_target_pairs={{0,6},{1,7},{2,0},{3,1},{4,2},{5,3},{6,4},{7,5},{8,12},{9,13},{10,... | collective-permute-start | bytes 98312 | tf_op jit(solution)/shard_map/ppermute | solution.py:365

commit v9 on v8

--- a/solution.py
+++ b/solution.py
@@ -80,11 +80,6 @@
         fetch.plan(u_hbm.at[me ^ 3], u_last),
         fetch.plan(near_hbm.at[me ^ 3], near_last),
     ]
-
-
-def start_all(copies):
-    for copy in copies:
-        copy.start()
 
 
 def wait_all(copies):
@@ -122,7 +117,8 @@
         for n, whole in enumerate((u_out, near_out, v_out))
     ]
     last = last_copies(me, fetch, u_hbm, near_hbm, u_last, near_last)
-    pl.when(me % 2 == 0)(lambda: start_all(last))
+    last[0].start()
+    pl.when(me % 2 == 0)(last[1].start)
     @pl.when(me >= 0)
     def _():
         wait_all(small)
@@ -153,7 +149,8 @@
         shift[...] = -(b_sigma[...] * (1.0 - rate * state) / state) * divisor
         wait_all(later)
 
-    pl.when(me % 2 == 0)(lambda: wait_all(last))
+    last[0].wait()
+    pl.when(me % 2 == 0)(last[1].wait)
 
 
 def middle_kernel(
@@ -164,7 +161,7 @@
     fetch = Fetches(sems, 0)
     copy = fetch(v_hbm.at[me ^ 3], v_last)
     last = last_copies(me, fetch, u_hbm, near_hbm, u_last, near_last)
-    pl.when(me % 2 != 0)(lambda: start_all(last))
+    pl.when(me % 2 != 0)(last[1].start)
 
     @pl.when(me >= 0)
     def _():
@@ -179,7 +176,7 @@
             )
 
     copy.wait()
-    pl.when(me % 2 != 0)(lambda: wait_all(last))
+    pl.when(me % 2 != 0)(last[1].wait)
 
 
 def last_kernel(
@@ -209,9 +206,9 @@
         return group * PACK + jnp.where(even, there, other) * half
 
     far = 1 - side
-    swap = [at(0, far, 1, side), at(1, far, 1, far), at(3, far, 3, side)]
-    direct = [at(2, far, 3, far), at(2, side, 2, far)]
-    join = [at(0, side, 0, side), at(1, side, 0, far), at(3, side, 2, side)]
+    swap = [at(0, far, 2, side), at(1, far, 2, far), at(3, far, 3, side)]
+    direct = [at(2, far, 3, far), at(2, side, 1, far)]
+    join = [at(0, side, 0, side), at(1, side, 0, far), at(3, side, 1, side)]
     return swap, direct, join
 
 
@@ -364,9 +361,9 @@
             pairs.append((i, (col * n_groups + group) * per_group + place))
         return lax.ppermute(value, ("col", "row"), pairs)
 
-    swapped = send(swapped, 0, 1, (True, False))
+    swapped = send(swapped, 0, 2, (True, False))
     other = send(other, 2, 3, (True, True))
-    same = send(same, 2, 2, (False, True))
+    same = send(same, 2, 1, (False, True))
     own, first, second = pl.pallas_call(
         join_kernel,
         out_shape=[pltpu.VMEM(shards, dtype) for dtype in (F32, BF16, BF16)],
@@ -375,7 +372,7 @@
         **params(0, 8 * swapped.size),
     )(total, swapped)
     received = [
-        other, same, send(first, 1, 0, (False, True)), send(second, 3, 2, (False, False))
+        other, same, send(first, 1, 0, (False, True)), send(second, 3, 1, (False, False))
     ]
     for place in reversed(range(per_group.bit_length() - 2)):
         shape = (own.shape[0] // 2, members, owned)

time: 21.6 us -> 21.5 us (level)
  waiting for transfers between devices: 2.63 us -> 2.25 us
  starting transfers between devices: 11.5 us -> 11.8 us
    ppermute x5, waiting for transfers between devices: 2.62 us -> 2.24 us  [send(): return lax.ppermute(value, ('col', 'row'), pairs)]
    ppermute x3, starting transfers between devices: 3.17 us -> 3.47 us  [col_swap(): return lax.ppermute(value, 'col', [(i, i ^ offset) for i in range(groups)])]
  transfers between devices with their start and end apart: 8 -> 8, of which waited for: 4 -> 3; matrix products, arithmetic and copies ran while one was open for 0% -> 0% of each run, Pallas kernels for 24% -> 24%
where the time goes in v9:
time: 21.5 us; the launch traced here: 21.3 us
  starting transfers between devices  11.8 us (55%)
  Pallas kernels  5.9 us (27%)
  waiting for transfers between devices  2.25 us (10%)
  between operations  0.68 us (3%)
  other arithmetic  0.67 us (3%)
    ppermute x5, starting transfers between devices, send(): return lax.ppermute(value, ('col', 'row'), pairs)  8.33 us
    pallas_call x1, Pallas kernels, body(): pl.pallas_call(own_kernel, out_shape=[total_shape, *[pltpu.VMEM((2, *w.sh...  3.93 us
    ppermute x3, starting transfers between devices, col_swap(): return lax.ppermute(value, 'col', [(i, i ^ offset) for i in range(groups)])  3.47 us
    ppermute x5, waiting for transfers between devices, send(): return lax.ppermute(value, ('col', 'row'), pairs)  2.24 us
    pallas_call x1, Pallas kernels, body(): pl.pallas_call(middle_kernel, out_shape=[total_shape, *last_shapes, pltpu...  1.25 us
    pallas_call x1, Pallas kernels, body(): pl.pallas_call(last_kernel, out_shape=[total_shape, pltpu.VMEM((3 * PACK...  0.69 us
    add x1, other arithmetic, body(): return (stress_rate, stress_rate * gain + shift)  0.67 us
  transfers between devices with their start and end apart: 8, of which 3 were waited for; matrix products, arithmetic and copies ran while one was open for 0% of the time, Pallas kernels for 24%

profile of v9, /device:TPU:0, one launch (start us, length us, event | category | flops | bytes accessed | tf_op | source)
XLA Modules:
  0.0 21.3 jit_solution(12809074323347535442)
XLA Ops:
  0.6 3.0 %collective-permute-start = (bf16[64,1024]{1,0:T(8,128)(2,1)}, bf16[64,1024]{1,0:T(8,128)(2,1)S(1)}, u32[]{:S(2)}, u32[]{:S(2)}) collective-permute-start(bf16[64,1024]{1,0:T(8,128)(2,1)} %slip_hbm.1), channel_id=1, source_target_pairs={{0,16},{8,24},{16,0},{24,8},{1,17},{9,25},{17,1},{25,9},{2,18},{10... | collective-permute-start | bytes 393224 | tf_op jit(solution)/shard_map/ppermute | solution.py:281
  3.6 0.0 collective-permute-start.2
  3.6 3.9 %shard_map.113 = (f32[16,64,128]{2,1,0:T(8,128)S(1)}, bf16[2,1024,512]{2,1,0:T(8,128)(2,1)S(1)}, bf16[2,16,256,128]{3,2,1,0:T(8,128)(2,1)S(1)}, bf16[2,1024,256]...) custom-call(bf16[64,1024]{1,0:T(8,128)(2,1)} %slip_hbm.1, ...), custom_call_target="tpu_custom_call" | custom-call | flops 167772160 | bytes 10485760 | tf_op jit(solution)/shard_map/pallas_call | solution.py:295
  7.6 0.0 collective-permute-done.across
  7.6 0.5 %collective-permute-start.1 = (bf16[64,1024]{1,0:T(8,128)(2,1)S(1)}, bf16[64,1024]{1,0:T(8,128)(2,1)S(1)}, u32[]{:S(2)}, u32[]{:S(2)}) collective-permute-start(bf16[64,1024]{1,0:T(8,128)(2,1)S(1)} %collective-permute-done.across), channel_id=1, source_target_pairs={{0,8},{8,0},{16,24},{24,16},{1,9},{9,1},{17,25},{25,17},{2,10},{10... | collective-permute-start | bytes 393224 | tf_op jit(solution)/shard_map/ppermute | solution.py:281
  8.1 0.0 collective-permute-done.2.sibling
  8.1 1.3 %shard_map.114 = (f32[16,64,128]{2,1,0:T(8,128)S(1)}, bf16[1024,512]{1,0:T(8,128)(2,1)S(1)}, bf16[1024,256]{1,0:T(8,128)(2,1)S(1)}, bf16[16,256,128]{2,1,0:T(8,128)(2,1)S(1)}) custom-call(bf16[64,1024]{1,0:T(8,128)(2,1)S(1)} %collective-permute-done.2.sibling, ...), custom_call_target="tpu_custom_call", output_to_operand_aliasing={{0}: (7, {}), {1}: (8, {}), {2}: (9, {})} | custom-call | flops 335544320 | bytes 5242880 | tf_op jit(solution)/shard_map/pallas_call | solution.py:327
  9.3 0.0 collective-permute-done.1.beyond
  9.3 0.7 %shard_map.115 = (f32[16,64,128]{2,1,0:T(8,128)S(1)}, bf16[6,64,128]{2,1,0:T(8,128)(2,1)S(1)}, bf16[1,64,256]{2,1,0:T(8,128)(2,1)S(1)}, bf16[1,64,256]{2,1,0:T(8,128)(2,1)S(1)}) custom-call(bf16[64,1024]{1,0:T(8,128)(2,1)S(1)} %collective-permute-done.1.beyond, bf16[1024,512]{1,0:T(8,128)(2,1)S(1)} %get-tuple-element.35.u_ref, ...), custom_call_target="tpu_custom_call", output_to_operand_aliasing={{0}: (6, {})} | custom-call | flops 167772160 | bytes 2621440 | tf_op jit(solution)/shard_map/pallas_call | solution.py:341
  10.0 1.6 %collective-permute-start.3 = (bf16[6,64,128]{2,1,0:T(8,128)(2,1)S(1)}, bf16[6,64,128]{2,1,0:T(8,128)(2,1)S(1)}, u32[]{:S(2)}, u32[]{:S(2)}) collective-permute-start(bf16[6,64,128]{2,1,0:T(8,128)(2,1)S(1)} %get-tuple-element.40), channel_id=1, source_target_pairs={{0,1},{1,0},{2,3},{3,2},{4,5},{5,4},{6,7},{7,6},{8,12},{9,13},{10,... | collective-permute-start | bytes 294920 | tf_op jit(solution)/shard_map/ppermute | solution.py:362
  11.6 2.5 %collective-permute-start.4 = (bf16[1,64,256]{2,1,0:T(8,128)(2,1)S(1)}, bf16[1,64,256]{2,1,0:T(8,128)(2,1)S(1)}, u32[]{:S(2)}, u32[]{:S(2)}) collective-permute-start(bf16[1,64,256]{2,1,0:T(8,128)(2,1)S(1)} %get-tuple-element.42), channel_id=1, source_target_pairs={{0,5},{1,4},{2,7},{3,6},{4,1},{5,0},{6,3},{7,2},{8,15},{9,14},{10,... | collective-permute-start | bytes 98312 | tf_op jit(solution)/shard_map/ppermute | solution.py:362
  14.2 0.3 %collective-permute-start.5 = (bf16[1,64,256]{2,1,0:T(8,128)(2,1)S(1)}, bf16[1,64,256]{2,1,0:T(8,128)(2,1)S(1)}, u32[]{:S(2)}, u32[]{:S(2)}) collective-permute-start(bf16[1,64,256]{2,1,0:T(8,128)(2,1)S(1)} %get-tuple-element.43), channel_id=1, source_target_pairs={{0,4},{1,5},{2,6},{3,7},{4,0},{5,1},{6,2},{7,3},{8,11},{9,10},{10,... | collective-permute-start | bytes 98312 | tf_op jit(solution)/shard_map/ppermute | solution.py:362
  14.5 0.2 %collective-permute-done.3.received = bf16[6,64,128]{2,1,0:T(8,128)(2,1)S(1)} collective-permute-done((bf16[6,64,128]{2,1,0:T(8,128)(2,1)S(1)}, bf16[6,64,128]{2,1,0:T(8,128)(2,1)S(1)}, u32[]{:S(2)}, u32[]{:S(2)}) %collective-permute-start.3) | collective-permute-done | bytes 98336 | tf_op jit(solution)/shard_map/ppermute | solution.py:362
  14.7 1.6 %collective-permute-start.6 = (bf16[1,64,256]{2,1,0:T(8,128)(2,1)S(1)}, bf16[1,64,256]{2,1,0:T(8,128)(2,1)S(1)}, u32[]{:S(2)}, u32[]{:S(2)}) collective-permute-start(bf16[1,64,256]{2,1,0:T(8,128)(2,1)S(1)} %get-tuple-element.44), channel_id=1, source_target_pairs={{0,2},{1,3},{2,4},{3,5},{4,6},{5,7},{6,0},{7,1},{8,9},{9,8},{10,11... | collective-permute-start | bytes 98312 | tf_op jit(solution)/shard_map/ppermute | solution.py:362
  16.4 2.2 %collective-permute-start.7 = (bf16[1,64,256]{2,1,0:T(8,128)(2,1)S(1)}, bf16[1,64,256]{2,1,0:T(8,128)(2,1)S(1)}, u32[]{:S(2)}, u32[]{:S(2)}) collective-permute-start(bf16[1,64,256]{2,1,0:T(8,128)(2,1)S(1)} %get-tuple-element.45), channel_id=1, source_target_pairs={{0,6},{1,7},{2,0},{3,1},{4,2},{5,3},{6,4},{7,5},{8,10},{9,11},{10,... | collective-permute-start | bytes 98312 | tf_op jit(solution)/shard_map/ppermute | solution.py:362
  18.6 0.0 collective-permute-done.4
  18.6 0.3 %collective-permute-done.5 = bf16[1,64,256]{2,1,0:T(8,128)(2,1)S(1)} collective-permute-done((bf16[1,64,256]{2,1,0:T(8,128)(2,1)S(1)}, bf16[1,64,256]{2,1,0:T(8,128)(2,1)S(1)}, u32[]{:S(2)}, u32[]{:S(2)}) %collective-permute-start.5) | collective-permute-done | bytes 32800 | tf_op jit(solution)/shard_map/ppermute | solution.py:362
  19.0 1.6 %collective-permute-done.6 = bf16[1,64,256]{2,1,0:T(8,128)(2,1)S(1)} collective-permute-done((bf16[1,64,256]{2,1,0:T(8,128)(2,1)S(1)}, bf16[1,64,256]{2,1,0:T(8,128)(2,1)S(1)}, u32[]{:S(2)}, u32[]{:S(2)}) %collective-permute-start.6) | collective-permute-done | bytes 32800 | tf_op jit(solution)/shard_map/ppermute | solution.py:362
  20.6 0.0 collective-permute-done.7
  20.6 0.7 %multiply_add_fusion = (f32[64,256]{1,0:T(8,128)}, f32[64,256]{1,0:T(8,128)}) fusion(f32[64,256]{1,0:T(8,128)S(1)} %get-tuple-element.47, f32[64,256]{1,0:T(8,128)S(1)} %get-tuple-element.46, bf16[1,64,256]{2,1,0:T(8,128)(2,1)S(1)} %collective-permute-done.7, bf16[1,64,256]{2,1,0:T(8,128)(2,1)S(1)} %collective-permute-done.6, ...), kind=kLoop, calls=%fused_computation.1 | loop fusion | flops 163840 | bytes 458752 | tf_op jit(solution)/shard_map/add | solution.py:390
  (1 shorter events, 0.0 us)
Async XLA Ops:
  0.6 7.0 %collective-permute-start = (bf16[64,1024]{1,0:T(8,128)(2,1)}, bf16[64,1024]{1,0:T(8,128)(2,1)S(1)}, u32[]{:S(2)}, u32[]{:S(2)}) collective-permute-start(bf16[64,1024]{1,0:T(8,128)(2,1)} %slip_hbm.1), channel_id=1, source_target_pairs={{0,16},{8,24},{16,0},{24,8},{1,17},{9,25},{17,1},{25,9},{2,18},{10... | collective-permute-start | bytes 393224 | tf_op jit(solution)/shard_map/ppermute | solution.py:281
  3.6 4.4 %collective-permute-start.2 = (bf16[64,1024]{1,0:T(8,128)(2,1)}, bf16[64,1024]{1,0:T(8,128)(2,1)S(1)}, u32[]{:S(2)}, u32[]{:S(2)}) collective-permute-start(bf16[64,1024]{1,0:T(8,128)(2,1)} %slip_hbm.1), channel_id=1, source_target_pairs={{0,8},{8,0},{16,24},{24,16},{1,9},{9,1},{17,25},{25,17},{2,10},{10... | collective-permute-start | bytes 393224 | tf_op jit(solution)/shard_map/ppermute | solution.py:281
  7.6 1.7 %collective-permute-start.1 = (bf16[64,1024]{1,0:T(8,128)(2,1)S(1)}, bf16[64,1024]{1,0:T(8,128)(2,1)S(1)}, u32[]{:S(2)}, u32[]{:S(2)}) collective-permute-start(bf16[64,1024]{1,0:T(8,128)(2,1)S(1)} %collective-permute-done.across), channel_id=1, source_target_pairs={{0,8},{8,0},{16,24},{24,16},{1,9},{9,1},{17,25},{25,17},{2,10},{10... | collective-permute-start | bytes 393224 | tf_op jit(solution)/shard_map/ppermute | solution.py:281
  10.0 4.7 %collective-permute-start.3 = (bf16[6,64,128]{2,1,0:T(8,128)(2,1)S(1)}, bf16[6,64,128]{2,1,0:T(8,128)(2,1)S(1)}, u32[]{:S(2)}, u32[]{:S(2)}) collective-permute-start(bf16[6,64,128]{2,1,0:T(8,128)(2,1)S(1)} %get-tuple-element.40), channel_id=1, source_target_pairs={{0,1},{1,0},{2,3},{3,2},{4,5},{5,4},{6,7},{7,6},{8,12},{9,13},{10,... | collective-permute-start | bytes 294920 | tf_op jit(solution)/shard_map/ppermute | solution.py:362
  11.6 7.0 %collective-permute-start.4 = (bf16[1,64,256]{2,1,0:T(8,128)(2,1)S(1)}, bf16[1,64,256]{2,1,0:T(8,128)(2,1)S(1)}, u32[]{:S(2)}, u32[]{:S(2)}) collective-permute-start(bf16[1,64,256]{2,1,0:T(8,128)(2,1)S(1)} %get-tuple-element.42), channel_id=1, source_target_pairs={{0,5},{1,4},{2,7},{3,6},{4,1},{5,0},{6,3},{7,2},{8,15},{9,14},{10,... | collective-permute-start | bytes 98312 | tf_op jit(solution)/shard_map/ppermute | solution.py:362
  14.2 4.8 %collective-permute-start.5 = (bf16[1,64,256]{2,1,0:T(8,128)(2,1)S(1)}, bf16[1,64,256]{2,1,0:T(8,128)(2,1)S(1)}, u32[]{:S(2)}, u32[]{:S(2)}) collective-permute-start(bf16[1,64,256]{2,1,0:T(8,128)(2,1)S(1)} %get-tuple-element.43), channel_id=1, source_target_pairs={{0,4},{1,5},{2,6},{3,7},{4,0},{5,1},{6,2},{7,3},{8,11},{9,10},{10,... | collective-permute-start | bytes 98312 | tf_op jit(solution)/shard_map/ppermute | solution.py:362
  14.7 5.9 %collective-permute-start.6 = (bf16[1,64,256]{2,1,0:T(8,128)(2,1)S(1)}, bf16[1,64,256]{2,1,0:T(8,128)(2,1)S(1)}, u32[]{:S(2)}, u32[]{:S(2)}) collective-permute-start(bf16[1,64,256]{2,1,0:T(8,128)(2,1)S(1)} %get-tuple-element.44), channel_id=1, source_target_pairs={{0,2},{1,3},{2,4},{3,5},{4,6},{5,7},{6,0},{7,1},{8,9},{9,8},{10,11... | collective-permute-start | bytes 98312 | tf_op jit(solution)/shard_map/ppermute | solution.py:362
  16.4 4.3 %collective-permute-start.7 = (bf16[1,64,256]{2,1,0:T(8,128)(2,1)S(1)}, bf16[1,64,256]{2,1,0:T(8,128)(2,1)S(1)}, u32[]{:S(2)}, u32[]{:S(2)}) collective-permute-start(bf16[1,64,256]{2,1,0:T(8,128)(2,1)S(1)} %get-tuple-element.45), channel_id=1, source_target_pairs={{0,6},{1,7},{2,0},{3,1},{4,2},{5,3},{6,4},{7,5},{8,10},{9,11},{10,... | collective-permute-start | bytes 98312 | tf_op jit(solution)/shard_map/ppermute | solution.py:362
